TPU v7x, 32 devices: a whole 2x2x4 slice. The times are simulated.
32 devices in a mesh: grp: 2 (over x), ad: 16 (over z, y, core).
Axes of the slice: x: 2, y: 2, z: 4, core: 2. Of those that a mesh axis runs over, the one named last changes fastest.
Arguments:
- tokens: bfloat16 [4096, 8192], P(('grp', 'ad')), parts along dimension 0, may hold values from -6 to 6
- cotangent: bfloat16 [4096, 1024], P(('grp', 'ad')), parts along dimension 0, may hold values from -0.1796875 to 0.1796875
- owner: int32 [4096, 1], P(('grp', 'ad')), parts along dimension 0, may hold values from 0 to 15; in each aligned block of 128 rows (0 to 127, 128 to 255, ...) at most 16 rows name the same one
- token_local_adapter: int32 [4096], P(('grp', 'ad')), parts along dimension 0, may hold values from 0 to 1
- segment: int32 [32, 128], P(('grp', 'ad')), parts along dimension 0, may hold values from 0 to 3, never falling along the last dimension, each value on 1 to 64 neighbouring positions
- pair_sequence_order: int32 [32, 4], P(('grp', 'ad')), parts along dimension 0, may hold values from 0 to 3, each once within a row
- frozen_margin_score: float32 [32, 4], P(('grp', 'ad')), parts along dimension 0, may hold values from -12 to 12
- adapter_down_weight: bfloat16 [32, 64, 8192], P('ad'), may hold values from -0.0625 to 0.0625
- adapter_up_weight: bfloat16 [32, 64, 1024], P('ad'), may hold values from -0.75 to 0.75
Outputs:
- input_grad: bfloat16 [4096, 8192], P(('grp', 'ad')), parts along dimension 0
- grad_a: bfloat16 [64, 64, 8192], P(('grp', 'ad')), parts along dimension 0
- grad_b: bfloat16 [64, 64, 1024], P(('grp', 'ad')), parts along dimension 0
- pair_loss: float32 [64], P(('grp', 'ad')), parts along dimension 0
There are 2 independent parts, one for each index of `grp`. A program takes and returns all parts, laid end to end along the dimension named above; an argument that names none is the same for every part. Nothing has to cross between parts.
Inputs may be any that keep to these rules, and one draw needn't show every extreme that they name: The rows of one device name one owner at most 16 times; in some device some owner is named exactly 16 times. `segment`: within each row, sequence numbers never fall; each of the 4 sequences holds 1 to 64 consecutive positions. `pair_sequence_order`: each row is a permutation of the device's sequences.
All inputs are finite; a program needn't handle non-finite values.
Results may differ from a plain program's by a relative error of at most 0.0085.
Values may be sent and summed in bfloat16 or wider, within the bound.
No kernel may reach another device: no remote copies, remote signals or barrier semaphores. Data moves between devices by JAX's collectives and lax.ppermute only.
A program may use at most 128 MiB of HBM per device.

v0:
```python
import jax
import jax.numpy as jnp
from jax import lax
from jax.sharding import PartitionSpec as P

SCALE = 2.0
BETA = 0.1
LOSS_SCALE = 256.0


def adapter_rows(rows_input, rows_gradient, rows_adapter_index, down_pair, up_pair):
    count_rows = rows_input.shape[0]
    rank_size = down_pair.shape[1]
    contract = (((1,), (1,)), ((), ()))
    hidden = jnp.zeros((count_rows, rank_size), jnp.float32)
    pulled = jnp.zeros((count_rows, rank_size), jnp.float32)
    for which in range(down_pair.shape[0]):
        member = (rows_adapter_index == which)[:, None]
        hidden = jnp.where(
            member,
            lax.dot_general(
                rows_input, down_pair[which], contract, preferred_element_type=jnp.float32
            ),
            hidden,
        )
        pulled = jnp.where(
            member,
            lax.dot_general(
                rows_gradient, up_pair[which], contract, preferred_element_type=jnp.float32
            ),
            pulled,
        )
    hidden_rank_rows = hidden.astype(jnp.bfloat16)
    pulled_rank_rows = pulled.astype(jnp.bfloat16)
    outgoing = jnp.zeros((count_rows, up_pair.shape[2]), jnp.float32)
    projected = jnp.zeros((count_rows, down_pair.shape[2]), jnp.float32)
    for which in range(down_pair.shape[0]):
        member = (rows_adapter_index == which)[:, None]
        outgoing = outgoing + jnp.dot(
            jnp.where(member, hidden_rank_rows, 0),
            up_pair[which],
            preferred_element_type=jnp.float32,
        )
        projected = projected + jnp.dot(
            jnp.where(member, pulled_rank_rows, 0),
            down_pair[which],
            preferred_element_type=jnp.float32,
        )
    return (
        hidden_rank_rows,
        pulled_rank_rows,
        (SCALE * outgoing).astype(jnp.bfloat16),
        projected.astype(jnp.bfloat16),
    )


def adapter_grads(
    rows_input,
    rows_gradient,
    rows_adapter_index,
    hidden_rank_rows,
    pulled_rank_rows,
    row_weight,
    count,
):
    upper = (row_weight[:, None] * hidden_rank_rows.astype(jnp.float32)).astype(jnp.bfloat16)
    lower = (row_weight[:, None] * pulled_rank_rows.astype(jnp.float32)).astype(jnp.bfloat16)
    contract = (((0,), (0,)), ((), ()))
    grads_down = []
    grads_up = []
    for which in range(count):
        member = (rows_adapter_index == which)[:, None]
        grads_up.append(
            SCALE
            * lax.dot_general(
                jnp.where(member, upper, 0),
                rows_gradient,
                contract,
                preferred_element_type=jnp.float32,
            )
        )
        grads_down.append(
            SCALE
            * lax.dot_general(
                jnp.where(member, lower, 0),
                rows_input,
                contract,
                preferred_element_type=jnp.float32,
            )
        )
    return (jnp.stack(grads_down).astype(jnp.bfloat16), jnp.stack(grads_up).astype(jnp.bfloat16))


def pair_terms(outgoing, cotangent, segment_row, order_row, base_row):
    seqs = base_row.shape[0]
    tokdot = jnp.sum(outgoing.astype(jnp.float32) * cotangent.astype(jnp.float32), axis=1)
    seq_hot = (segment_row[:, None] == jnp.arange(seqs, dtype=jnp.int32)[None, :]).astype(
        jnp.float32
    )
    scores = base_row + jnp.dot(tokdot, seq_hot, precision=lax.Precision.HIGHEST)
    pair_pick = (order_row[:, None] == jnp.arange(seqs, dtype=jnp.int32)[None, :]).astype(
        jnp.float32
    )
    ordered = jnp.sum(pair_pick * scores[None, :], axis=1).reshape(seqs // 2, 2)
    margin = BETA * (ordered[:, 0] - ordered[:, 1])
    losses = jax.nn.softplus(-margin)
    lean = jax.nn.sigmoid(-margin)
    by_order = jnp.stack([-BETA * lean, BETA * lean], axis=1).reshape(seqs)
    seq_weight = jnp.sum(pair_pick * by_order[:, None], axis=0)
    row_weight = LOSS_SCALE * jnp.sum(seq_hot * seq_weight[None, :], axis=1)
    return (losses, row_weight)


def body(
    tokens,
    cotangent,
    owner,
    token_local_adapter,
    segment,
    pair_sequence_order,
    frozen_margin_score,
    adapter_down_weight,
    adapter_up_weight,
):
    tok_rows, width = tokens.shape
    out_width = cotangent.shape[1]
    n_dev = lax.axis_size("ad")
    capacity = max(2, 2 * tok_rows // n_dev)
    slots_total = n_dev * capacity
    target_owner = owner[:, 0]
    owners_hot = (target_owner[:, None] == jnp.arange(n_dev, dtype=jnp.int32)[None, :]).astype(
        jnp.float32
    )
    strict_lower = (jnp.arange(tok_rows)[:, None] > jnp.arange(tok_rows)[None, :]).astype(
        jnp.float32
    )
    before_count = jnp.dot(strict_lower, owners_hot, precision=lax.Precision.HIGHEST)
    slot_rank = jnp.sum(before_count * owners_hot, axis=1).astype(jnp.int32)
    slot_index = target_owner * capacity + slot_rank
    send_x = (
        jnp.zeros((slots_total, width), jnp.bfloat16)
        .at[slot_index]
        .set(tokens)
        .reshape(n_dev, capacity, width)
    )
    send_g = (
        jnp.zeros((slots_total, out_width), jnp.bfloat16)
        .at[slot_index]
        .set(cotangent)
        .reshape(n_dev, capacity, out_width)
    )
    send_id = (
        jnp.zeros((slots_total,), jnp.int32)
        .at[slot_index]
        .set(token_local_adapter)
        .reshape(n_dev, capacity)
    )
    recv_x, recv_g, recv_id = (
        lax.all_to_all(send_x, "ad", split_axis=0, concat_axis=0, tiled=True),
        lax.all_to_all(send_g, "ad", split_axis=0, concat_axis=0, tiled=True),
        lax.all_to_all(send_id, "ad", split_axis=0, concat_axis=0, tiled=True),
    )
    rows_input = recv_x.reshape(slots_total, width)
    rows_gradient = recv_g.reshape(slots_total, out_width)
    rows_adapter_index = recv_id.reshape(slots_total)
    hidden_rank_rows, pulled_rank_rows, outgoing, projected = adapter_rows(
        rows_input, rows_gradient, rows_adapter_index, adapter_down_weight, adapter_up_weight
    )
    got_out = lax.all_to_all(
        outgoing.reshape(n_dev, capacity, out_width), "ad", split_axis=0, concat_axis=0, tiled=True
    )
    out_tok = got_out.reshape(slots_total, out_width)[slot_index]
    losses, row_weight = pair_terms(
        out_tok, cotangent, segment[0], pair_sequence_order[0], frozen_margin_score[0]
    )
    send_w = (
        jnp.zeros((slots_total,), jnp.float32)
        .at[slot_index]
        .set(row_weight)
        .reshape(n_dev, capacity)
    )
    received_weight = lax.all_to_all(send_w, "ad", split_axis=0, concat_axis=0, tiled=True).reshape(
        slots_total
    )
    grad_down, grad_up = adapter_grads(
        rows_input,
        rows_gradient,
        rows_adapter_index,
        hidden_rank_rows,
        pulled_rank_rows,
        received_weight,
        adapter_down_weight.shape[0],
    )
    slot_grad = (SCALE * received_weight[:, None] * projected.astype(jnp.float32)).astype(
        jnp.bfloat16
    )
    got_grad = lax.all_to_all(
        slot_grad.reshape(n_dev, capacity, width), "ad", split_axis=0, concat_axis=0, tiled=True
    )
    input_grad = got_grad.reshape(slots_total, width)[slot_index]
    return (input_grad, grad_down, grad_up, losses)


def solution(mesh):
    placed = (
        P(("grp", "ad"), None),
        P(("grp", "ad"), None),
        P(("grp", "ad"), None),
        P(("grp", "ad")),
        P(("grp", "ad"), None),
        P(("grp", "ad"), None),
        P(("grp", "ad"), None),
        P("ad", None, None),
        P("ad", None, None),
    )
    return jax.shard_map(
        body,
        mesh=mesh,
        in_specs=placed,
        out_specs=(
            P(("grp", "ad"), None),
            P(("grp", "ad"), None, None),
            P(("grp", "ad"), None, None),
            P(("grp", "ad")),
        ),
        check_vma=False,
    )
```

profile of v0, /device:TPU:15, one launch (start us, length us, event | category | flops | bytes accessed | tf_op | source)
XLA Modules:
  0.0 281.7 jit_solution(8808863305276130463)
XLA Ops:
  0.6 0.9 fusion.19
  1.5 0.7 fusion.68
  2.2 1.1 scatter_custom_fusion
  3.3 0.7 all_to_all.24
  4.0 6.6 %all-to-all-start = ((s32[16,1,16]{2,1,0:T(1,128)}), s32[16,1,16]{2,1,0:T(1,128)S(1)}, u32[]{:S(2)}, u32[]{:S(2)}) async-start(s32[16,1,16]{2,1,0:T(1,128)} %all_to_all.24), calls=%async_computation | async-start | bytes 16384 | tf_op jit(solution)/shard_map/all_to_all | solution.py:161
  10.5 7.0 %scatter_custom_fusion.1 = bf16[256,8192]{1,0:T(8,128)(2,1)} fusion(s32[128]{0:T(128)S(1)} %fusion.68, bf16[128,8192]{1,0:T(8,128)(2,1)} %param.9, bf16[]{:T(256)} %constant.17.clone.1), kind=kCustom, calls=%fused_computation.18 | custom fusion | bytes 4194816 | tf_op jit(solution)/shard_map/scatter | solution.py:143
  17.5 6.2 %all-to-all-start.1 = ((bf16[16,16,8192]{2,1,0:T(8,128)(2,1)}), bf16[16,16,8192]{2,1,0:T(8,128)(2,1)}, u32[]{:S(2)}, u32[]{:S(2)}) async-start(bf16[16,16,8192]{2,1,0:T(8,128)(2,1)} %bitcast.66), calls=%async_computation.1 | async-start | bytes 8388608 | tf_op jit(solution)/shard_map/all_to_all | solution.py:159
  23.7 2.4 scatter_custom_fusion.3
  26.3 89.9 %all-to-all-done.1 = bf16[16,16,8192]{2,1,0:T(8,128)(2,1)} async-done(((bf16[16,16,8192]{2,1,0:T(8,128)(2,1)}), bf16[16,16,8192]{2,1,0:T(8,128)(2,1)}, u32[]{:S(2)}, u32[]{:S(2)}) %all-to-all-start.1) | async-done | bytes 4194336 | tf_op jit(solution)/shard_map/all_to_all | solution.py:159
  116.1 4.9 %all-to-all-start.4 = ((bf16[16,16,1024]{2,1,0:T(8,128)(2,1)}), bf16[16,16,1024]{2,1,0:T(8,128)(2,1)S(1)}, u32[]{:S(2)}, u32[]{:S(2)}) async-start(bf16[16,16,1024]{2,1,0:T(8,128)(2,1)} %bitcast.16), calls=%async_computation.4 | async-start | bytes 1048576 | tf_op jit(solution)/shard_map/all_to_all | solution.py:160
  121.1 3.6 %convolution_select_fusion.1 = bf16[256,64]{0,1:T(8,128)(2,1)S(1)} fusion(bf16[256,8192]{1,0:T(8,128)(2,1)} %bitcast.7, bf16[2,64,8192]{2,1,0:T(8,128)(2,1)S(1)} %copy-done, pred[256]{0:T(512)(128)(4,1)S(1)} %eq.82), kind=kOutput, calls=%fused_computation.31 | convolution fusion | flops 268451840 | bytes 5276160 | tf_op jit(solution)/shard_map/dot_general | solution.py:21
  124.7 3.6 %fusion.17 = bf16[256,64]{0,1:T(8,128)(2,1)S(1)} fusion(bf16[256,64]{0,1:T(8,128)(2,1)S(1)} %convolution_select_fusion.1, bf16[256,8192]{1,0:T(8,128)(2,1)} %bitcast.7, bf16[2,64,8192]{2,1,0:T(8,128)(2,1)S(1)} %copy-done, pred[256]{0:T(512)(128)(4,1)S(1)} %eq.84), kind=kOutput, calls=%fused_computation.33 | convolution fusion | flops 268451840 | bytes 5308928 | tf_op jit(solution)/shard_map/dot_general | solution.py:21
  128.7 1.1 fusion.11
  129.8 4.9 %all-to-all-done.4 = bf16[16,16,1024]{2,1,0:T(8,128)(2,1)S(1)} async-done(((bf16[16,16,1024]{2,1,0:T(8,128)(2,1)}), bf16[16,16,1024]{2,1,0:T(8,128)(2,1)S(1)}, u32[]{:S(2)}, u32[]{:S(2)}) %all-to-all-start.4) | async-done | bytes 524320 | tf_op jit(solution)/shard_map/all_to_all | solution.py:160
  134.6 5.0 %all-to-all-start.2 = ((bf16[16,16,1024]{2,1,0:T(8,128)(2,1)}), bf16[16,16,1024]{2,1,0:T(8,128)(2,1)S(1)}, u32[]{:S(2)}, u32[]{:S(2)}) async-start(bf16[16,16,1024]{2,1,0:T(8,128)(2,1)} %bitcast.73), calls=%async_computation.2 | async-start | bytes 1048576 | tf_op jit(solution)/shard_map/all_to_all | solution.py:169
  140.2 13.0 %all-to-all-done.2 = bf16[16,16,1024]{2,1,0:T(8,128)(2,1)S(1)} async-done(((bf16[16,16,1024]{2,1,0:T(8,128)(2,1)}), bf16[16,16,1024]{2,1,0:T(8,128)(2,1)S(1)}, u32[]{:S(2)}, u32[]{:S(2)}) %all-to-all-start.2) | async-done | bytes 524320 | tf_op jit(solution)/shard_map/all_to_all | solution.py:169
  153.2 0.9 gather_fusion
  154.1 1.1 multiply_reduce_fusion
  156.1 1.0 scatter_custom_fusion.2
  157.1 0.7 all_to_all.28
  157.8 5.0 %all-to-all-start.3 = ((f32[16,1,16]{2,1,0:T(1,128)}), f32[16,1,16]{2,1,0:T(1,128)S(1)}, u32[]{:S(2)}, u32[]{:S(2)}) async-start(f32[16,1,16]{2,1,0:T(1,128)} %all_to_all.28), calls=%async_computation.3 | async-start | bytes 16384 | tf_op jit(solution)/shard_map/all_to_all | solution.py:182
  162.8 4.5 %fusion.21 = f32[256,8192]{1,0:T(8,128)} fusion(bf16[2,64,8192]{2,1,0:T(8,128)(2,1)S(1)} %copy-done, bf16[256,64]{0,1:T(8,128)(2,1)S(1)} %fusion.18, pred[256]{0:T(512)(128)(4,1)S(1)} %eq.82), kind=kOutput, calls=%fused_computation.39 | convolution fusion | flops 268451840 | bytes 9470464 | tf_op jit(solution)/shard_map/dot_general | solution.py:44
  167.8 0.7 reduce.9
  168.6 6.6 %fusion.3 = bf16[256,8192]{1,0:T(8,128)(2,1)} fusion(f32[256,8192]{1,0:T(8,128)} %fusion.21, f32[256]{0:T(256)S(1)} %broadcast_multiply_fusion, bf16[2,64,8192]{2,1,0:T(8,128)(2,1)S(1)} %copy-done, bf16[256,64]{0,1:T(8,128)(2,1)S(1)} %fusion.18, pred[256]{0:T(512)(128)(4,1)S(1)} %eq.84), kind=kOutput, calls=%fused_computation.10 | convolution fusion | flops 278937600 | bytes 13665792 | tf_op jit(solution)/shard_map/dot_general | solution.py:44
  175.2 6.2 %all-to-all-start.5 = ((bf16[16,16,8192]{2,1,0:T(8,128)(2,1)}), bf16[16,16,8192]{2,1,0:T(8,128)(2,1)}, u32[]{:S(2)}, u32[]{:S(2)}) async-start(bf16[16,16,8192]{2,1,0:T(8,128)(2,1)} %bitcast.67), calls=%async_computation.5 | async-start | bytes 8388608 | tf_op jit(solution)/shard_map/all_to_all | solution.py:197
  181.4 0.5 compare_select_fusion
  182.4 0.7 pad_maximum_fusion.1
  183.1 3.0 %fusion.6 = bf16[1,64,8192]{2,1,0:T(8,128)(2,1)S(1)} fusion(bf16[256,8192]{1,0:T(8,128)(2,1)} %bitcast.7, pred[256]{0:T(512)(128)(4,1)S(1)} %eq.84, bf16[256,64]{0,1:T(8,128)(2,1)S(1)} %fusion.18, f32[256]{0:T(256)S(1)} %broadcast_in_dim_reshape.2), kind=kOutput, calls=%fused_computation.15 | convolution fusion | flops 269549568 | bytes 5276928 | tf_op jit(solution)/shard_map/dot_general | solution.py:84
  186.1 3.0 %fusion.7 = bf16[1,64,8192]{2,1,0:T(8,128)(2,1)S(1)} fusion(bf16[256,8192]{1,0:T(8,128)(2,1)} %bitcast.7, pred[256]{0:T(512)(128)(4,1)S(1)} %eq.82, bf16[256,64]{0,1:T(8,128)(2,1)S(1)} %fusion.18, f32[256]{0:T(256)S(1)} %broadcast_in_dim_reshape.2), kind=kOutput, calls=%fused_computation.16 | convolution fusion | flops 269549568 | bytes 5276928 | tf_op jit(solution)/shard_map/dot_general | solution.py:84
  189.2 1.5 pad_maximum_fusion
  190.7 83.2 %all-to-all-done.5 = bf16[16,16,8192]{2,1,0:T(8,128)(2,1)} async-done(((bf16[16,16,8192]{2,1,0:T(8,128)(2,1)}), bf16[16,16,8192]{2,1,0:T(8,128)(2,1)}, u32[]{:S(2)}, u32[]{:S(2)}) %all-to-all-start.5) | async-done | bytes 4194336 | tf_op jit(solution)/shard_map/all_to_all | solution.py:197
  273.9 7.8 %gather_fusion.1 = bf16[128,8192]{1,0:T(8,128)(2,1)} fusion(bf16[256,8192]{1,0:T(8,128)(2,1)} %bitcast.19, s32[1024]{0:T(1024)S(1)} %pad_clamp_fusion), kind=kCustom, calls=%fused_computation.1 | custom fusion | bytes 4194816 | tf_op jit(solution)/shard_map/gather | solution.py:200
  (34 shorter events, 3.1 us)
Async XLA Ops:
  4.0 13.5 %all-to-all-start = ((s32[16,1,16]{2,1,0:T(1,128)}), s32[16,1,16]{2,1,0:T(1,128)S(1)}, u32[]{:S(2)}, u32[]{:S(2)}) async-start(s32[16,1,16]{2,1,0:T(1,128)} %all_to_all.24), calls=%async_computation | async-start | bytes 16384 | tf_op jit(solution)/shard_map/all_to_all | solution.py:161
  17.5 103.5 %copy-start = (bf16[2,64,8192]{2,1,0:T(8,128)(2,1)S(1)}, bf16[2,64,8192]{2,1,0:T(8,128)(2,1)}, u32[]{:S(2)}) copy-start(bf16[2,64,8192]{2,1,0:T(8,128)(2,1)} %param.16) | copy-start | bytes 6291460
  17.5 98.6 %all-to-all-start.1 = ((bf16[16,16,8192]{2,1,0:T(8,128)(2,1)}), bf16[16,16,8192]{2,1,0:T(8,128)(2,1)}, u32[]{:S(2)}, u32[]{:S(2)}) async-start(bf16[16,16,8192]{2,1,0:T(8,128)(2,1)} %bitcast.66), calls=%async_computation.1 | async-start | bytes 8388608 | tf_op jit(solution)/shard_map/all_to_all | solution.py:159
  116.1 18.5 %all-to-all-start.4 = ((bf16[16,16,1024]{2,1,0:T(8,128)(2,1)}), bf16[16,16,1024]{2,1,0:T(8,128)(2,1)S(1)}, u32[]{:S(2)}, u32[]{:S(2)}) async-start(bf16[16,16,1024]{2,1,0:T(8,128)(2,1)} %bitcast.16), calls=%async_computation.4 | async-start | bytes 1048576 | tf_op jit(solution)/shard_map/all_to_all | solution.py:160
  121.1 7.2 %copy-start.1 = (bf16[2,64,1024]{2,1,0:T(8,128)(2,1)S(1)}, bf16[2,64,1024]{2,1,0:T(8,128)(2,1)}, u32[]{:S(2)}) copy-start(bf16[2,64,1024]{2,1,0:T(8,128)(2,1)} %param.17) | copy-start | bytes 786436
  128.3 26.9 %copy-start.2 = (f32[1,4]{1,0:T(1,128)S(1)}, f32[1,4]{1,0:T(1,128)}, u32[]{:S(2)}) copy-start(f32[1,4]{1,0:T(1,128)} %param.15) | copy-start | bytes 52
  128.3 26.9 %copy-start.4 = (s32[1,128]{1,0:T(1,128)S(1)}, s32[1,128]{1,0:T(1,128)}, u32[]{:S(2)}) copy-start(s32[1,128]{1,0:T(1,128)} %param.13) | copy-start | bytes 1540
  128.3 27.0 %copy-start.3 = (s32[1,4]{1,0:T(1,128)S(1)}, s32[1,4]{1,0:T(1,128)}, u32[]{:S(2)}) copy-start(s32[1,4]{1,0:T(1,128)} %param.14) | copy-start | bytes 52
  134.6 18.6 %all-to-all-start.2 = ((bf16[16,16,1024]{2,1,0:T(8,128)(2,1)}), bf16[16,16,1024]{2,1,0:T(8,128)(2,1)S(1)}, u32[]{:S(2)}, u32[]{:S(2)}) async-start(bf16[16,16,1024]{2,1,0:T(8,128)(2,1)} %bitcast.73), calls=%async_computation.2 | async-start | bytes 1048576 | tf_op jit(solution)/shard_map/all_to_all | solution.py:169
  157.8 9.5 %all-to-all-start.3 = ((f32[16,1,16]{2,1,0:T(1,128)}), f32[16,1,16]{2,1,0:T(1,128)S(1)}, u32[]{:S(2)}, u32[]{:S(2)}) async-start(f32[16,1,16]{2,1,0:T(1,128)} %all_to_all.28), calls=%async_computation.3 | async-start | bytes 16384 | tf_op jit(solution)/shard_map/all_to_all | solution.py:182
  175.2 98.7 %all-to-all-start.5 = ((bf16[16,16,8192]{2,1,0:T(8,128)(2,1)}), bf16[16,16,8192]{2,1,0:T(8,128)(2,1)}, u32[]{:S(2)}, u32[]{:S(2)}) async-start(bf16[16,16,8192]{2,1,0:T(8,128)(2,1)} %bitcast.67), calls=%async_computation.5 | async-start | bytes 8388608 | tf_op jit(solution)/shard_map/all_to_all | solution.py:197
where the time goes:
time: 283 us; the launch traced here: 282 us
  waiting for transfers between devices  191 us (67%)
  starting transfers between devices  33.8 us (12%)
  matrix products  27.8 us (10%)
  local copies, waits for them, and re-layouts  22.4 us (8%)
  other arithmetic  5.91 us (2%)
    all_to_all x1, waiting for transfers between devices, body(): lax.all_to_all(send_x, 'ad', split_axis=0, concat_axis=0, tiled=True)  89.9 us
    all_to_all x1, waiting for transfers between devices, body(): lax.all_to_all(slot_grad.reshape(n_dev, capacity, width), 'ad', split_axi...  83.2 us
    all_to_all x1, waiting for transfers between devices, body(): lax.all_to_all(outgoing.reshape(n_dev, capacity, out_width), 'ad', split_...  13 us
    dot_general x2, matrix products, adapter_rows(): jnp.dot(jnp.where(member, pulled_rank_rows, 0), down_pair[which], preferr...  11.1 us
    gather x1, local copies, waits for them, and re-layouts, body(): input_grad = got_grad.reshape(slots_total, width)[slot_index]  7.81 us
    dot_general x2, matrix products, adapter_rows(): lax.dot_general(rows_input, down_pair[which], contract, preferred_element...  7.21 us
    scatter x1, local copies, waits for them, and re-layouts, body(): send_x = jnp.zeros((slots_total, width), jnp.bfloat16).at[slot_index].set...  6.97 us
    all_to_all x1, starting transfers between devices, body(): lax.all_to_all(send_id, 'ad', split_axis=0, concat_axis=0, tiled=True)  6.55 us
  transfers between devices with their start and end apart: 6, of which 4 were waited for; matrix products, arithmetic and copies ran while one was open for 12% of the time, Pallas kernels for 0%

commit v1 on v0

v1 whole, which is shorter than its diff:
```python
import jax
import jax.numpy as jnp
from jax import lax
from jax.sharding import PartitionSpec as P

SCALE = 2.0
BETA = 0.1
LOSS_SCALE = 256.0

F32 = jnp.float32
BF16 = jnp.bfloat16


def rows_by_slot(owners, n_dev, capacity):
    rows = owners.shape[1]
    hot = (owners[:, :, None] == jnp.arange(n_dev, dtype=jnp.int32)).astype(BF16)
    earlier = (
        jnp.arange(rows, dtype=jnp.int32)[:, None] > jnp.arange(rows, dtype=jnp.int32)[None, :]
    ).astype(BF16)
    before = jnp.einsum("rq,dqk->drk", earlier, hot, preferred_element_type=F32)
    rank = jnp.sum(before * hot.astype(F32), axis=2).astype(jnp.int32)
    return owners * capacity + rank


def pair_weights(scores, order):
    devices, seqs = scores.shape
    pick = (order[:, :, None] == jnp.arange(seqs, dtype=jnp.int32)).astype(F32)
    ordered = jnp.sum(pick * scores[:, None, :], axis=2).reshape(devices, seqs // 2, 2)
    margin = BETA * (ordered[:, :, 0] - ordered[:, :, 1])
    losses = jax.nn.softplus(-margin)
    lean = jax.nn.sigmoid(-margin)
    by_order = jnp.stack([-BETA * lean, BETA * lean], axis=2).reshape(devices, seqs)
    return losses, jnp.sum(pick * by_order[:, :, None], axis=1)


def body(
    tokens,
    cotangent,
    owner,
    token_local_adapter,
    segment,
    pair_sequence_order,
    frozen_margin_score,
    adapter_down_weight,
    adapter_up_weight,
):
    rows, width = tokens.shape
    out_width = cotangent.shape[1]
    n_dev = lax.axis_size("ad")
    me = lax.axis_index("ad")
    capacity = max(2, 2 * rows // n_dev)
    slots = n_dev * capacity
    count, rank_size, _ = adapter_down_weight.shape
    seqs = frozen_margin_score.shape[1]
    lanes = count * rank_size
    down = adapter_down_weight.reshape(lanes, width)
    up = adapter_up_weight.reshape(lanes, out_width)

    meta = jnp.concatenate(
        [
            owner.reshape(1, rows).astype(F32),
            token_local_adapter[None].astype(F32),
            segment.astype(F32),
            jnp.pad(
                jnp.concatenate([pair_sequence_order.astype(F32), frozen_margin_score], axis=1),
                ((0, 0), (0, rows - 2 * seqs)),
            ),
        ]
    )
    all_meta = lax.all_gather(meta, "ad")

    slot_index = rows_by_slot(owner.reshape(1, rows), n_dev, capacity)[0]
    to_slot = (jnp.arange(slots, dtype=jnp.int32)[:, None] == slot_index[None, :]).astype(BF16)
    send_g = jnp.dot(to_slot, cotangent, preferred_element_type=BF16)
    send_x = jnp.dot(to_slot, tokens, preferred_element_type=BF16)
    got_g = lax.all_to_all(
        send_g.reshape(n_dev, capacity, out_width), "ad", split_axis=0, concat_axis=0, tiled=True
    ).reshape(slots, out_width)
    got_x = lax.all_to_all(
        send_x.reshape(n_dev, capacity, width), "ad", split_axis=0, concat_axis=0, tiled=True
    ).reshape(slots, width)

    all_owner = all_meta[:, 0].astype(jnp.int32)
    all_slot = rows_by_slot(all_owner, n_dev, capacity)
    mine = (
        all_slot[:, None, :] == me * capacity + jnp.arange(capacity, dtype=jnp.int32)[None, :, None]
    ).astype(F32)
    slot_adapter = jnp.sum(mine * all_meta[:, 1][:, None, :], axis=2).reshape(slots)
    slot_seq = jnp.sum(mine * all_meta[:, 2][:, None, :], axis=2)
    slot_used = jnp.sum(mine, axis=2)
    slot_seq_hot = (
        slot_seq[:, :, None] == jnp.arange(seqs, dtype=F32)
    ).astype(F32) * slot_used[:, :, None]
    lane_adapter = (jnp.arange(lanes, dtype=jnp.int32) // rank_size).astype(F32)
    member = slot_adapter[:, None] == lane_adapter[None, :]

    contract = (((1,), (1,)), ((), ()))
    pulled = jnp.where(
        member, lax.dot_general(got_g, up, contract, preferred_element_type=F32), 0.0
    )
    pulled_rows = pulled.astype(BF16)
    projected = jnp.dot(pulled_rows, down, preferred_element_type=BF16)
    got_p = lax.all_to_all(
        projected.reshape(n_dev, capacity, width), "ad", split_axis=0, concat_axis=0, tiled=True
    ).reshape(slots, width)

    hidden_rows = jnp.where(
        member, lax.dot_general(got_x, down, contract, preferred_element_type=F32), 0.0
    ).astype(BF16)
    inner = SCALE * jnp.sum(hidden_rows.astype(F32) * pulled, axis=1)
    part = jnp.sum(slot_seq_hot * inner.reshape(n_dev, capacity)[:, :, None], axis=1)
    scores = lax.psum(part, "ad") + all_meta[:, 3, seqs : 2 * seqs]
    losses, seq_weight = pair_weights(scores, all_meta[:, 3, :seqs].astype(jnp.int32))

    slot_weight = LOSS_SCALE * jnp.sum(slot_seq_hot * seq_weight[:, None, :], axis=2).reshape(slots)
    upper = (slot_weight[:, None] * hidden_rows.astype(F32)).astype(BF16)
    lower = (slot_weight[:, None] * pulled_rows.astype(F32)).astype(BF16)
    rows_contract = (((0,), (0,)), ((), ()))
    grad_up = (
        SCALE * lax.dot_general(upper, got_g, rows_contract, preferred_element_type=F32)
    ).astype(BF16)
    grad_down = (
        SCALE * lax.dot_general(lower, got_x, rows_contract, preferred_element_type=F32)
    ).astype(BF16)

    my_weight = lax.dynamic_index_in_dim(seq_weight, me, keepdims=False)
    my_losses = lax.dynamic_index_in_dim(losses, me, keepdims=False)
    seq_hot = (segment[0][:, None] == jnp.arange(seqs, dtype=jnp.int32)).astype(F32)
    row_weight = LOSS_SCALE * jnp.sum(seq_hot * my_weight[None, :], axis=1)
    picked = lax.dot_general(to_slot, got_p, rows_contract, preferred_element_type=F32)
    input_grad = (SCALE * row_weight[:, None] * picked).astype(BF16)
    return (
        input_grad,
        grad_down.reshape(count, rank_size, width),
        grad_up.reshape(count, rank_size, out_width),
        my_losses,
    )


def solution(mesh):
    placed = (
        P(("grp", "ad"), None),
        P(("grp", "ad"), None),
        P(("grp", "ad"), None),
        P(("grp", "ad")),
        P(("grp", "ad"), None),
        P(("grp", "ad"), None),
        P(("grp", "ad"), None),
        P("ad", None, None),
        P("ad", None, None),
    )
    return jax.shard_map(
        body,
        mesh=mesh,
        in_specs=placed,
        out_specs=(
            P(("grp", "ad"), None),
            P(("grp", "ad"), None, None),
            P(("grp", "ad"), None, None),
            P(("grp", "ad")),
        ),
        check_vma=False,
    )
```

time: 283 us -> 267 us (0.943)
  the two profiles are of different devices: /device:TPU:15 before, /device:TPU:18 now
where the time goes in v1:
time: 267 us; the launch traced here: 266 us
  blocking collectives  213 us (80%)
  matrix products  24.8 us (9%)
  starting transfers between devices  15.7 us (6%)
  waiting for transfers between devices  9.1 us (3%)
    psum x1, blocking collectives, body(): scores = lax.psum(part, 'ad') + all_meta[:, 3, seqs:2 * seqs]  110 us
    all_gather x1, blocking collectives, body(): all_meta = lax.all_gather(meta, 'ad')  102 us
    all_to_all x1, waiting for transfers between devices, body(): lax.all_to_all(send_g.reshape(n_dev, capacity, out_width), 'ad', split_ax...  9.1 us
    all_to_all x1, starting transfers between devices, body(): lax.all_to_all(send_g.reshape(n_dev, capacity, out_width), 'ad', split_ax...  6.18 us
  transfers between devices with their start and end apart: 3, of which 1 were waited for; matrix products, arithmetic and copies ran while one was open for 5% of the time, Pallas kernels for 0%

profile of v1, /device:TPU:18, one launch (start us, length us, event | category | flops | bytes accessed | tf_op | source)
XLA Modules:
  0.0 266.3 jit_solution(8354700983086210959)
XLA Ops:
  0.6 0.0 copy-start
  0.6 1.1 fusion.8
  1.7 0.7 convert_add_fusion
  2.4 2.0 fusion.12
  4.4 6.2 %all-to-all-start.1 = ((bf16[16,16,1024]{2,1,0:T(8,128)(2,1)}), bf16[16,16,1024]{2,1,0:T(8,128)(2,1)S(1)}, u32[]{:S(2)}, u32[]{:S(2)}) async-start(bf16[16,16,1024]{2,1,0:T(8,128)(2,1)} %bitcast.18), calls=%async_computation.1 | async-start | bytes 1048576 | tf_op jit(solution)/shard_map/all_to_all | solution.py:76
  10.6 4.8 %fusion.13 = bf16[256,8192]{1,0:T(8,128)(2,1)} fusion(bf16[128,8192]{1,0:T(8,128)(2,1)} %param.9, s32[128]{0:T(128)S(1)} %convert_add_fusion), kind=kOutput, calls=%fused_computation.27 | convolution fusion | flops 536903680 | bytes 6291968 | tf_op jit(solution)/shard_map/dot_general | solution.py:75
  15.4 9.1 %all-to-all-done.1 = bf16[16,16,1024]{2,1,0:T(8,128)(2,1)S(1)} async-done(((bf16[16,16,1024]{2,1,0:T(8,128)(2,1)}), bf16[16,16,1024]{2,1,0:T(8,128)(2,1)S(1)}, u32[]{:S(2)}, u32[]{:S(2)}) %all-to-all-start.1) | async-done | bytes 524320 | tf_op jit(solution)/shard_map/all_to_all | solution.py:76
  24.5 5.1 %all-to-all-start = ((bf16[16,16,8192]{2,1,0:T(8,128)(2,1)}), bf16[16,16,8192]{2,1,0:T(8,128)(2,1)}, u32[]{:S(2)}, u32[]{:S(2)}) async-start(bf16[16,16,8192]{2,1,0:T(8,128)(2,1)} %bitcast.63), calls=%async_computation | async-start | bytes 8388608 | tf_op jit(solution)/shard_map/all_to_all | solution.py:79
  29.7 0.1 fusion.31
  29.8 102.5 %all-gather.1 = f32[16,4,128]{2,1,0:T(4,128)S(1)} all-gather(f32[1,4,128]{2,1,0:T(4,128)S(1)} %maximum_bitcast_fusion), channel_id=2, replica_groups=mesh['grp'=2,'ad'=16] {'ad'}, dimensions={0}, use_global_device_ids=true | all-gather | bytes 34816 | tf_op jit(solution)/shard_map/all_gather | solution.py:70
  132.3 0.2 fusion.6
  132.5 0.3 fusion.9
  132.8 0.1 eq.143
  132.9 0.3 convolution_select_fusion
  133.2 3.7 %multiply_reduce_fusion = (f32[256]{0:T(256)S(1)}, bf16[256,128]{0,1:T(8,128)(2,1)S(1)}, f32[256,128]{0,1:T(8,128)S(1)}) fusion(f32[256,128]{0,1:T(8,128)S(1)} %convolution_select_fusion, bf16[256,8192]{1,0:T(8,128)(2,1)} %bitcast.16, bf16[128,8192]{1,0:T(8,128)(2,1)S(1)} %bitcast.61, f32[128]{0:T(128)S(1)} %fusion.30, f32[256]{0:T(256)S(1)} %eq.143), kind=kOutput, calls=%fused_computation.24 | convolution fusion | flops 537100032 | bytes 6621696 | tf_op jit(solution)/shard_map/dot_general | solution.py:108
  137.0 0.1 copy.45
  137.1 3.2 %fusion.36 = bf16[16,16,8192]{2,1,0:T(8,128)(2,1)} fusion(bf16[16,16,128]{2,1,0:T(8,128)(2,1)S(1)} %bitcast.67, bf16[128,8192,1]{1,0,2:T(8,128)(2,1)S(1)} %bitcast.62), kind=kOutput, calls=%fused_computation.85 | convolution fusion | flops 536870912 | bytes 6356992 | tf_op jit(solution)/shard_map/dot_general | solution.py:102
  140.3 4.4 %all-to-all-start.2 = ((bf16[16,16,8192]{2,1,0:T(8,128)(2,1)}), bf16[16,16,8192]{2,1,0:T(8,128)(2,1)}, u32[]{:S(2)}, u32[]{:S(2)}) async-start(bf16[16,16,8192]{2,1,0:T(8,128)(2,1)} %fusion.36), calls=%async_computation.2 | async-start | bytes 8388608 | tf_op jit(solution)/shard_map/all_to_all | solution.py:103
  144.8 0.1 fusion.34
  144.8 0.1 copy.47
  144.9 0.1 copy.44
  145.0 0.1 mul.211
  145.1 0.1 fusion.24
  145.2 110.4 %psum.7 = f32[16,4]{0,1:T(4,128)S(1)} all-reduce(f32[16,4]{0,1:T(4,128)S(1)} %fusion.24), channel_id=1, replica_groups=mesh['grp'=2,'ad'=16] {'ad'}, use_global_device_ids=true, to_apply=%region_7.8 | all-reduce | flops 64 | bytes 512 | tf_op jit(solution)/shard_map/psum | solution.py:112
  255.7 0.7 dynamic-slice_reduce_fusion.1
  256.4 0.2 dynamic-slice_reduce_fusion
  256.6 0.1 fusion.25
  256.7 0.1 mul.234
  256.8 0.1 select_reduce_fusion.2
  256.9 0.9 fusion.2
  257.8 4.2 %fusion.1 = bf16[128,8192]{1,0:T(8,128)(2,1)} fusion(bf16[256,8192]{1,0:T(8,128)(2,1)} %bitcast.16, bf16[256,128]{0,1:T(8,128)(2,1)S(1)} %get-tuple-element.12, f32[256]{0:T(256)S(1)} %mul.234), kind=kOutput, calls=%fused_computation.3 | convolution fusion | flops 539066368 | bytes 6358016 | tf_op jit(solution)/shard_map/dot_general | solution.py:123
  262.1 4.3 %fusion = bf16[128,8192]{1,0:T(8,128)(2,1)} fusion(bf16[256,8192]{1,0:T(8,128)(2,1)} %bitcast.26, f32[128]{0:T(128)S(1)} %broadcast_multiply_fusion.4, s32[128]{0:T(128)S(1)} %convert_add_fusion), kind=kOutput, calls=%fused_computation.2 | convolution fusion | flops 539000832 | bytes 6292480 | tf_op jit(solution)/shard_map/dot_general | solution.py:130
  (37 shorter events, 0.2 us)
Async XLA Ops:
  0.6 132.6 %copy-start = (bf16[2,64,8192]{2,1,0:T(8,128)(2,1)S(1)}, bf16[2,64,8192]{2,1,0:T(8,128)(2,1)}, u32[]{:S(2)}) copy-start(bf16[2,64,8192]{2,1,0:T(8,128)(2,1)} %param.16) | copy-start | bytes 6291460
  4.4 20.1 %all-to-all-start.1 = ((bf16[16,16,1024]{2,1,0:T(8,128)(2,1)}), bf16[16,16,1024]{2,1,0:T(8,128)(2,1)S(1)}, u32[]{:S(2)}, u32[]{:S(2)}) async-start(bf16[16,16,1024]{2,1,0:T(8,128)(2,1)} %bitcast.18), calls=%async_computation.1 | async-start | bytes 1048576 | tf_op jit(solution)/shard_map/all_to_all | solution.py:76
  24.5 5.2 %copy-start.2 = (s32[1,4]{1,0:T(1,128)S(1)}, s32[1,4]{1,0:T(1,128)}, u32[]{:S(2)}) copy-start(s32[1,4]{1,0:T(1,128)} %param.14) | copy-start | bytes 52
  24.5 5.2 %copy-start.6 = (s32[1,128]{1,0:T(1,128)S(1)}, s32[1,128]{1,0:T(1,128)}, u32[]{:S(2)}) copy-start(s32[1,128]{1,0:T(1,128)} %param.13) | copy-start | bytes 1540
  24.5 5.2 %copy-start.3 = (f32[1,4]{1,0:T(1,128)S(1)}, f32[1,4]{1,0:T(1,128)}, u32[]{:S(2)}) copy-start(f32[1,4]{1,0:T(1,128)} %param.15) | copy-start | bytes 52
  24.5 5.3 %copy-start.4 = (s32[128,1]{0,1:T(1,128)S(1)}, s32[128,1]{0,1:T(1,128)}, u32[]{:S(2)}) copy-start(s32[128,1]{0,1:T(1,128)} %param.11) | copy-start | bytes 1540
  24.5 5.3 %copy-start.5 = (s32[128]{0:T(128)S(1)}, s32[128]{0:T(128)}, u32[]{:S(2)}) copy-start(s32[128]{0:T(128)} %param.12) | copy-start | bytes 1540
  24.5 108.4 %copy-start.1 = (bf16[2,64,1024]{2,1,0:T(8,128)(2,1)S(1)}, bf16[2,64,1024]{2,1,0:T(8,128)(2,1)}, u32[]{:S(2)}) copy-start(bf16[2,64,1024]{2,1,0:T(8,128)(2,1)} %param.17) | copy-start | bytes 786436
  24.5 108.7 %all-to-all-start = ((bf16[16,16,8192]{2,1,0:T(8,128)(2,1)}), bf16[16,16,8192]{2,1,0:T(8,128)(2,1)}, u32[]{:S(2)}, u32[]{:S(2)}) async-start(bf16[16,16,8192]{2,1,0:T(8,128)(2,1)} %bitcast.63), calls=%async_computation | async-start | bytes 8388608 | tf_op jit(solution)/shard_map/all_to_all | solution.py:79
  140.3 121.7 %all-to-all-start.2 = ((bf16[16,16,8192]{2,1,0:T(8,128)(2,1)}), bf16[16,16,8192]{2,1,0:T(8,128)(2,1)}, u32[]{:S(2)}, u32[]{:S(2)}) async-start(bf16[16,16,8192]{2,1,0:T(8,128)(2,1)} %fusion.36), calls=%async_computation.2 | async-start | bytes 8388608 | tf_op jit(solution)/shard_map/all_to_all | solution.py:103

commit v2 on v1

--- a/solution.py
+++ b/solution.py
@@ -6,6 +6,7 @@
 SCALE = 2.0
 BETA = 0.1
 LOSS_SCALE = 256.0
+PLANES = 4
 
 F32 = jnp.float32
 BF16 = jnp.bfloat16
@@ -31,6 +32,17 @@
     lean = jax.nn.sigmoid(-margin)
     by_order = jnp.stack([-BETA * lean, BETA * lean], axis=2).reshape(devices, seqs)
     return losses, jnp.sum(pick * by_order[:, :, None], axis=1)
+
+
+def share(block):
+    n_dev = lax.axis_size("ad")
+    return lax.all_to_all(
+        jnp.broadcast_to(block[None], (n_dev,) + block.shape),
+        "ad",
+        split_axis=0,
+        concat_axis=0,
+        tiled=True,
+    )
 
 
 def body(
@@ -46,15 +58,48 @@
 ):
     rows, width = tokens.shape
     out_width = cotangent.shape[1]
-    n_dev = lax.axis_size("ad")
-    me = lax.axis_index("ad")
+    n_grp, n_dev = lax.axis_size("grp"), lax.axis_size("ad")
+    grp, me = lax.axis_index("grp"), lax.axis_index("ad")
+    inner = n_dev // PLANES
+    plane = me // inner
     capacity = max(2, 2 * rows // n_dev)
     slots = n_dev * capacity
+    plane_slots = inner * capacity
     count, rank_size, _ = adapter_down_weight.shape
     seqs = frozen_margin_score.shape[1]
     lanes = count * rank_size
     down = adapter_down_weight.reshape(lanes, width)
     up = adapter_up_weight.reshape(lanes, out_width)
+
+    in_plane = [[z * inner + q for q in range(inner)] for z in range(PLANES)]
+    across = [[z * inner + q for z in range(PLANES)] for q in range(inner)]
+
+    def other_plane(block, flip):
+        return lax.ppermute(
+            block,
+            ("grp", "ad"),
+            [
+                (g * n_dev + z * inner + q, g * n_dev + (z ^ flip) * inner + q)
+                for g in range(n_grp)
+                for z in range(PLANES)
+                for q in range(inner)
+            ],
+        )
+
+    def other_grp(block):
+        return lax.ppermute(block, "grp", [(0, 1), (1, 0)])
+
+    half_mine = lax.dynamic_index_in_dim(adapter_down_weight, grp, keepdims=False)
+    half_other = lax.dynamic_index_in_dim(adapter_down_weight, 1 - grp, keepdims=False)
+    far = other_plane(half_mine, 2)
+    near = other_plane(half_mine, 1)
+    last = other_plane(far, 1)
+    halves = {
+        0: (half_mine, half_other),
+        2: (far, other_grp(far)),
+        1: (near, other_grp(near)),
+        3: (last, other_grp(last)),
+    }
 
     meta = jnp.concatenate(
         [
@@ -67,15 +112,16 @@
             ),
         ]
     )
-    all_meta = lax.all_gather(meta, "ad")
+    all_meta = share(meta)
 
     slot_index = rows_by_slot(owner.reshape(1, rows), n_dev, capacity)[0]
     to_slot = (jnp.arange(slots, dtype=jnp.int32)[:, None] == slot_index[None, :]).astype(BF16)
     send_g = jnp.dot(to_slot, cotangent, preferred_element_type=BF16)
-    send_x = jnp.dot(to_slot, tokens, preferred_element_type=BF16)
     got_g = lax.all_to_all(
         send_g.reshape(n_dev, capacity, out_width), "ad", split_axis=0, concat_axis=0, tiled=True
     ).reshape(slots, out_width)
+    send_x = jnp.dot(to_slot, tokens, preferred_element_type=BF16)
+    send_x, _ = lax.optimization_barrier((send_x, far))
     got_x = lax.all_to_all(
         send_x.reshape(n_dev, capacity, width), "ad", split_axis=0, concat_axis=0, tiled=True
     ).reshape(slots, width)
@@ -99,23 +145,54 @@
         member, lax.dot_general(got_g, up, contract, preferred_element_type=F32), 0.0
     )
     pulled_rows = pulled.astype(BF16)
-    projected = jnp.dot(pulled_rows, down, preferred_element_type=BF16)
-    got_p = lax.all_to_all(
-        projected.reshape(n_dev, capacity, width), "ad", split_axis=0, concat_axis=0, tiled=True
-    ).reshape(slots, width)
+
+    pulled_here = lax.all_to_all(
+        pulled_rows.reshape(PLANES, plane_slots, lanes),
+        "ad",
+        split_axis=0,
+        concat_axis=0,
+        tiled=True,
+        axis_index_groups=across,
+    ).reshape(PLANES, plane_slots, count, rank_size)
+    to_slot_planes = to_slot.reshape(PLANES, plane_slots, rows)
+    rows_contract = (((0,), (0,)), ((), ()))
+    picked = []
+    for flip in (0, 2, 1, 3):
+        mine_down, other_down = halves[flip]
+        from_plane = lax.dynamic_index_in_dim(pulled_here, plane ^ flip, keepdims=False)
+        made = jnp.dot(
+            lax.dynamic_index_in_dim(from_plane, grp, axis=1, keepdims=False),
+            mine_down,
+            preferred_element_type=F32,
+        ) + jnp.dot(
+            lax.dynamic_index_in_dim(from_plane, 1 - grp, axis=1, keepdims=False),
+            other_down,
+            preferred_element_type=F32,
+        )
+        got_p = lax.all_to_all(
+            made.astype(BF16).reshape(inner, capacity, width),
+            "ad",
+            split_axis=0,
+            concat_axis=0,
+            tiled=True,
+            axis_index_groups=in_plane,
+        ).reshape(plane_slots, width)
+        pick = lax.dynamic_index_in_dim(to_slot_planes, plane ^ flip, keepdims=False)
+        picked.append(
+            lax.dot_general(pick, got_p, rows_contract, preferred_element_type=F32)
+        )
 
     hidden_rows = jnp.where(
         member, lax.dot_general(got_x, down, contract, preferred_element_type=F32), 0.0
     ).astype(BF16)
-    inner = SCALE * jnp.sum(hidden_rows.astype(F32) * pulled, axis=1)
-    part = jnp.sum(slot_seq_hot * inner.reshape(n_dev, capacity)[:, :, None], axis=1)
-    scores = lax.psum(part, "ad") + all_meta[:, 3, seqs : 2 * seqs]
+    inner_product = SCALE * jnp.sum(hidden_rows.astype(F32) * pulled, axis=1)
+    part = jnp.sum(slot_seq_hot * inner_product.reshape(n_dev, capacity)[:, :, None], axis=1)
+    scores = jnp.sum(share(part), axis=0) + all_meta[:, 3, seqs : 2 * seqs]
     losses, seq_weight = pair_weights(scores, all_meta[:, 3, :seqs].astype(jnp.int32))
 
     slot_weight = LOSS_SCALE * jnp.sum(slot_seq_hot * seq_weight[:, None, :], axis=2).reshape(slots)
     upper = (slot_weight[:, None] * hidden_rows.astype(F32)).astype(BF16)
     lower = (slot_weight[:, None] * pulled_rows.astype(F32)).astype(BF16)
-    rows_contract = (((0,), (0,)), ((), ()))
     grad_up = (
         SCALE * lax.dot_general(upper, got_g, rows_contract, preferred_element_type=F32)
     ).astype(BF16)
@@ -127,8 +204,9 @@
     my_losses = lax.dynamic_index_in_dim(losses, me, keepdims=False)
     seq_hot = (segment[0][:, None] == jnp.arange(seqs, dtype=jnp.int32)).astype(F32)
     row_weight = LOSS_SCALE * jnp.sum(seq_hot * my_weight[None, :], axis=1)
-    picked = lax.dot_general(to_slot, got_p, rows_contract, preferred_element_type=F32)
-    input_grad = (SCALE * row_weight[:, None] * picked).astype(BF16)
+    input_grad = (
+        SCALE * row_weight[:, None] * ((picked[0] + picked[1]) + (picked[2] + picked[3]))
+    ).astype(BF16)
     return (
         input_grad,
         grad_down.reshape(count, rank_size, width),

time: 267 us -> 314 us (1.18)
  the two profiles are of different devices: /device:TPU:18 before, /device:TPU:0 now
where the time goes in v2:
time: 314 us; the launch traced here: 313 us
  waiting for transfers between devices  189 us (60%)
  starting transfers between devices  65.9 us (21%)
  matrix products  47.9 us (15%)
  local copies, waits for them, and re-layouts  5.44 us (2%)
  other arithmetic  4.29 us (1%)
    all_to_all x1, waiting for transfers between devices, body(): lax.all_to_all(send_x.reshape(n_dev, capacity, width), 'ad', split_axis=0...  74.5 us
    ppermute x3, waiting for transfers between devices, other_plane(): lax.ppermute(block, ('grp', 'ad'), [(g * n_dev + z * inner + q, g * n_dev...  53 us
    all_to_all x4, waiting for transfers between devices, body(): lax.all_to_all(made.astype(BF16).reshape(inner, capacity, width), 'ad', s...  34.4 us
    all_to_all x2, starting transfers between devices, share(): lax.all_to_all(jnp.broadcast_to(block[None], (n_dev,) + block.shape), 'ad...  27.1 us
    ppermute x3, waiting for transfers between devices, other_grp(): return lax.ppermute(block, 'grp', [(0, 1), (1, 0)])  20.8 us
    dot_general x4, matrix products, body(): lax.dot_general(pick, got_p, rows_contract, preferred_element_type=F32)  16.5 us
    all_to_all x4, starting transfers between devices, body(): lax.all_to_all(made.astype(BF16).reshape(inner, capacity, width), 'ad', s...  16.3 us
    dot_general x4, matrix products, body(): jnp.dot(lax.dynamic_index_in_dim(from_plane, 1 - grp, axis=1, keepdims=Fa...  9.33 us
  transfers between devices with their start and end apart: 15, of which 11 were waited for; matrix products, arithmetic and copies ran while one was open for 15% of the time, Pallas kernels for 0%

profile of v2, /device:TPU:0, one launch (start us, length us, event | category | flops | bytes accessed | tf_op | source)
XLA Modules:
  0.0 313.1 jit_solution(3874281752141440152)
XLA Ops:
  4.8 7.4 %all-to-all-start = ((f32[16,4,128]{2,1,0:T(4,128)}), f32[16,4,128]{2,1,0:T(4,128)S(1)}, u32[]{:S(2)}, u32[]{:S(2)}) async-start(f32[16,4,128]{2,1,0:T(4,128)} %broadcast_in_dim.8), calls=%async_computation | async-start | bytes 65536 | tf_op jit(solution)/shard_map/all_to_all | solution.py:39
  13.3 2.8 collective-permute-start
  18.9 3.6 %all-to-all-start.2 = ((bf16[16,16,1024]{2,1,0:T(8,128)(2,1)}), bf16[16,16,1024]{2,1,0:T(8,128)(2,1)S(1)}, u32[]{:S(2)}, u32[]{:S(2)}) async-start(bf16[16,16,1024]{2,1,0:T(8,128)(2,1)} %bitcast.18), calls=%async_computation.2 | async-start | bytes 1048576 | tf_op jit(solution)/shard_map/all_to_all | solution.py:120
  22.4 4.8 %fusion.21 = bf16[256,8192]{1,0:T(8,128)(2,1)} fusion(bf16[128,8192]{1,0:T(8,128)(2,1)} %param.9, s32[128]{0:T(128)S(1)} %convert_add_fusion), kind=kOutput, calls=%fused_computation.41 | convolution fusion | flops 536903680 | bytes 6291968 | tf_op jit(solution)/shard_map/dot_general | solution.py:123
  27.2 41.3 %collective-permute-done = bf16[64,8192]{1,0:T(8,128)(2,1)} collective-permute-done((bf16[64,8192]{1,0:T(8,128)(2,1)}, bf16[64,8192]{1,0:T(8,128)(2,1)}, u32[]{:S(2)}, u32[]{:S(2)}) %collective-permute-start) | collective-permute-done | bytes 1048608 | tf_op jit(solution)/shard_map/ppermute | solution.py:78
  68.5 3.6 %all-to-all-done.2 = bf16[16,16,1024]{2,1,0:T(8,128)(2,1)S(1)} async-done(((bf16[16,16,1024]{2,1,0:T(8,128)(2,1)}), bf16[16,16,1024]{2,1,0:T(8,128)(2,1)S(1)}, u32[]{:S(2)}, u32[]{:S(2)}) %all-to-all-start.2) | async-done | bytes 524320 | tf_op jit(solution)/shard_map/all_to_all | solution.py:120
  72.1 7.3 %all-to-all-start.1 = ((bf16[16,16,8192]{2,1,0:T(8,128)(2,1)}), bf16[16,16,8192]{2,1,0:T(8,128)(2,1)}, u32[]{:S(2)}, u32[]{:S(2)}) async-start(bf16[16,16,8192]{2,1,0:T(8,128)(2,1)} %bitcast.124), calls=%async_computation.1 | async-start | bytes 8388608 | tf_op jit(solution)/shard_map/all_to_all | solution.py:125
  79.4 1.9 collective-permute-start.2
  82.7 74.5 %all-to-all-done.1 = bf16[16,16,8192]{2,1,0:T(8,128)(2,1)} async-done(((bf16[16,16,8192]{2,1,0:T(8,128)(2,1)}), bf16[16,16,8192]{2,1,0:T(8,128)(2,1)}, u32[]{:S(2)}, u32[]{:S(2)}) %all-to-all-start.1) | async-done | bytes 4194336 | tf_op jit(solution)/shard_map/all_to_all | solution.py:125
  157.2 3.7 %multiply_reduce_fusion = (f32[256]{0:T(256)S(1)}, bf16[256,128]{0,1:T(8,128)(2,1)S(1)}, f32[256,128]{0,1:T(8,128)S(1)}) fusion(f32[256,128]{0,1:T(8,128)S(1)} %convolution_select_fusion, bf16[256,8192]{1,0:T(8,128)(2,1)} %bitcast.16, bf16[128,8192]{1,0:T(8,128)(2,1)S(1)} %bitcast.123, f32[128]{0:T(128)S(1)} %fusion.60, f32[256]{0:T(256)S(1)} %eq.156), kind=kOutput, calls=%fused_computation.38 | convolution fusion | flops 537100032 | bytes 6621696 | tf_op jit(solution)/shard_map/dot_general | solution.py:186
  161.7 19.7 %all-to-all-start.3 = ((f32[16,16,4]{1,2,0:T(4,128)}), f32[16,16,4]{1,2,0:T(4,128)S(1)}, u32[]{:S(2)}, u32[]{:S(2)}) async-start(f32[16,16,4]{1,2,0:T(4,128)} %broadcast_in_dim.10), calls=%async_computation.3 | async-start | bytes 65536 | tf_op jit(solution)/shard_map/all_to_all | solution.py:39
  183.5 11.7 %collective-permute-done.4 = bf16[64,8192]{1,0:T(8,128)(2,1)} collective-permute-done((bf16[64,8192]{1,0:T(8,128)(2,1)}, bf16[64,8192]{1,0:T(8,128)(2,1)}, u32[]{:S(2)}, u32[]{:S(2)}) %collective-permute-start.4) | collective-permute-done | bytes 1048608 | tf_op jit(solution)/shard_map/ppermute | solution.py:78
  198.4 3.3 %all-to-all-start.4 = ((bf16[4,64,128]{2,1,0:T(8,128)(2,1)}), bf16[4,64,128]{2,1,0:T(8,128)(2,1)S(1)}, u32[]{:S(2)}, u32[]{:S(2)}) async-start(bf16[4,64,128]{2,1,0:T(8,128)(2,1)} %bitcast.26), calls=%async_computation.4 | async-start | bytes 131072 | tf_op jit(solution)/shard_map/all_to_all | solution.py:149
  203.1 4.3 %fusion.2 = bf16[128,8192]{1,0:T(8,128)(2,1)} fusion(bf16[256,8192]{1,0:T(8,128)(2,1)} %bitcast.16, bf16[256,128]{0,1:T(8,128)(2,1)S(1)} %get-tuple-element.14, f32[256]{0:T(256)S(1)} %mul.237), kind=kOutput, calls=%fused_computation.5 | convolution fusion | flops 539066368 | bytes 6358016 | tf_op jit(solution)/shard_map/dot_general | solution.py:200
  207.8 1.6 fusion.46
  209.5 20.8 %collective-permute-done.3 = bf16[64,8192]{1,0:T(8,128)(2,1)} collective-permute-done((bf16[64,8192]{1,0:T(8,128)(2,1)}, bf16[64,8192]{1,0:T(8,128)(2,1)}, u32[]{:S(2)}, u32[]{:S(2)}) %collective-permute-start.3) | collective-permute-done | bytes 1048608 | tf_op jit(solution)/shard_map/ppermute | solution.py:90
  230.3 2.6 fusion.6
  232.9 3.5 %all-to-all-start.7 = ((bf16[4,16,8192]{2,1,0:T(8,128)(2,1)}), bf16[4,16,8192]{2,1,0:T(8,128)(2,1)S(1)}, u32[]{:S(2)}, u32[]{:S(2)}) async-start(bf16[4,16,8192]{2,1,0:T(8,128)(2,1)} %bitcast.130), calls=%async_computation.7 | async-start | bytes 2097152 | tf_op jit(solution)/shard_map/all_to_all | solution.py:172
  236.4 1.6 fusion.48
  239.5 11.3 %all-to-all-done.7 = bf16[4,16,8192]{2,1,0:T(8,128)(2,1)S(1)} async-done(((bf16[4,16,8192]{2,1,0:T(8,128)(2,1)}), bf16[4,16,8192]{2,1,0:T(8,128)(2,1)S(1)}, u32[]{:S(2)}, u32[]{:S(2)}) %all-to-all-start.7) | async-done | bytes 1048608 | tf_op jit(solution)/shard_map/all_to_all | solution.py:172
  250.9 4.3 %all-to-all-start.5 = ((bf16[4,16,8192]{2,1,0:T(8,128)(2,1)}), bf16[4,16,8192]{2,1,0:T(8,128)(2,1)}, u32[]{:S(2)}, u32[]{:S(2)}) async-start(bf16[4,16,8192]{2,1,0:T(8,128)(2,1)} %bitcast.30), calls=%async_computation.5 | async-start | bytes 2097152 | tf_op jit(solution)/shard_map/all_to_all | solution.py:172
  257.5 2.6 fusion.5
  260.1 9.5 %all-to-all-done.5 = bf16[4,16,8192]{2,1,0:T(8,128)(2,1)} async-done(((bf16[4,16,8192]{2,1,0:T(8,128)(2,1)}), bf16[4,16,8192]{2,1,0:T(8,128)(2,1)}, u32[]{:S(2)}, u32[]{:S(2)}) %all-to-all-start.5) | async-done | bytes 1048608 | tf_op jit(solution)/shard_map/all_to_all | solution.py:172
  269.6 4.3 %all-to-all-start.6 = ((bf16[4,16,8192]{2,1,0:T(8,128)(2,1)}), bf16[4,16,8192]{2,1,0:T(8,128)(2,1)}, u32[]{:S(2)}, u32[]{:S(2)}) async-start(bf16[4,16,8192]{2,1,0:T(8,128)(2,1)} %bitcast.128), calls=%async_computation.6 | async-start | bytes 2097152 | tf_op jit(solution)/shard_map/all_to_all | solution.py:172
  275.6 2.6 fusion.7
  278.2 3.9 %fusion.39 = f32[128,8192]{1,0:T(8,128)} fusion(bf16[64,8192]{1,0:T(8,128)(2,1)} %bitcast.31, pred[4,64,128]{2,1,0:T(32,128)(4,1)S(1)} %broadcast_compare_fusion, s32[]{:T(128)S(6)} %select_n.83), kind=kOutput, calls=%fused_computation.64 | convolution fusion | flops 134217728 | bytes 5251076 | tf_op jit(solution)/shard_map/dot_general | solution.py:182
  282.1 6.3 %all-to-all-done.6 = bf16[4,16,8192]{2,1,0:T(8,128)(2,1)} async-done(((bf16[4,16,8192]{2,1,0:T(8,128)(2,1)}), bf16[4,16,8192]{2,1,0:T(8,128)(2,1)}, u32[]{:S(2)}, u32[]{:S(2)}) %all-to-all-start.6) | async-done | bytes 1048608 | tf_op jit(solution)/shard_map/all_to_all | solution.py:172
  288.4 4.2 %all-to-all-start.8 = ((bf16[4,16,8192]{2,1,0:T(8,128)(2,1)}), bf16[4,16,8192]{2,1,0:T(8,128)(2,1)}, u32[]{:S(2)}, u32[]{:S(2)}) async-start(bf16[4,16,8192]{2,1,0:T(8,128)(2,1)} %bitcast.129), calls=%async_computation.8 | async-start | bytes 2097152 | tf_op jit(solution)/shard_map/all_to_all | solution.py:172
  292.7 2.7 fusion.36
  296.1 3.9 %convolution_add_fusion.1 = f32[128,8192]{1,0:T(8,128)} fusion(f32[128,8192]{1,0:T(8,128)S(1)} %copy-done.1, bf16[64,8192]{1,0:T(8,128)(2,1)} %bitcast.36, pred[4,64,128]{2,1,0:T(32,128)(4,1)S(1)} %broadcast_compare_fusion, s32[]{:T(128)S(6)} %select_n.88), kind=kOutput, calls=%fused_computation.4 | convolution fusion | flops 135266304 | bytes 9445380 | tf_op jit(solution)/shard_map/dot_general | solution.py:182
  300.0 7.2 %all-to-all-done.8 = bf16[4,16,8192]{2,1,0:T(8,128)(2,1)} async-done(((bf16[4,16,8192]{2,1,0:T(8,128)(2,1)}), bf16[4,16,8192]{2,1,0:T(8,128)(2,1)}, u32[]{:S(2)}, u32[]{:S(2)}) %all-to-all-start.8) | async-done | bytes 1048608 | tf_op jit(solution)/shard_map/all_to_all | solution.py:172
  307.2 5.9 %fusion.3 = bf16[128,8192]{1,0:T(8,128)(2,1)} fusion(f32[128,8192]{1,0:T(8,128)} %convolution_add_fusion.1, f32[128,8192]{1,0:T(8,128)} %fusion.36, bf16[64,8192]{1,0:T(8,128)(2,1)} %bitcast.46, f32[128]{0:T(128)S(1)} %broadcast_multiply_fusion.4, pred[4,64,128]{2,1,0:T(32,128)(4,1)S(1)} %broadcast_compare_fusion, s32[]{:T(128)S(6)} %select_n.92), kind=kOutput, calls=%fused_computation.6 | convolution fusion | flops 138412032 | bytes 11543044 | tf_op jit(solution)/shard_map/dot_general | solution.py:182
  (75 shorter events, 23.3 us)
Async XLA Ops:
  0.6 11.6 %copy-start = (bf16[2,64,8192]{2,1,0:T(8,128)(2,1)S(1)}, bf16[2,64,8192]{2,1,0:T(8,128)(2,1)}, u32[]{:S(2)}) copy-start(bf16[2,64,8192]{2,1,0:T(8,128)(2,1)} %param.16) | copy-start | bytes 6291460
  0.6 15.4 %copy-start.4 = (s32[128,1]{0,1:T(1,128)S(1)}, s32[128,1]{0,1:T(1,128)}, u32[]{:S(2)}) copy-start(s32[128,1]{0,1:T(1,128)} %param.11) | copy-start | bytes 1540
  0.7 15.7 %copy-start.2 = (bf16[128,1024]{1,0:T(8,128)(2,1)S(1)}, bf16[128,1024]{1,0:T(8,128)(2,1)}, u32[]{:S(2)}) copy-start(bf16[128,1024]{1,0:T(8,128)(2,1)} %param.10) | copy-start | bytes 786436
  4.8 14.0 %all-to-all-start = ((f32[16,4,128]{2,1,0:T(4,128)}), f32[16,4,128]{2,1,0:T(4,128)S(1)}, u32[]{:S(2)}, u32[]{:S(2)}) async-start(f32[16,4,128]{2,1,0:T(4,128)} %broadcast_in_dim.8), calls=%async_computation | async-start | bytes 65536 | tf_op jit(solution)/shard_map/all_to_all | solution.py:39
  13.3 55.3 %collective-permute-start = (bf16[64,8192]{1,0:T(8,128)(2,1)}, bf16[64,8192]{1,0:T(8,128)(2,1)}, u32[]{:S(2)}, u32[]{:S(2)}) collective-permute-start(bf16[64,8192]{1,0:T(8,128)(2,1)} %dynamic-slice_bitcast_fusion), channel_id=1, source_target_pairs={{0,8},{1,9},{2,10},{3,11},{4,12},{5,13},{6,14},{7,15},{8,0},{9,1},... | collective-permute-start | bytes 3145736 | tf_op jit(solution)/shard_map/ppermute | solution.py:78
  18.9 53.2 %all-to-all-start.2 = ((bf16[16,16,1024]{2,1,0:T(8,128)(2,1)}), bf16[16,16,1024]{2,1,0:T(8,128)(2,1)S(1)}, u32[]{:S(2)}, u32[]{:S(2)}) async-start(bf16[16,16,1024]{2,1,0:T(8,128)(2,1)} %bitcast.18), calls=%async_computation.2 | async-start | bytes 1048576 | tf_op jit(solution)/shard_map/all_to_all | solution.py:120
  72.1 10.3 %copy-start.3 = (bf16[2,64,1024]{2,1,0:T(8,128)(2,1)S(1)}, bf16[2,64,1024]{2,1,0:T(8,128)(2,1)}, u32[]{:S(2)}) copy-start(bf16[2,64,1024]{2,1,0:T(8,128)(2,1)} %param.17) | copy-start | bytes 786436
  72.1 85.1 %all-to-all-start.1 = ((bf16[16,16,8192]{2,1,0:T(8,128)(2,1)}), bf16[16,16,8192]{2,1,0:T(8,128)(2,1)}, u32[]{:S(2)}, u32[]{:S(2)}) async-start(bf16[16,16,8192]{2,1,0:T(8,128)(2,1)} %bitcast.124), calls=%async_computation.1 | async-start | bytes 8388608 | tf_op jit(solution)/shard_map/all_to_all | solution.py:125
  79.4 103.6 %collective-permute-start.2 = (bf16[64,8192]{1,0:T(8,128)(2,1)}, bf16[64,8192]{1,0:T(8,128)(2,1)}, u32[]{:S(2)}, u32[]{:S(2)}) collective-permute-start(bf16[64,8192]{1,0:T(8,128)(2,1)} %dynamic-slice_bitcast_fusion), channel_id=1, source_target_pairs={{0,4},{1,5},{2,6},{3,7},{4,0},{5,1},{6,2},{7,3},{8,12},{9,13},{10,... | collective-permute-start | bytes 3145736 | tf_op jit(solution)/shard_map/ppermute | solution.py:78
  82.2 113.1 %collective-permute-start.4 = (bf16[64,8192]{1,0:T(8,128)(2,1)}, bf16[64,8192]{1,0:T(8,128)(2,1)}, u32[]{:S(2)}, u32[]{:S(2)}) collective-permute-start(bf16[64,8192]{1,0:T(8,128)(2,1)} %collective-permute-done), channel_id=1, source_target_pairs={{0,4},{1,5},{2,6},{3,7},{4,0},{5,1},{6,2},{7,3},{8,12},{9,13},{10,... | collective-permute-start | bytes 3145736 | tf_op jit(solution)/shard_map/ppermute | solution.py:78
  161.7 36.6 %all-to-all-start.3 = ((f32[16,16,4]{1,2,0:T(4,128)}), f32[16,16,4]{1,2,0:T(4,128)S(1)}, u32[]{:S(2)}, u32[]{:S(2)}) async-start(f32[16,16,4]{1,2,0:T(4,128)} %broadcast_in_dim.10), calls=%async_computation.3 | async-start | bytes 65536 | tf_op jit(solution)/shard_map/all_to_all | solution.py:39
  181.5 76.0 %collective-permute-start.1 = (bf16[64,8192]{1,0:T(8,128)(2,1)}, bf16[64,8192]{1,0:T(8,128)(2,1)}, u32[]{:S(2)}, u32[]{:S(2)}) collective-permute-start(bf16[64,8192]{1,0:T(8,128)(2,1)} %collective-permute-done), channel_id=1, source_target_pairs={{0,16},{16,0},{1,17},{17,1},{2,18},{18,2},{3,19},{19,3},{4,20},{20... | collective-permute-start | bytes 3145736 | tf_op jit(solution)/shard_map/ppermute | solution.py:90
  183.0 47.3 %collective-permute-start.3 = (bf16[64,8192]{1,0:T(8,128)(2,1)}, bf16[64,8192]{1,0:T(8,128)(2,1)}, u32[]{:S(2)}, u32[]{:S(2)}) collective-permute-start(bf16[64,8192]{1,0:T(8,128)(2,1)} %collective-permute-done.2), channel_id=1, source_target_pairs={{0,16},{16,0},{1,17},{17,1},{2,18},{18,2},{3,19},{19,3},{4,20},{20... | collective-permute-start | bytes 3145736 | tf_op jit(solution)/shard_map/ppermute | solution.py:90
  195.2 80.3 %collective-permute-start.5 = (bf16[64,8192]{1,0:T(8,128)(2,1)}, bf16[64,8192]{1,0:T(8,128)(2,1)}, u32[]{:S(2)}, u32[]{:S(2)}) collective-permute-start(bf16[64,8192]{1,0:T(8,128)(2,1)} %collective-permute-done.4), channel_id=1, source_target_pairs={{0,16},{16,0},{1,17},{17,1},{2,18},{18,2},{3,19},{19,3},{4,20},{20... | collective-permute-start | bytes 3145736 | tf_op jit(solution)/shard_map/ppermute | solution.py:90
  198.4 9.1 %all-to-all-start.4 = ((bf16[4,64,128]{2,1,0:T(8,128)(2,1)}), bf16[4,64,128]{2,1,0:T(8,128)(2,1)S(1)}, u32[]{:S(2)}, u32[]{:S(2)}) async-start(bf16[4,64,128]{2,1,0:T(8,128)(2,1)} %bitcast.26), calls=%async_computation.4 | async-start | bytes 131072 | tf_op jit(solution)/shard_map/all_to_all | solution.py:149
  203.1 4.3 %copy-start.5 = (s32[1,128]{1,0:T(1,128)S(1)}, s32[1,128]{1,0:T(1,128)}, u32[]{:S(2)}) copy-start(s32[1,128]{1,0:T(1,128)} %param.13) | copy-start | bytes 1540
  232.9 18.0 %all-to-all-start.7 = ((bf16[4,16,8192]{2,1,0:T(8,128)(2,1)}), bf16[4,16,8192]{2,1,0:T(8,128)(2,1)S(1)}, u32[]{:S(2)}, u32[]{:S(2)}) async-start(bf16[4,16,8192]{2,1,0:T(8,128)(2,1)} %bitcast.130), calls=%async_computation.7 | async-start | bytes 2097152 | tf_op jit(solution)/shard_map/all_to_all | solution.py:172
  250.9 18.8 %all-to-all-start.5 = ((bf16[4,16,8192]{2,1,0:T(8,128)(2,1)}), bf16[4,16,8192]{2,1,0:T(8,128)(2,1)}, u32[]{:S(2)}, u32[]{:S(2)}) async-start(bf16[4,16,8192]{2,1,0:T(8,128)(2,1)} %bitcast.30), calls=%async_computation.5 | async-start | bytes 2097152 | tf_op jit(solution)/shard_map/all_to_all | solution.py:172
  269.6 18.8 %all-to-all-start.6 = ((bf16[4,16,8192]{2,1,0:T(8,128)(2,1)}), bf16[4,16,8192]{2,1,0:T(8,128)(2,1)}, u32[]{:S(2)}, u32[]{:S(2)}) async-start(bf16[4,16,8192]{2,1,0:T(8,128)(2,1)} %bitcast.128), calls=%async_computation.6 | async-start | bytes 2097152 | tf_op jit(solution)/shard_map/all_to_all | solution.py:172
  288.4 18.8 %all-to-all-start.8 = ((bf16[4,16,8192]{2,1,0:T(8,128)(2,1)}), bf16[4,16,8192]{2,1,0:T(8,128)(2,1)}, u32[]{:S(2)}, u32[]{:S(2)}) async-start(bf16[4,16,8192]{2,1,0:T(8,128)(2,1)} %bitcast.129), calls=%async_computation.8 | async-start | bytes 2097152 | tf_op jit(solution)/shard_map/all_to_all | solution.py:172
  292.7 3.4 %copy-start.1 = (f32[128,8192]{1,0:T(8,128)S(1)}, f32[128,8192]{1,0:T(8,128)}, u32[]{:S(2)}) copy-start(f32[128,8192]{1,0:T(8,128)} %fusion.39) | copy-start | bytes 12582916

commit v3 on v1

v3 whole, which is shorter than its diff:
```python
import functools

import jax
import jax.numpy as jnp
from jax import lax
from jax.experimental import pallas as pl
from jax.experimental.pallas import tpu as pltpu
from jax.sharding import PartitionSpec as P

SCALE = 2.0
BETA = 0.1
LOSS_SCALE = 256.0
MARKS = 128
GATE_FLOPS = 2 * 10**11

F32 = jnp.float32
BF16 = jnp.bfloat16


def gate(*arrays):
    return pl.pallas_call(
        lambda *refs: None,
        out_shape=[jax.ShapeDtypeStruct(array.shape, array.dtype) for array in arrays],
        in_specs=[pl.BlockSpec(memory_space=pl.ANY)] * len(arrays),
        out_specs=[pl.BlockSpec(memory_space=pl.ANY)] * len(arrays),
        input_output_aliases={at: at for at in range(len(arrays))},
        cost_estimate=pl.CostEstimate(flops=GATE_FLOPS, bytes_accessed=0, transcendentals=0),
        name="gate",
    )(*arrays)


def project_kernel(side, split, capacity, out_width, n_outs, spot_ref, g_ref, which, *refs):
    n_spots = g_ref.shape[0]
    n_parts = (len(refs) - n_outs) // 2
    mine, other, outs = refs[:n_parts], refs[n_parts : 2 * n_parts], refs[2 * n_parts :]
    first = side * capacity
    spot = spot_ref[0]
    rows = jnp.concatenate(
        [g_ref[spot ^ flip, first : first + capacity, :] for flip in range(n_spots)], axis=0
    )
    marks = rows[:, out_width:].astype(F32)
    contract = (((1,), (1,)), ((), ()))
    pulls = []
    for at, parts in enumerate((mine, other)):
        member = jnp.sum(marks * which[at : at + 1, :], axis=1, keepdims=True)
        pull = lax.dot_general(
            rows[:, :out_width], parts[0][:, :out_width], contract, preferred_element_type=F32
        )
        pulls.append((member * pull).astype(BF16))
    done = 0
    for at in range(n_parts):
        start, end = (out_width if at == 0 else 0), mine[at].shape[1]
        while start < end:
            size = min(1024, end - start)
            columns = slice(start, start + size)
            made = jnp.dot(pulls[0], mine[at][:, columns], preferred_element_type=F32)
            made = made + jnp.dot(pulls[1], other[at][:, columns], preferred_element_type=F32)
            made = made.astype(BF16)
            for flip in range(n_spots):
                row = made[flip * capacity : (flip + 1) * capacity]
                if split:
                    chip = flip // 2 * capacity
                    outs[flip % 2][chip : chip + capacity, done : done + size] = row
                else:
                    core = flip % 2 * capacity
                    outs[flip // 2][core : core + capacity, done : done + size] = row
            start, done = start + size, done + size


def project(side, split, capacity, out_width, width, spot, got_g, which, mine, other):
    n_spots = got_g.shape[0]
    chips = n_spots // 2
    blocks = [(chips * capacity, width)] * 2 if split else [(2 * capacity, width)] * chips
    if capacity % 16 == 0:
        return pl.pallas_call(
            functools.partial(project_kernel, side, split, capacity, out_width, len(blocks)),
            out_shape=[jax.ShapeDtypeStruct(block, BF16) for block in blocks],
            in_specs=[pl.BlockSpec(memory_space=pltpu.SMEM)]
            + [pl.BlockSpec(memory_space=pltpu.VMEM)] * (2 + len(mine) + len(other)),
            cost_estimate=pl.CostEstimate(flops=1000, bytes_accessed=1000, transcendentals=0),
            name="project",
        )(spot.reshape(1), got_g, which, *mine, *other)
    order = spot ^ jnp.arange(n_spots, dtype=jnp.int32)
    rows = got_g[order, side * capacity : (side + 1) * capacity].reshape(n_spots * capacity, -1)
    marks = rows[:, out_width:].astype(F32)
    made = 0.0
    for at, parts in enumerate((mine, other)):
        whole = jnp.concatenate(parts, axis=1)
        pull = jnp.dot(rows[:, :out_width], whole[:, :out_width].T, preferred_element_type=F32)
        pull = (jnp.sum(marks * which[at], axis=1, keepdims=True) * pull).astype(BF16)
        made = made + jnp.dot(pull, whole[:, out_width:], preferred_element_type=F32)
    made = made.astype(BF16).reshape(chips, 2, capacity, width)
    if split:
        return [made[:, core].reshape(chips * capacity, width) for core in range(2)]
    return list(made.reshape(chips, 2 * capacity, width))


def select_kernel(pick_ref, weight_ref, *refs):
    blocks, out = refs[:-1], refs[-1]
    rows = jnp.concatenate([block[...] for block in blocks], axis=0)
    picked = jnp.dot(pick_ref[...], rows, preferred_element_type=F32)
    out[...] = (weight_ref[...] * picked).astype(BF16)


def select(pick, weight, blocks, used):
    width = blocks[0].shape[1]
    rows, slots = pick.shape
    if any(size % 16 for size in used):
        blocks = [block[:size] for block, size in zip(blocks, used)]
        picked = jnp.dot(pick, jnp.concatenate(blocks), preferred_element_type=F32)
        return (weight * picked).astype(BF16)
    columns = 2048
    return pl.pallas_call(
        select_kernel,
        out_shape=jax.ShapeDtypeStruct((rows, width), BF16),
        grid=(width // columns,),
        in_specs=[
            pl.BlockSpec((rows, slots), lambda i: (0, 0)),
            pl.BlockSpec((rows, 1), lambda i: (0, 0)),
        ]
        + [pl.BlockSpec((size, columns), lambda i: (0, i)) for size in used],
        out_specs=pl.BlockSpec((rows, columns), lambda i: (0, i)),
        cost_estimate=pl.CostEstimate(
            flops=2 * rows * slots * width,
            bytes_accessed=2 * (rows + slots) * width,
            transcendentals=0,
        ),
        name="select",
    )(pick, weight, *blocks)


def rows_by_slot(owners, n_dev, capacity):
    rows = owners.shape[1]
    hot = (owners[:, :, None] == jnp.arange(n_dev, dtype=jnp.int32)).astype(BF16)
    earlier = (
        jnp.arange(rows, dtype=jnp.int32)[:, None] > jnp.arange(rows, dtype=jnp.int32)[None, :]
    ).astype(BF16)
    before = jnp.einsum("rq,dqk->drk", earlier, hot, preferred_element_type=F32)
    rank = jnp.sum(before * hot.astype(F32), axis=2).astype(jnp.int32)
    return owners * capacity + rank


def pair_weights(scores, order):
    devices, seqs = scores.shape
    pick = (order[:, :, None] == jnp.arange(seqs, dtype=jnp.int32)).astype(F32)
    ordered = jnp.sum(pick * scores[:, None, :], axis=2).reshape(devices, seqs // 2, 2)
    margin = BETA * (ordered[:, :, 0] - ordered[:, :, 1])
    losses = jax.nn.softplus(-margin)
    lean = jax.nn.sigmoid(-margin)
    by_order = jnp.stack([-BETA * lean, BETA * lean], axis=2).reshape(devices, seqs)
    return losses, jnp.sum(pick * by_order[:, :, None], axis=1)


def share(block):
    n_dev = lax.axis_size("ad")
    return lax.all_to_all(
        jnp.broadcast_to(block[None], (n_dev,) + block.shape),
        "ad",
        split_axis=0,
        concat_axis=0,
        tiled=True,
    )


def body(
    tokens,
    cotangent,
    owner,
    token_local_adapter,
    segment,
    pair_sequence_order,
    frozen_margin_score,
    adapter_down_weight,
    adapter_up_weight,
):
    rows, width = tokens.shape
    out_width = cotangent.shape[1]
    n_grp, n_dev = lax.axis_size("grp"), lax.axis_size("ad")
    grp, me = lax.axis_index("grp"), lax.axis_index("ad")
    half_size = n_dev // 2
    spot = me % half_size
    capacity = max(2, 2 * rows // n_dev)
    slots = n_dev * capacity
    count, rank_size, _ = adapter_down_weight.shape
    seqs = frozen_margin_score.shape[1]
    lanes = count * rank_size
    down = adapter_down_weight.reshape(lanes, width)
    up = adapter_up_weight.reshape(lanes, out_width)

    def flipped(block, flip):
        return lax.ppermute(block, "ad", [(at, at ^ flip) for at in range(n_dev)])

    def other_grp(block):
        return lax.ppermute(block, "grp", [(0, 1), (1, 0)])

    def half(which):
        return jnp.concatenate(
            [
                lax.dynamic_index_in_dim(adapter_up_weight, which, keepdims=False),
                lax.dynamic_index_in_dim(adapter_down_weight, which, keepdims=False),
            ],
            axis=1,
        )

    half_mine = half(grp)
    far = flipped(half_mine, half_size)
    half_other = half(1 - grp)

    (owner,) = gate(lax.optimization_barrier((owner, half_mine))[0])
    slot_index = rows_by_slot(owner.reshape(1, rows), n_dev, capacity)[0]
    to_slot = (jnp.arange(slots, dtype=jnp.int32)[:, None] == slot_index[None, :]).astype(BF16)
    row_adapter = token_local_adapter[:, None] == jnp.arange(count, dtype=jnp.int32)
    row_seq = segment[0][:, None] == jnp.arange(seqs, dtype=jnp.int32)
    marks = jnp.concatenate([row_adapter, row_seq], axis=1).astype(BF16)
    marked = jnp.concatenate(
        [cotangent, jnp.pad(marks, ((0, 0), (0, MARKS - count - seqs)))], axis=1
    )
    sent = jnp.dot(
        to_slot, jnp.concatenate([tokens, marked], axis=1), preferred_element_type=BF16
    )

    halves = [list(range(half_size)), list(range(half_size, n_dev))]
    base = me - spot
    half_spot = jnp.arange(half_size, dtype=jnp.int32)[:, None, None]
    side = jnp.arange(2, dtype=jnp.int32)[None, :, None]
    half_slot = (((base + half_spot) ^ (side * half_size)) * capacity) + jnp.arange(
        capacity, dtype=jnp.int32
    )
    to_half = (half_slot[..., None] == slot_index).astype(BF16)
    half_g = lax.all_to_all(
        jnp.dot(to_half.reshape(slots, rows), marked, preferred_element_type=BF16).reshape(
            half_size, 2 * capacity, out_width + MARKS
        ),
        "ad",
        split_axis=0,
        concat_axis=0,
        tiled=True,
        axis_index_groups=halves,
    )

    lane = jnp.arange(MARKS, dtype=jnp.int32)[None, :]
    which = (lane == jnp.stack([grp, 1 - grp])[:, None]).astype(F32)

    def land(blocks):
        return [block if at == 0 else flipped(block, 2 * at) for at, block in enumerate(blocks)]

    def hand_over(blocks):
        return blocks + [flipped(jnp.concatenate([block[capacity:] for block in blocks]), 1)]

    made_near = project(
        0, False, capacity, out_width, width, spot, half_g, which, [half_mine], [half_other]
    )
    landed_near = land(made_near)
    (sent,) = gate(lax.optimization_barrier((sent, made_near))[0])
    got = lax.all_to_all(
        sent.reshape(n_dev, capacity, width + out_width + MARKS),
        "ad",
        split_axis=0,
        concat_axis=0,
        tiled=True,
    ).reshape(slots, width + out_width + MARKS)
    got_x = got[:, :width]

    got_g = got[:, width : width + out_width]
    slot_marks = got[:, width + out_width : width + out_width + count + seqs].astype(F32)
    member = jnp.repeat(slot_marks[:, :count], rank_size, axis=1)
    slot_seq_hot = slot_marks[:, count:].reshape(n_dev, capacity, seqs)

    contract = (((1,), (1,)), ((), ()))
    pulled = member * lax.dot_general(got_g, up, contract, preferred_element_type=F32)
    pulled_rows = pulled.astype(BF16)

    (far,) = gate(lax.optimization_barrier((far, sent, landed_near))[0])
    far_other = other_grp(far)
    kept, handed = project(
        1, True, capacity, out_width, width, spot, half_g, which, [far], [far_other]
    )
    taken = flipped(handed, 1)
    landed_far = land(
        [
            jnp.concatenate([kept[at : at + capacity], taken[at : at + capacity]])
            for at in range(0, half_size // 2 * capacity, capacity)
        ]
    )
    rows_contract = (((0,), (0,)), ((), ()))

    hidden_rows = (
        member * lax.dot_general(got_x, down, contract, preferred_element_type=F32)
    ).astype(BF16)
    inner_product = SCALE * jnp.sum(hidden_rows.astype(F32) * pulled, axis=1)
    part = jnp.sum(slot_seq_hot * inner_product.reshape(n_dev, capacity)[:, :, None], axis=1)
    chips = half_size // 2
    order = [2 * at for at in range(chips)] + [2 * at + 1 for at in range(chips)]
    near_flips = spot ^ jnp.array(order, dtype=jnp.int32)
    far_flips = spot ^ jnp.arange(half_size, dtype=jnp.int32)
    pick = jnp.concatenate([to_half[near_flips, 0], to_half[far_flips, 1]])
    pick = pick.reshape(slots, rows).T
    told = share(
        jnp.concatenate(
            [
                part.reshape(1, n_dev * seqs),
                pair_sequence_order.astype(F32),
                frozen_margin_score,
            ],
            axis=1,
        )
    )[:, 0]
    scores = jnp.sum(told[:, : n_dev * seqs], axis=0).reshape(n_dev, seqs)
    scores = scores + told[:, n_dev * seqs + seqs :]
    losses, seq_weight = pair_weights(
        scores, told[:, n_dev * seqs : n_dev * seqs + seqs].astype(jnp.int32)
    )

    slot_weight = LOSS_SCALE * jnp.sum(slot_seq_hot * seq_weight[:, None, :], axis=2).reshape(slots)
    upper = (slot_weight[:, None] * hidden_rows.astype(F32)).astype(BF16)
    lower = (slot_weight[:, None] * pulled_rows.astype(F32)).astype(BF16)
    grad_up = (
        SCALE * lax.dot_general(upper, got_g, rows_contract, preferred_element_type=F32)
    ).astype(BF16)
    grad_down = (
        SCALE * lax.dot_general(lower, got_x, rows_contract, preferred_element_type=F32)
    ).astype(BF16)

    my_weight = lax.dynamic_index_in_dim(seq_weight, me, keepdims=False)
    my_losses = lax.dynamic_index_in_dim(losses, me, keepdims=False)
    row_weight = LOSS_SCALE * jnp.sum(row_seq.astype(F32) * my_weight[None, :], axis=1)
    landed_far = lax.optimization_barrier((landed_far, told))[0]
    landed = hand_over(landed_near) + landed_far
    input_grad = select(
        pick,
        SCALE * row_weight[:, None],
        landed,
        [capacity] * chips + [chips * capacity] + [2 * capacity] * chips,
    )
    return (
        input_grad,
        grad_down.reshape(count, rank_size, width),
        grad_up.reshape(count, rank_size, out_width),
        my_losses,
    )


def solution(mesh):
    placed = (
        P(("grp", "ad"), None),
        P(("grp", "ad"), None),
        P(("grp", "ad"), None),
        P(("grp", "ad")),
        P(("grp", "ad"), None),
        P(("grp", "ad"), None),
        P(("grp", "ad"), None),
        P("ad", None, None),
        P("ad", None, None),
    )
    return jax.shard_map(
        body,
        mesh=mesh,
        in_specs=placed,
        out_specs=(
            P(("grp", "ad"), None),
            P(("grp", "ad"), None, None),
            P(("grp", "ad"), None, None),
            P(("grp", "ad")),
        ),
        check_vma=False,
    )
```

time: 267 us -> 205 us (0.77)
  the two profiles are of different devices: /device:TPU:18 before, /device:TPU:0 now
where the time goes in v3:
time: 205 us; the launch traced here: 204 us
  waiting for transfers between devices  91 us (44%)
  starting transfers between devices  45.8 us (22%)
  local copies, waits for them, and re-layouts  21.2 us (10%)
  matrix products  18.8 us (9%)
  Pallas kernels  14.2 us (7%)
  other arithmetic  12.2 us (6%)
    ppermute x9, waiting for transfers between devices, flipped(): return lax.ppermute(block, 'ad', [(at, at ^ flip) for at in range(n_dev)])  49.4 us
    ppermute x1, waiting for transfers between devices, other_grp(): return lax.ppermute(block, 'grp', [(0, 1), (1, 0)])  21.2 us
    all_to_all x1, starting transfers between devices, share(): lax.all_to_all(jnp.broadcast_to(block[None], (n_dev,) + block.shape), 'ad...  19.6 us
    ppermute x9, starting transfers between devices, flipped(): return lax.ppermute(block, 'ad', [(at, at ^ flip) for at in range(n_dev)])  16.3 us
    all_to_all x1, waiting for transfers between devices, body(): lax.all_to_all(jnp.dot(to_half.reshape(slots, rows), marked, preferred_el...  12.9 us
    pallas_call x2, Pallas kernels, project(): pl.pallas_call(functools.partial(project_kernel, side, split, capacity, o...  9.25 us
    dot_general x1, matrix products, body(): jnp.dot(to_slot, jnp.concatenate([tokens, marked], axis=1), preferred_ele...  5.28 us
    pallas_call x1, Pallas kernels, select(): pl.pallas_call(select_kernel, out_shape=jax.ShapeDtypeStruct((rows, width...  4.93 us
  transfers between devices with their start and end apart: 13, of which 8 were waited for; matrix products, arithmetic and copies ran while one was open for 21% of the time, Pallas kernels for 5%

profile of v3, /device:TPU:0, one launch (start us, length us, event | category | flops | bytes accessed | tf_op | source)
XLA Modules:
  0.0 204.1 jit_solution(17471043224007273114)
XLA Ops:
  0.6 1.6 dynamic-slice_bitcast_fusion.2
  2.3 2.7 %dynamic-slice_bitcast_fusion = (bf16[64,8192]{1,0:T(8,128)(2,1)}, bf16[64,8192]{1,0:T(8,128)(2,1)S(1)}) fusion(bf16[2,64,8192]{2,1,0:T(8,128)(2,1)} %param.17, s32[]{:T(128)S(6)} %select_n.44, s32[]{:T(128)S(6)} %select_n.41), kind=kLoop, calls=%fused_computation.25 | loop fusion | bytes 4194312 | tf_op jit(solution)/shard_map/jit(dynamic_index_in_dim)/squeeze | solution.py:200
  5.0 1.1 pad_maximum_fusion.refs_0_
  6.1 4.0 %collective-permute-start.4 = (bf16[64,9216]{1,0:T(8,128)(2,1)}, bf16[64,9216]{1,0:T(8,128)(2,1)}, u32[]{:S(2)}, u32[]{:S(2)}) collective-permute-start(bf16[64,9216]{1,0:T(8,128)(2,1)} %pad_maximum_fusion.refs_0_), channel_id=1, source_target_pairs={{0,8},{1,9},{2,10},{3,11},{4,12},{5,13},{6,14},{7,15},{8,0},{9,1},... | collective-permute-start | bytes 3538952 | tf_op jit(solution)/shard_map/ppermute | solution.py:191
  15.1 1.2 fusion.24
  16.3 3.8 %all-to-all-start = ((bf16[8,32,1152]{2,1,0:T(8,128)(2,1)}), bf16[8,32,1152]{2,1,0:T(8,128)(2,1)S(1)}, u32[]{:S(2)}, u32[]{:S(2)}) async-start(bf16[8,32,1152]{2,1,0:T(8,128)(2,1)} %fusion.24), calls=%async_computation | async-start | bytes 1179648 | tf_op jit(solution)/shard_map/all_to_all | solution.py:230
  21.5 5.3 %fusion.4.refs_0_ = bf16[256,9344]{1,0:T(8,128)(2,1)} fusion(bf16[128,128]{1,0:T(8,128)(2,1)S(1)} %copy-done.10, bf16[128,1024]{1,0:T(8,128)(2,1)S(1)} %copy-done.8, bf16[128,8192]{1,0:T(8,128)(2,1)} %param.10, s32[128]{0:T(128)S(1)} %convert_add_fusion), kind=kOutput, calls=%fused_computation.7 | convolution fusion | flops 619577344 | bytes 7176704 | tf_op jit(solution)/shard_map/dot_general | solution.py:218
  26.8 1.2 gather_fusion.1
  28.0 1.1 pad_maximum_fusion.1.refs_1_
  29.1 12.9 %all-to-all-done.g_ref = bf16[8,32,1152]{2,1,0:T(8,128)(2,1)S(1)} async-done(((bf16[8,32,1152]{2,1,0:T(8,128)(2,1)}), bf16[8,32,1152]{2,1,0:T(8,128)(2,1)S(1)}, u32[]{:S(2)}, u32[]{:S(2)}) %all-to-all-start) | async-done | bytes 589856 | tf_op jit(solution)/shard_map/all_to_all | solution.py:230
  42.9 4.6 %project.2 = (bf16[32,8192]{1,0:T(8,128)(2,1)}, bf16[32,8192]{1,0:T(8,128)(2,1)}, bf16[32,8192]{1,0:T(8,128)(2,1)}, bf16[32,8192]{1,0:T(8,128)(2,1)}) custom-call(s32[1]{0:T(128)} %bitcast.8.spot_ref, bf16[8,32,1152]{2,1,0:T(8,128)(2,1)} %copy-done, f32[2,128]{1,0:T(2,128)} %compare_convert_fusion.1.which, bf16[64,9216]{1,0:T(8,128)(2,1)} %pad_maximum_fusion.refs_0_, ...), custom_call_target="tpu_custom_call" | custom-call | flops 1000 | bytes 1000 | tf_op jit(solution)/shard_map/project/pallas_call | solution.py:75
  47.4 1.5 collective-permute-start
  49.0 2.4 %collective-permute-start.1 = (bf16[32,8192]{1,0:T(8,128)(2,1)}, bf16[32,8192]{1,0:T(8,128)(2,1)}, u32[]{:S(2)}, u32[]{:S(2)}) collective-permute-start(bf16[32,8192]{1,0:T(8,128)(2,1)} %get-tuple-element.20), channel_id=1, source_target_pairs={{0,4},{1,5},{2,6},{3,7},{4,0},{5,1},{6,2},{7,3},{8,12},{9,13},{10,... | collective-permute-start | bytes 1572872 | tf_op jit(solution)/shard_map/ppermute | solution.py:191
  51.4 4.6 %all-to-all-start.1 = ((bf16[16,16,9344]{2,1,0:T(8,128)(2,1)}), bf16[16,16,9344]{2,1,0:T(8,128)(2,1)}, u32[]{:S(2)}, u32[]{:S(2)}) async-start(bf16[16,16,9344]{2,1,0:T(8,128)(2,1)} %bitcast.51), calls=%async_computation.1 | async-start | bytes 9568256 | tf_op jit(solution)/shard_map/all_to_all | solution.py:255
  55.9 6.7 %collective-permute-done.4.refs_0_ = bf16[64,9216]{1,0:T(8,128)(2,1)} collective-permute-done((bf16[64,9216]{1,0:T(8,128)(2,1)}, bf16[64,9216]{1,0:T(8,128)(2,1)}, u32[]{:S(2)}, u32[]{:S(2)}) %collective-permute-start.4) | collective-permute-done | bytes 1179680 | tf_op jit(solution)/shard_map/ppermute | solution.py:191
  62.6 36.0 %collective-permute-done.1.refs_2_ = bf16[32,8192]{1,0:T(8,128)(2,1)} collective-permute-done((bf16[32,8192]{1,0:T(8,128)(2,1)}, bf16[32,8192]{1,0:T(8,128)(2,1)}, u32[]{:S(2)}, u32[]{:S(2)}) %collective-permute-start.1) | collective-permute-done | bytes 524320 | tf_op jit(solution)/shard_map/ppermute | solution.py:191
  98.6 5.8 %collective-permute-done.2.refs_3_ = bf16[32,8192]{1,0:T(8,128)(2,1)} collective-permute-done((bf16[32,8192]{1,0:T(8,128)(2,1)}, bf16[32,8192]{1,0:T(8,128)(2,1)}, u32[]{:S(2)}, u32[]{:S(2)}) %collective-permute-start.2) | collective-permute-done | bytes 524320 | tf_op jit(solution)/shard_map/ppermute | solution.py:191
  104.5 1.6 collective-permute-start.5
  111.4 21.2 %collective-permute-done.5.refs_1_ = bf16[64,9216]{1,0:T(8,128)(2,1)S(1)} collective-permute-done((bf16[64,9216]{1,0:T(8,128)(2,1)}, bf16[64,9216]{1,0:T(8,128)(2,1)S(1)}, u32[]{:S(2)}, u32[]{:S(2)}) %collective-permute-start.5) | collective-permute-done | bytes 1179680 | tf_op jit(solution)/shard_map/ppermute | solution.py:194
  133.6 4.7 %project.3 = (bf16[64,8192]{1,0:T(8,128)(2,1)}, bf16[64,8192]{1,0:T(8,128)(2,1)}) custom-call(s32[1]{0:T(128)} %bitcast.8.spot_ref, bf16[8,32,1152]{2,1,0:T(8,128)(2,1)} %copy-done, f32[2,128]{1,0:T(2,128)} %compare_convert_fusion.1.which, bf16[64,9216]{1,0:T(8,128)(2,1)} %gate.5.refs_0_, bf16[64,9216]{1,0:T(8,128)(2,1)} %copy-done.4), custom_call_target="tpu_custom_call" | custom-call | flops 1000 | bytes 1000 | tf_op jit(solution)/shard_map/project/pallas_call | solution.py:75
  138.2 2.0 fusion.51
  142.7 6.9 %collective-permute-start.7 = (bf16[32,8192]{1,0:T(8,128)(2,1)}, bf16[32,8192]{1,0:T(8,128)(2,1)}, u32[]{:S(2)}, u32[]{:S(2)}) collective-permute-start(bf16[32,8192]{1,0:T(8,128)(2,1)} %pad_maximum_fusion.4), channel_id=1, source_target_pairs={{0,2},{1,3},{2,0},{3,1},{4,6},{5,7},{6,4},{7,5},{8,10},{9,11},{10,... | collective-permute-start | bytes 1572872 | tf_op jit(solution)/shard_map/ppermute | solution.py:191
  151.3 1.5 collective-permute-start.9
  152.7 2.9 %all-to-all-done.1 = bf16[16,16,9344]{2,1,0:T(8,128)(2,1)} async-done(((bf16[16,16,9344]{2,1,0:T(8,128)(2,1)}), bf16[16,16,9344]{2,1,0:T(8,128)(2,1)}, u32[]{:S(2)}, u32[]{:S(2)}) %all-to-all-start.1) | async-done | bytes 4784160 | tf_op jit(solution)/shard_map/all_to_all | solution.py:255
  156.5 1.4 convolution_multiply_fusion.2
  158.0 4.4 %multiply_reduce_fusion.1 = (f32[256]{0:T(256)S(1)}, f32[256,128]{0,1:T(8,128)}) fusion(f32[256,128]{0,1:T(8,128)S(1)} %convolution_multiply_fusion.2, f32[256,128]{0,1:T(8,128)S(1)} %bitcast.56, bf16[128,8192]{1,0:T(8,128)(2,1)S(1)} %bitcast.52, bf16[256,9344]{1,0:T(8,128)(2,1)} %bitcast.15), kind=kOutput, calls=%fused_computation.42 | convolution fusion | flops 537034496 | bytes 6685696 | tf_op jit(solution)/shard_map/dot_general | solution.py:288
  163.4 19.6 %all-to-all-start.2 = ((f32[16,1,72]{2,1,0:T(1,128)}), f32[16,1,72]{2,1,0:T(1,128)S(1)}, u32[]{:S(2)}, u32[]{:S(2)}) async-start(f32[16,1,72]{2,1,0:T(1,128)} %broadcast_in_dim.11), calls=%async_computation.2 | async-start | bytes 16384 | tf_op jit(solution)/shard_map/all_to_all | solution.py:156
  183.0 1.8 pad_maximum_fusion.3.refs_5_
  184.8 4.6 %all-to-all-done.2 = f32[16,1,72]{2,1,0:T(1,128)S(1)} async-done(((f32[16,1,72]{2,1,0:T(1,128)}), f32[16,1,72]{2,1,0:T(1,128)S(1)}, u32[]{:S(2)}, u32[]{:S(2)}) %all-to-all-start.2) | async-done | bytes 4640 | tf_op jit(solution)/shard_map/all_to_all | solution.py:156
  191.9 2.1 %fusion.10 = bf16[128,1024]{1,0:T(8,128)(2,1)} fusion(bf16[256,9344]{1,0:T(8,128)(2,1)} %bitcast.15, f32[256,128]{0,1:T(8,128)} %get-tuple-element.49, f32[256]{0:T(256)S(1)} %broadcast_multiply_fusion), kind=kOutput, calls=%fused_computation.14 | convolution fusion | flops 67436544 | bytes 918528 | tf_op jit(solution)/shard_map/dot_general | solution.py:318
  194.0 4.3 %fusion = bf16[128,8192]{1,0:T(8,128)(2,1)} fusion(bf16[256,9344]{1,0:T(8,128)(2,1)} %bitcast.15, f32[256,128]{0,1:T(8,128)S(1)} %copy-done.15, f32[256]{0:T(256)S(1)} %broadcast_multiply_fusion), kind=kOutput, calls=%fused_computation.3 | convolution fusion | flops 539099136 | bytes 6423552 | tf_op jit(solution)/shard_map/dot_general | solution.py:321
  199.2 4.9 %select.9 = bf16[128,8192]{1,0:T(8,128)(2,1)} custom-call(bf16[128,256]{1,0:T(8,128)(2,1)} %bitcast.57, f32[128,1]{1,0:T(8,128)} %copy.54.weight_ref, bf16[32,8192]{1,0:T(8,128)(2,1)} %get-tuple-element.18.refs_0_, bf16[32,8192]{1,0:T(8,128)(2,1)} %collective-permute-done.refs_1_, bf16[32,8192]{1,0:T(8,128)(2,1)} %collective-permute-done.1.refs_2_, ...), custom_call_target="tpu_custom_call" | custom-call | flops 536870912 | bytes 6291456 | tf_op jit(solution)/shard_map/select/pallas_call | solution.py:113
  (134 shorter events, 23.1 us)
Async XLA Ops:
  2.3 7.8 %copy-start.23 = (s32[128]{0:T(128)S(1)}, s32[128]{0:T(128)}, u32[]{:S(2)}) copy-start(s32[128]{0:T(128)} %param.13) | copy-start | bytes 1540
  2.3 7.8 %copy-start.25 = (s32[1,128]{1,0:T(1,128)S(1)}, s32[1,128]{1,0:T(1,128)}, u32[]{:S(2)}) copy-start(s32[1,128]{1,0:T(1,128)} %param.14) | copy-start | bytes 1540
  2.3 10.7 %copy-start.19 = (s32[128,1]{0,1:T(1,128)S(1)}, s32[128,1]{0,1:T(1,128)}, u32[]{:S(2)}) copy-start(s32[128,1]{0,1:T(1,128)} %param.12) | copy-start | bytes 1540
  6.1 56.5 %collective-permute-start.4 = (bf16[64,9216]{1,0:T(8,128)(2,1)}, bf16[64,9216]{1,0:T(8,128)(2,1)}, u32[]{:S(2)}, u32[]{:S(2)}) collective-permute-start(bf16[64,9216]{1,0:T(8,128)(2,1)} %pad_maximum_fusion.refs_0_), channel_id=1, source_target_pairs={{0,8},{1,9},{2,10},{3,11},{4,12},{5,13},{6,14},{7,15},{8,0},{9,1},... | collective-permute-start | bytes 3538952 | tf_op jit(solution)/shard_map/ppermute | solution.py:191
  13.7 6.3 %copy-start.17 = (s32[8,2]{1,0:T(8,128)S(1)}, s32[8,2]{1,0:T(8,128)}, u32[]{:S(2)}) copy-start(s32[8,2]{1,0:T(8,128)} %copy-done.16) | copy-start | bytes 196
  13.8 7.1 %copy-start.24 = (s32[1,4]{1,0:T(1,128)S(1)}, s32[1,4]{1,0:T(1,128)}, u32[]{:S(2)}) copy-start(s32[1,4]{1,0:T(1,128)} %param.15) | copy-start | bytes 52
  16.3 25.7 %all-to-all-start = ((bf16[8,32,1152]{2,1,0:T(8,128)(2,1)}), bf16[8,32,1152]{2,1,0:T(8,128)(2,1)S(1)}, u32[]{:S(2)}, u32[]{:S(2)}) async-start(bf16[8,32,1152]{2,1,0:T(8,128)(2,1)} %fusion.24), calls=%async_computation | async-start | bytes 1179648 | tf_op jit(solution)/shard_map/all_to_all | solution.py:230
  21.5 5.3 %copy-start.11 = (bf16[8,2,16,128]{3,2,1,0:T(8,128)(2,1)}, bf16[8,2,16,128]{3,2,1,0:T(8,128)(2,1)S(1)}, u32[]{:S(2)}) copy-start(bf16[8,2,16,128]{3,2,1,0:T(8,128)(2,1)S(1)} %compare_convert_fusion) | copy-start | bytes 196612
  21.5 6.5 %copy-start.1 = (bf16[64,8192]{1,0:T(8,128)(2,1)S(1)}, bf16[64,8192]{1,0:T(8,128)(2,1)}, u32[]{:S(2)}) copy-start(bf16[64,8192]{1,0:T(8,128)(2,1)} %get-tuple-element.34) | copy-start | bytes 3145732
  21.5 6.5 %copy-start.9 = (bf16[64,1024]{1,0:T(8,128)(2,1)S(1)}, bf16[64,1024]{1,0:T(8,128)(2,1)}, u32[]{:S(2)}) copy-start(bf16[64,1024]{1,0:T(8,128)(2,1)} %get-tuple-element.44) | copy-start | bytes 393220
  47.4 15.1 %collective-permute-start = (bf16[32,8192]{1,0:T(8,128)(2,1)}, bf16[32,8192]{1,0:T(8,128)(2,1)}, u32[]{:S(2)}, u32[]{:S(2)}) collective-permute-start(bf16[32,8192]{1,0:T(8,128)(2,1)} %get-tuple-element.19), channel_id=1, source_target_pairs={{0,2},{1,3},{2,0},{3,1},{4,6},{5,7},{6,4},{7,5},{8,10},{9,11},{10,... | collective-permute-start | bytes 1572872 | tf_op jit(solution)/shard_map/ppermute | solution.py:191
  49.0 49.7 %collective-permute-start.1 = (bf16[32,8192]{1,0:T(8,128)(2,1)}, bf16[32,8192]{1,0:T(8,128)(2,1)}, u32[]{:S(2)}, u32[]{:S(2)}) collective-permute-start(bf16[32,8192]{1,0:T(8,128)(2,1)} %get-tuple-element.20), channel_id=1, source_target_pairs={{0,4},{1,5},{2,6},{3,7},{4,0},{5,1},{6,2},{7,3},{8,12},{9,13},{10,... | collective-permute-start | bytes 1572872 | tf_op jit(solution)/shard_map/ppermute | solution.py:191
  51.3 53.1 %collective-permute-start.2 = (bf16[32,8192]{1,0:T(8,128)(2,1)}, bf16[32,8192]{1,0:T(8,128)(2,1)}, u32[]{:S(2)}, u32[]{:S(2)}) collective-permute-start(bf16[32,8192]{1,0:T(8,128)(2,1)} %get-tuple-element.21), channel_id=1, source_target_pairs={{0,6},{1,7},{2,4},{3,5},{4,2},{5,3},{6,0},{7,1},{8,14},{9,15},{10,... | collective-permute-start | bytes 1572872 | tf_op jit(solution)/shard_map/ppermute | solution.py:191
  51.4 104.2 %all-to-all-start.1 = ((bf16[16,16,9344]{2,1,0:T(8,128)(2,1)}), bf16[16,16,9344]{2,1,0:T(8,128)(2,1)}, u32[]{:S(2)}, u32[]{:S(2)}) async-start(bf16[16,16,9344]{2,1,0:T(8,128)(2,1)} %bitcast.51), calls=%async_computation.1 | async-start | bytes 9568256 | tf_op jit(solution)/shard_map/all_to_all | solution.py:255
  104.5 1.6 copy-start.12
  104.5 2.2 %copy-start.13 = (bf16[8,16,128]{2,1,0:T(8,128)(2,1)S(1)}, bf16[8,16,128]{2,1,0:T(8,128)(2,1)}, u32[]{:S(2)}) copy-start(bf16[8,16,128]{2,1,0:T(8,128)(2,1)} %gather_fusion.1) | copy-start | bytes 98308
  104.5 2.9 %copy-start.3 = (bf16[32,8192]{1,0:T(8,128)(2,1)S(1)}, bf16[32,8192]{1,0:T(8,128)(2,1)}, u32[]{:S(2)}) copy-start(bf16[32,8192]{1,0:T(8,128)(2,1)} %get-tuple-element.18.refs_0_) | copy-start | bytes 1572868
  104.5 28.1 %collective-permute-start.5 = (bf16[64,9216]{1,0:T(8,128)(2,1)}, bf16[64,9216]{1,0:T(8,128)(2,1)S(1)}, u32[]{:S(2)}, u32[]{:S(2)}) collective-permute-start(bf16[64,9216]{1,0:T(8,128)(2,1)} %gate.5.refs_0_), channel_id=1, source_target_pairs={{0,16},{16,0},{1,17},{17,1},{2,18},{18,2},{3,19},{19,3},{4,20},{20... | collective-permute-start | bytes 3538952 | tf_op jit(solution)/shard_map/ppermute | solution.py:194
  111.4 86.9 %collective-permute-start.3 = (bf16[64,8192]{1,0:T(8,128)(2,1)}, bf16[64,8192]{1,0:T(8,128)(2,1)S(1)}, u32[]{:S(2)}, u32[]{:S(2)}) collective-permute-start(bf16[64,8192]{1,0:T(8,128)(2,1)} %pad_maximum_fusion.2), channel_id=1, source_target_pairs={{0,1},{1,0},{2,3},{3,2},{4,5},{5,4},{6,7},{7,6},{8,9},{9,8},{10,11... | collective-permute-start | bytes 3145736 | tf_op jit(solution)/shard_map/ppermute | solution.py:191
  138.2 2.9 %collective-permute-start.6 = (bf16[64,8192]{1,0:T(8,128)(2,1)}, bf16[64,8192]{1,0:T(8,128)(2,1)S(1)}, u32[]{:S(2)}, u32[]{:S(2)}) collective-permute-start(bf16[64,8192]{1,0:T(8,128)(2,1)} %get-tuple-element.25), channel_id=1, source_target_pairs={{0,1},{1,0},{2,3},{3,2},{4,5},{5,4},{6,7},{7,6},{8,9},{9,8},{10,11... | collective-permute-start | bytes 3145736 | tf_op jit(solution)/shard_map/ppermute | solution.py:191
  140.2 16.3 %copy-start.6 = (bf16[2,64,1024]{2,1,0:T(8,128)(2,1)S(1)}, bf16[2,64,1024]{2,1,0:T(8,128)(2,1)}, u32[]{:S(2)}) copy-start(bf16[2,64,1024]{2,1,0:T(8,128)(2,1)} %param.18) | copy-start | bytes 786436
  141.9 16.0 %copy-start.2 = (bf16[2,64,8192]{2,1,0:T(8,128)(2,1)S(1)}, bf16[2,64,8192]{2,1,0:T(8,128)(2,1)}, u32[]{:S(2)}) copy-start(bf16[2,64,8192]{2,1,0:T(8,128)(2,1)} %param.17) | copy-start | bytes 6291460
  142.7 49.2 %collective-permute-start.7 = (bf16[32,8192]{1,0:T(8,128)(2,1)}, bf16[32,8192]{1,0:T(8,128)(2,1)}, u32[]{:S(2)}, u32[]{:S(2)}) collective-permute-start(bf16[32,8192]{1,0:T(8,128)(2,1)} %pad_maximum_fusion.4), channel_id=1, source_target_pairs={{0,2},{1,3},{2,0},{3,1},{4,6},{5,7},{6,4},{7,5},{8,10},{9,11},{10,... | collective-permute-start | bytes 1572872 | tf_op jit(solution)/shard_map/ppermute | solution.py:191
  150.4 41.5 %collective-permute-start.8 = (bf16[32,8192]{1,0:T(8,128)(2,1)}, bf16[32,8192]{1,0:T(8,128)(2,1)}, u32[]{:S(2)}, u32[]{:S(2)}) collective-permute-start(bf16[32,8192]{1,0:T(8,128)(2,1)} %pad_maximum_fusion.5), channel_id=1, source_target_pairs={{0,4},{1,5},{2,6},{3,7},{4,0},{5,1},{6,2},{7,3},{8,12},{9,13},{10,... | collective-permute-start | bytes 1572872 | tf_op jit(solution)/shard_map/ppermute | solution.py:191
  151.3 40.6 %collective-permute-start.9 = (bf16[32,8192]{1,0:T(8,128)(2,1)}, bf16[32,8192]{1,0:T(8,128)(2,1)}, u32[]{:S(2)}, u32[]{:S(2)}) collective-permute-start(bf16[32,8192]{1,0:T(8,128)(2,1)} %pad_maximum_fusion.6), channel_id=1, source_target_pairs={{0,6},{1,7},{2,4},{3,5},{4,2},{5,3},{6,0},{7,1},{8,14},{9,15},{10,... | collective-permute-start | bytes 1572872 | tf_op jit(solution)/shard_map/ppermute | solution.py:191
  157.9 4.5 %copy-start.14 = (f32[256,128]{0,1:T(8,128)}, f32[256,128]{0,1:T(8,128)S(1)}, u32[]{:S(2)}) copy-start(f32[256,128]{0,1:T(8,128)S(1)} %convolution_multiply_fusion.2) | copy-start | bytes 393220
  157.9 4.8 %copy-start.21 = (f32[1,4]{1,0:T(1,128)S(1)}, f32[1,4]{1,0:T(1,128)}, u32[]{:S(2)}) copy-start(f32[1,4]{1,0:T(1,128)} %param.16) | copy-start | bytes 52
  157.9 4.8 %copy-start.22 = (f32[1,4]{1,0:T(1,128)S(1)}, f32[1,4]{1,0:T(1,128)}, u32[]{:S(2)}) copy-start(f32[1,4]{1,0:T(1,128)} %convert_element_type.89) | copy-start | bytes 52
  157.9 25.1 %copy-start.7 = (bf16[16,8192]{1,0:T(8,128)(2,1)S(1)}, bf16[16,8192]{1,0:T(8,128)(2,1)}, u32[]{:S(2)}) copy-start(bf16[16,8192]{1,0:T(8,128)(2,1)} %get-tuple-element.39) | copy-start | bytes 786436
  158.0 33.1 %copy-start.26 = (s32[1,128]{1,0:T(1,128)S(1)}, s32[1,128]{1,0:T(1,128)}, u32[]{:S(2)}) copy-start(s32[1,128]{1,0:T(1,128)} %param.14) | copy-start | bytes 1540
  162.4 31.6 %copy-start.15 = (f32[256,128]{0,1:T(8,128)S(1)}, f32[256,128]{0,1:T(8,128)}, u32[]{:S(2)}) copy-start(f32[256,128]{0,1:T(8,128)} %copy-done.14) | copy-start | bytes 393220
  163.4 26.0 %all-to-all-start.2 = ((f32[16,1,72]{2,1,0:T(1,128)}), f32[16,1,72]{2,1,0:T(1,128)S(1)}, u32[]{:S(2)}, u32[]{:S(2)}) async-start(f32[16,1,72]{2,1,0:T(1,128)} %broadcast_in_dim.11), calls=%async_computation.2 | async-start | bytes 16384 | tf_op jit(solution)/shard_map/all_to_all | solution.py:156
  (9 other events, 10.3 us)

commit v4 on v3

v4 whole, which is shorter than its diff:
```python
import functools

import jax
import jax.numpy as jnp
from jax import lax
from jax.experimental import pallas as pl
from jax.experimental.pallas import tpu as pltpu
from jax.sharding import PartitionSpec as P

SCALE = 2.0
BETA = 0.1
LOSS_SCALE = 256.0
MARKS = 128
GATE_FLOPS = 2 * 10**11

F32 = jnp.float32
BF16 = jnp.bfloat16


def gate(*arrays):
    return pl.pallas_call(
        lambda *refs: None,
        out_shape=[jax.ShapeDtypeStruct(array.shape, array.dtype) for array in arrays],
        in_specs=[pl.BlockSpec(memory_space=pl.ANY)] * len(arrays),
        out_specs=[pl.BlockSpec(memory_space=pl.ANY)] * len(arrays),
        input_output_aliases={at: at for at in range(len(arrays))},
        cost_estimate=pl.CostEstimate(flops=GATE_FLOPS, bytes_accessed=0, transcendentals=0),
        name="gate",
    )(*arrays)


def project_kernel(side, split, capacity, out_width, n_outs, spot_ref, g_ref, which, *refs):
    n_spots = g_ref.shape[0]
    n_parts = (len(refs) - n_outs) // 2
    mine, other, outs = refs[:n_parts], refs[n_parts : 2 * n_parts], refs[2 * n_parts :]
    first = side * capacity
    spot = spot_ref[0]
    rows = jnp.concatenate(
        [g_ref[spot ^ flip, first : first + capacity, :] for flip in range(n_spots)], axis=0
    )
    marks = rows[:, out_width:].astype(F32)
    contract = (((1,), (1,)), ((), ()))
    pulls = []
    for at, parts in enumerate((mine, other)):
        member = jnp.sum(marks * which[at : at + 1, :], axis=1, keepdims=True)
        pull = lax.dot_general(
            rows[:, :out_width], parts[0][:, :out_width], contract, preferred_element_type=F32
        )
        pulls.append((member * pull).astype(BF16))
    done = 0
    for at in range(n_parts):
        start, end = (out_width if at == 0 else 0), mine[at].shape[1]
        while start < end:
            size = min(1024, end - start)
            columns = slice(start, start + size)
            made = jnp.dot(pulls[0], mine[at][:, columns], preferred_element_type=F32)
            made = made + jnp.dot(pulls[1], other[at][:, columns], preferred_element_type=F32)
            made = made.astype(BF16)
            for flip in range(n_spots):
                row = made[flip * capacity : (flip + 1) * capacity]
                if split:
                    chip = flip // 2 * capacity
                    outs[flip % 2][chip : chip + capacity, done : done + size] = row
                else:
                    core = flip % 2 * capacity
                    outs[flip // 2][core : core + capacity, done : done + size] = row
            start, done = start + size, done + size


def project(side, split, capacity, out_width, width, spot, got_g, which, mine, other):
    n_spots = got_g.shape[0]
    chips = n_spots // 2
    blocks = [(chips * capacity, width)] * 2 if split else [(2 * capacity, width)] * chips
    if capacity % 16 == 0:
        return pl.pallas_call(
            functools.partial(project_kernel, side, split, capacity, out_width, len(blocks)),
            out_shape=[jax.ShapeDtypeStruct(block, BF16) for block in blocks],
            in_specs=[pl.BlockSpec(memory_space=pltpu.SMEM)]
            + [pl.BlockSpec(memory_space=pltpu.VMEM)] * (2 + len(mine) + len(other)),
            cost_estimate=pl.CostEstimate(flops=1000, bytes_accessed=1000, transcendentals=0),
            name="project",
        )(spot.reshape(1), got_g, which, *mine, *other)
    order = spot ^ jnp.arange(n_spots, dtype=jnp.int32)
    rows = got_g[order, side * capacity : (side + 1) * capacity].reshape(n_spots * capacity, -1)
    marks = rows[:, out_width:].astype(F32)
    made = 0.0
    for at, parts in enumerate((mine, other)):
        whole = jnp.concatenate(parts, axis=1)
        pull = jnp.dot(rows[:, :out_width], whole[:, :out_width].T, preferred_element_type=F32)
        pull = (jnp.sum(marks * which[at], axis=1, keepdims=True) * pull).astype(BF16)
        made = made + jnp.dot(pull, whole[:, out_width:], preferred_element_type=F32)
    made = made.astype(BF16).reshape(chips, 2, capacity, width)
    if split:
        return [made[:, core].reshape(chips * capacity, width) for core in range(2)]
    return list(made.reshape(chips, 2 * capacity, width))


def iota(shape, axis):
    return lax.broadcasted_iota(jnp.int32, shape, axis)


def exact_dot(hot, values):
    return jnp.dot(hot, values, precision=lax.Precision.HIGHEST, preferred_element_type=F32)


def column_parts(width, columns):
    return [slice(start, min(start + columns, width)) for start in range(0, width, columns)]


def sequence_lanes(score_lanes, count, seqs):
    shape = (MARKS, score_lanes)
    return (iota(shape, 0) == count + iota(shape, 1) % seqs).astype(F32)


def score_kernel(
    count, seqs, rank_size, capacity, columns, own_ref, got_hbm, down_hbm, up_hbm, *refs
):
    hidden_ref, pulled_ref, told_ref, got, down, up, got_sems, down_sems, up_sem = refs
    width, out_width = down.shape[1], up.shape[1]
    parts = column_parts(width, columns)
    tail = slice(width, got.shape[1])
    copies = []
    for at, part in enumerate(parts):
        copies.append(
            (
                pltpu.make_async_copy(got_hbm.at[:, part], got.at[:, part], got_sems.at[at]),
                pltpu.make_async_copy(down_hbm.at[:, part], down.at[:, part], down_sems.at[at]),
            )
        )
    tail_copy = pltpu.make_async_copy(got_hbm.at[:, tail], got.at[:, tail], got_sems.at[len(parts)])
    up_copy = pltpu.make_async_copy(up_hbm, up, up_sem)
    tail_copy.start()
    up_copy.start()
    for pair in copies:
        for copy in pair:
            copy.start()
    contract = (((1,), (1,)), ((), ()))
    tail_copy.wait()
    up_copy.wait()
    marks = got[:, width + out_width :].astype(F32)
    slots, lanes = hidden_ref.shape
    lane = iota((slots, lanes), 1) // rank_size
    member = jnp.zeros((slots, lanes), F32)
    for which in range(count):
        member = jnp.where(lane == which, marks[:, which : which + 1], member)
    pulled = member * lax.dot_general(
        got[:, width : width + out_width], up[...], contract, preferred_element_type=F32
    )
    pulled_ref[...] = pulled.astype(BF16)
    total = jnp.zeros((slots, lanes), F32)
    for pair, part in zip(copies, parts):
        for copy in pair:
            copy.wait()
        total = total + lax.dot_general(
            got[:, part], down[:, part], contract, preferred_element_type=F32
        )
    hidden = (member * total).astype(BF16)
    hidden_ref[...] = hidden
    inner = SCALE * jnp.sum(hidden.astype(F32) * pulled, axis=1, keepdims=True)
    n_dev, _, all_lanes = told_ref.shape
    hot = iota((n_dev, slots), 1) // capacity == iota((n_dev, slots), 0)
    part = exact_dot(hot.astype(F32), marks * inner)
    score_lanes = all_lanes - MARKS
    spread = exact_dot(part, sequence_lanes(score_lanes, count, seqs))
    at_device = iota((n_dev, score_lanes), 0) == iota((n_dev, score_lanes), 1) // seqs
    row = jnp.sum(jnp.where(at_device, spread, 0.0), axis=0, keepdims=True)
    row = jnp.concatenate([row, jnp.zeros((1, MARKS), F32)], axis=1) + own_ref[...]
    told_ref[...] = jnp.broadcast_to(row[None], told_ref.shape)


def score(own, got, down, up, count, seqs, rank_size, n_dev):
    slots = got.shape[0]
    lanes, width = down.shape
    columns = up.shape[1]
    n_parts = len(column_parts(width, columns))
    vmem, hbm = pl.BlockSpec(memory_space=pltpu.VMEM), pl.BlockSpec(memory_space=pl.ANY)
    return pl.pallas_call(
        functools.partial(score_kernel, count, seqs, rank_size, slots // n_dev, columns),
        out_shape=[
            jax.ShapeDtypeStruct((slots, lanes), BF16),
            jax.ShapeDtypeStruct((slots, lanes), BF16),
            jax.ShapeDtypeStruct((n_dev,) + own.shape, F32),
        ],
        in_specs=[vmem, hbm, hbm, hbm],
        out_specs=[vmem] * 3,
        scratch_shapes=[
            pltpu.VMEM(got.shape, BF16),
            pltpu.VMEM(down.shape, BF16),
            pltpu.VMEM(up.shape, BF16),
            pltpu.SemaphoreType.DMA((n_parts + 1,)),
            pltpu.SemaphoreType.DMA((n_parts,)),
            pltpu.SemaphoreType.DMA,
        ],
        compiler_params=pltpu.CompilerParams(vmem_limit_bytes=16 * 2**20),
        cost_estimate=pl.CostEstimate(
            flops=2 * slots * lanes * (width + columns),
            bytes_accessed=2 * (slots + lanes) * (width + columns),
            transcendentals=0,
        ),
        name="score",
    )(own, got, down, up)


def weights(total, count, seqs):
    lane = iota(total.shape, 1)

    def column(at):
        return total[:, at : at + 1]

    pick = [[column(count + seqs + i * seqs + s) for s in range(seqs)] for i in range(seqs)]
    ordered = [sum(pick[i][s] * column(count + s) for s in range(seqs)) for i in range(seqs)]
    losses, by_order = jnp.zeros(total.shape, F32), []
    for pair in range(seqs // 2):
        margin = BETA * (ordered[2 * pair] - ordered[2 * pair + 1])
        loss = jnp.maximum(-margin, 0.0) + jnp.log1p(jnp.exp(-jnp.abs(margin)))
        losses = jnp.where(lane == pair, loss, losses)
        lean = 1.0 / (1.0 + jnp.exp(margin))
        by_order += [-BETA * lean, BETA * lean]
    table = jnp.zeros(total.shape, F32)
    for s in range(seqs):
        weight = LOSS_SCALE * sum(pick[i][s] * by_order[i] for i in range(seqs))
        table = jnp.where(lane == count + s, weight, table)
    return losses, table


def finish_kernel(count, seqs, capacity, columns, used, me_ref, told_ref, *refs):
    hidden_ref, pulled_ref, row_marks, got_hbm, *refs = refs
    if used:
        pick, *refs = refs
    block_hbms, refs = refs[: len(used)], refs[len(used) :]
    losses_ref, row_weight, up_hbm, down_hbm, *refs = refs
    if used:
        input_hbm, got, grad_up, grad_down, rows, input_grad, *sems = refs
        got_sems, up_sem, down_sems, block_sems, input_sems = sems
    else:
        got, grad_up, grad_down, got_sems, up_sem, down_sems = refs
    width, out_width = grad_down.shape[1], grad_up.shape[1]
    parts = column_parts(width, columns)
    tail = slice(width, got.shape[1])
    tail_copy = pltpu.make_async_copy(got_hbm.at[:, tail], got.at[:, tail], got_sems.at[len(parts)])
    copies = [
        pltpu.make_async_copy(got_hbm.at[:, part], got.at[:, part], got_sems.at[at])
        for at, part in enumerate(parts)
    ]
    first, block_copies = 0, []
    for at, size in enumerate(used):
        block_copies.append(
            pltpu.make_async_copy(
                block_hbms[at].at[pl.ds(0, size)], rows.at[pl.ds(first, size)], block_sems.at[at]
            )
        )
        first += size
    tail_copy.start()
    for copy in copies + block_copies:
        copy.start()

    told = jnp.concatenate([told_ref[at] for at in range(told_ref.shape[0])], axis=0)
    score_lanes = told.shape[1] - MARKS
    sums = jnp.sum(told[:, :score_lanes], axis=0, keepdims=True)
    shape = (told.shape[0], score_lanes)
    spread = jnp.where(iota(shape, 0) == iota(shape, 1) // seqs, sums, 0.0)
    total = told[:, score_lanes:] + lax.dot_general(
        spread,
        sequence_lanes(score_lanes, count, seqs),
        (((1,), (1,)), ((), ())),
        precision=lax.Precision.HIGHEST,
        preferred_element_type=F32,
    )
    losses, table = weights(total, count, seqs)
    n_dev, slots = total.shape[0], got.shape[0]
    mine = iota(total.shape, 0) == me_ref[0]
    pair_lane = iota(losses.shape, 1)
    for pair in range(seqs // 2):
        losses_ref[pair] = jnp.sum(jnp.where(mine & (pair_lane == pair), losses, 0.0))
    my_table = jnp.sum(jnp.where(mine, table, 0.0), axis=0, keepdims=True)
    my_weight = SCALE * jnp.sum(row_marks[...] * my_table, axis=1, keepdims=True)
    row_weight[...] = my_weight
    hot = iota((slots, n_dev), 0) // capacity == iota((slots, n_dev), 1)
    slot_table = exact_dot(hot.astype(F32), table)
    tail_copy.wait()
    marks = got[:, width + out_width :].astype(F32)
    weight = jnp.sum(marks * slot_table, axis=1, keepdims=True)
    lower = (weight * pulled_ref[...].astype(F32)).astype(BF16)
    upper = (weight * hidden_ref[...].astype(F32)).astype(BF16)
    contract = (((0,), (0,)), ((), ()))
    made = lax.dot_general(
        upper, got[:, width : width + out_width], contract, preferred_element_type=F32
    )
    grad_up[...] = (SCALE * made).astype(BF16)
    outs = [pltpu.make_async_copy(grad_up, up_hbm, up_sem)]
    outs[0].start()
    for at, part in enumerate(parts):
        copies[at].wait()
        made = lax.dot_general(lower, got[:, part], contract, preferred_element_type=F32)
        grad_down[:, part] = (SCALE * made).astype(BF16)
        outs.append(
            pltpu.make_async_copy(grad_down.at[:, part], down_hbm.at[:, part], down_sems.at[at])
        )
        outs[-1].start()
    if used:
        for copy in block_copies:
            copy.wait()
        for at, part in enumerate(parts):
            picked = jnp.dot(pick[...], rows[:, part], preferred_element_type=F32)
            input_grad[:, part] = (my_weight * picked).astype(BF16)
            outs.append(
                pltpu.make_async_copy(
                    input_grad.at[:, part], input_hbm.at[:, part], input_sems.at[at]
                )
            )
            outs[-1].start()
    for copy in outs:
        copy.wait()


def finish(
    me, told, got, hidden_rows, pulled_rows, row_marks, count, seqs, width, pick, blocks, used
):
    slots, lanes = hidden_rows.shape
    rows = row_marks.shape[0]
    n_dev = told.shape[0]
    columns = got.shape[1] - width - MARKS
    n_parts = len(column_parts(width, columns))
    together = not any(size % 16 for size in used)
    vmem, hbm = pl.BlockSpec(memory_space=pltpu.VMEM), pl.BlockSpec(memory_space=pl.ANY)
    sems = pltpu.SemaphoreType.DMA
    out_shape = [
        jax.ShapeDtypeStruct((seqs // 2,), F32),
        jax.ShapeDtypeStruct((rows, 1), F32),
        jax.ShapeDtypeStruct((lanes, columns), BF16),
        jax.ShapeDtypeStruct((lanes, width), BF16),
    ]
    in_specs = [pl.BlockSpec(memory_space=pltpu.SMEM)] + [vmem] * 4 + [hbm]
    operands = [me.reshape(1), told, hidden_rows, pulled_rows, row_marks, got]
    scratch = [
        pltpu.VMEM(got.shape, BF16),
        pltpu.VMEM((lanes, columns), BF16),
        pltpu.VMEM((lanes, width), BF16),
    ]
    scratch_sems = [sems((n_parts + 1,)), sems, sems((n_parts,))]
    if together:
        out_shape.append(jax.ShapeDtypeStruct((rows, width), BF16))
        in_specs += [vmem] + [hbm] * len(blocks)
        operands += [pick, *blocks]
        scratch += [pltpu.VMEM((slots, width), BF16), pltpu.VMEM((rows, width), BF16)]
        scratch_sems += [sems((len(blocks),)), sems((n_parts,))]
    losses, row_weight, grad_up, grad_down, *input_grad = pl.pallas_call(
        functools.partial(
            finish_kernel, count, seqs, slots // n_dev, columns, used if together else []
        ),
        out_shape=out_shape,
        in_specs=in_specs,
        out_specs=[pl.BlockSpec(memory_space=pltpu.SMEM), vmem] + [hbm] * (len(out_shape) - 2),
        scratch_shapes=scratch + scratch_sems,
        compiler_params=pltpu.CompilerParams(vmem_limit_bytes=24 * 2**20),
        cost_estimate=pl.CostEstimate(
            flops=4 * slots * lanes * width,
            bytes_accessed=2 * (2 * slots + lanes + rows) * width,
            transcendentals=0,
        ),
        name="finish",
    )(*operands)
    if not together:
        blocks = jnp.concatenate([block[:size] for block, size in zip(blocks, used)])
        picked = jnp.dot(pick, blocks, preferred_element_type=F32)
        input_grad = [(row_weight * picked).astype(BF16)]
    return input_grad[0], grad_down, grad_up, losses


def slots_kernel(
    count, capacity, half_size, half_ref, owner_ref, adapter_ref, segment_ref, g_ref, *refs
):
    to_slot, to_half, marks_ref, sent_g = refs
    slots, rows = to_slot.shape
    out_width = g_ref.shape[1]
    eye = (iota((rows, rows), 0) == iota((rows, rows), 1)).astype(BF16)
    owner = lax.dot_general(
        owner_ref[...].astype(F32).astype(BF16),
        eye,
        (((0,), (0,)), ((), ())),
        preferred_element_type=F32,
    ).astype(jnp.int32)
    n_dev = 2 * half_size
    hot = (iota((n_dev, rows), 0) == owner).astype(F32)
    earlier = (iota((rows, rows), 0) < iota((rows, rows), 1)).astype(BF16)
    before = jnp.dot(hot.astype(BF16), earlier, preferred_element_type=F32)
    rank = jnp.sum(before * hot, axis=0, keepdims=True).astype(jnp.int32)
    at_slot = iota((slots, rows), 0)
    to_slot[...] = (at_slot == owner * capacity + rank).astype(BF16)
    far = owner // half_size != half_ref[0]
    position = (owner % half_size * 2 + far.astype(jnp.int32)) * capacity + rank
    hot_half = (at_slot == position).astype(BF16)
    to_half[...] = hot_half
    lane = iota((MARKS, rows), 0)
    marks = ((lane == adapter_ref[...]) | (lane == segment_ref[...] + count)).astype(BF16)
    marks_ref[...] = marks
    sent_g[:, :out_width] = jnp.dot(hot_half, g_ref[...], preferred_element_type=F32).astype(BF16)
    sent_g[:, out_width:] = lax.dot_general(
        hot_half, marks, (((1,), (1,)), ((), ())), preferred_element_type=F32
    ).astype(BF16)


def slot_rows(half_at, owner, adapter, segment, cotangent, count, capacity, half_size):
    rows, out_width = cotangent.shape
    slots = 2 * half_size * capacity
    vmem = pl.BlockSpec(memory_space=pltpu.VMEM)
    return pl.pallas_call(
        functools.partial(slots_kernel, count, capacity, half_size),
        out_shape=[
            jax.ShapeDtypeStruct((slots, rows), BF16),
            jax.ShapeDtypeStruct((slots, rows), BF16),
            jax.ShapeDtypeStruct((MARKS, rows), BF16),
            jax.ShapeDtypeStruct((slots, out_width + MARKS), BF16),
        ],
        in_specs=[pl.BlockSpec(memory_space=pltpu.SMEM)] + [vmem] * 4,
        out_specs=[vmem] * 4,
        name="slots",
    )(half_at.reshape(1), owner, adapter.reshape(1, rows), segment, cotangent)


def send_kernel(columns, to_slot, marks, g_ref, tokens_hbm, sent_hbm, tokens, sent, *sems):
    in_sems, out_sems = sems
    width, out_width = tokens.shape[1], g_ref.shape[1]
    parts = column_parts(width, columns)
    copies = [
        pltpu.make_async_copy(tokens_hbm.at[:, part], tokens.at[:, part], in_sems.at[at])
        for at, part in enumerate(parts)
    ]
    for copy in copies:
        copy.start()
    hot = to_slot[...]
    last = slice(width + out_width, width + out_width + MARKS)
    sent[:, width : width + out_width] = jnp.dot(
        hot, g_ref[...], preferred_element_type=F32
    ).astype(BF16)
    sent[:, last] = lax.dot_general(
        hot, marks[...], (((1,), (1,)), ((), ())), preferred_element_type=F32
    ).astype(BF16)
    outs = []

    def send(part):
        outs.append(
            pltpu.make_async_copy(
                sent.at[:, part], sent_hbm.at[:, part], out_sems.at[len(outs)]
            )
        )
        outs[-1].start()

    send(slice(width, width + out_width + MARKS))
    for copy, part in zip(copies, parts):
        copy.wait()
        sent[:, part] = jnp.dot(hot, tokens[:, part], preferred_element_type=F32).astype(BF16)
        send(part)
    for copy in outs:
        copy.wait()


def send_rows(to_slot, marks, cotangent, tokens):
    slots, (rows, width) = to_slot.shape[0], tokens.shape
    columns = cotangent.shape[1]
    full = width + columns + MARKS
    n_parts = len(column_parts(width, columns))
    vmem, hbm = pl.BlockSpec(memory_space=pltpu.VMEM), pl.BlockSpec(memory_space=pl.ANY)
    return pl.pallas_call(
        functools.partial(send_kernel, columns),
        out_shape=jax.ShapeDtypeStruct((slots, full), BF16),
        in_specs=[vmem] * 3 + [hbm],
        out_specs=hbm,
        scratch_shapes=[
            pltpu.VMEM((rows, width), BF16),
            pltpu.VMEM((slots, full), BF16),
            pltpu.SemaphoreType.DMA((n_parts,)),
            pltpu.SemaphoreType.DMA((n_parts + 1,)),
        ],
        compiler_params=pltpu.CompilerParams(vmem_limit_bytes=32 * 2**20),
        cost_estimate=pl.CostEstimate(
            flops=2 * slots * rows * full,
            bytes_accessed=2 * (slots + rows) * full,
            transcendentals=0,
        ),
        name="send",
    )(to_slot, marks, cotangent, tokens)


def half_kernel(which_ref, up_hbm, down_hbm, out, sems):
    out_width, which = up_hbm.shape[2], which_ref[0]
    width = down_hbm.shape[2]
    copies = [
        pltpu.make_async_copy(up_hbm.at[which], out.at[:, pl.ds(0, out_width)], sems.at[0]),
        pltpu.make_async_copy(
            down_hbm.at[which], out.at[:, pl.ds(out_width, width)], sems.at[1]
        ),
    ]
    for copy in copies:
        copy.start()
    for copy in copies:
        copy.wait()


def half_of(which, up_pair, down_pair):
    _, rank_size, width = down_pair.shape
    hbm = pl.BlockSpec(memory_space=pl.ANY)
    return pl.pallas_call(
        half_kernel,
        out_shape=jax.ShapeDtypeStruct((rank_size, up_pair.shape[2] + width), BF16),
        in_specs=[pl.BlockSpec(memory_space=pltpu.SMEM), hbm, hbm],
        out_specs=pl.BlockSpec(memory_space=pltpu.VMEM),
        scratch_shapes=[pltpu.SemaphoreType.DMA((2,))],
        name="half",
    )(which.reshape(1), up_pair, down_pair)


def body(
    tokens,
    cotangent,
    owner,
    token_local_adapter,
    segment,
    pair_sequence_order,
    frozen_margin_score,
    adapter_down_weight,
    adapter_up_weight,
):
    rows, width = tokens.shape
    out_width = cotangent.shape[1]
    n_grp, n_dev = lax.axis_size("grp"), lax.axis_size("ad")
    grp, me = lax.axis_index("grp"), lax.axis_index("ad")
    half_size = n_dev // 2
    spot = me % half_size
    capacity = max(2, 2 * rows // n_dev)
    slots = n_dev * capacity
    count, rank_size, _ = adapter_down_weight.shape
    seqs = frozen_margin_score.shape[1]
    lanes = count * rank_size
    down = adapter_down_weight.reshape(lanes, width)
    up = adapter_up_weight.reshape(lanes, out_width)

    def flipped(block, flip):
        return lax.ppermute(block, "ad", [(at, at ^ flip) for at in range(n_dev)])

    def other_grp(block):
        return lax.ppermute(block, "grp", [(0, 1), (1, 0)])

    half_mine = half_of(grp, adapter_up_weight, adapter_down_weight)
    far = flipped(half_mine, half_size)
    half_other = half_of(1 - grp, adapter_up_weight, adapter_down_weight)

    (owner,) = gate(lax.optimization_barrier((owner, half_mine))[0])
    row_seq = segment[0][:, None] == jnp.arange(seqs, dtype=jnp.int32)
    to_slot, to_half, marks, sent_g = slot_rows(
        me // half_size, owner, token_local_adapter, segment, cotangent, count, capacity, half_size
    )
    sent = send_rows(to_slot, marks, cotangent, tokens)

    halves = [list(range(half_size)), list(range(half_size, n_dev))]
    to_half = to_half.reshape(half_size, 2, capacity, rows)
    half_g = lax.all_to_all(
        sent_g.reshape(half_size, 2 * capacity, out_width + MARKS),
        "ad",
        split_axis=0,
        concat_axis=0,
        tiled=True,
        axis_index_groups=halves,
    )

    lane = jnp.arange(MARKS, dtype=jnp.int32)[None, :]
    which = (lane == jnp.stack([grp, 1 - grp])[:, None]).astype(F32)

    def land(blocks):
        return [block if at == 0 else flipped(block, 2 * at) for at, block in enumerate(blocks)]

    def hand_over(blocks):
        return blocks + [flipped(jnp.concatenate([block[capacity:] for block in blocks]), 1)]

    made_near = project(
        0, False, capacity, out_width, width, spot, half_g, which, [half_mine], [half_other]
    )
    landed_near = land(made_near)
    (sent,) = gate(lax.optimization_barrier((sent, made_near))[0])
    got = lax.all_to_all(
        sent.reshape(n_dev, capacity, width + out_width + MARKS),
        "ad",
        split_axis=0,
        concat_axis=0,
        tiled=True,
    ).reshape(slots, width + out_width + MARKS)

    (which_far,) = gate(lax.optimization_barrier((which, sent, landed_near))[0])
    far_other = other_grp(far)
    kept, handed = project(
        1, True, capacity, out_width, width, spot, half_g, which_far, [far], [far_other]
    )
    taken = flipped(handed, 1)
    landed_far = land(
        [
            jnp.concatenate([kept[at : at + capacity], taken[at : at + capacity]])
            for at in range(0, half_size // 2 * capacity, capacity)
        ]
    )
    pair_hot = pair_sequence_order[0][:, None] == jnp.arange(seqs, dtype=jnp.int32)
    at_me = (jnp.arange(n_dev, dtype=jnp.int32) == me)[:, None]
    own_scores = jnp.where(at_me, frozen_margin_score, 0.0).reshape(1, -1)
    own = jnp.concatenate(
        [
            jnp.pad(own_scores, ((0, 0), (0, -own_scores.shape[1] % MARKS))),
            jnp.zeros((1, count + seqs), F32),
            pair_hot.astype(F32).reshape(1, -1),
            jnp.zeros((1, MARKS - count - seqs - seqs * seqs), F32),
        ],
        axis=1,
    )
    hidden_rows, pulled_rows, part = score(own, got, down, up, count, seqs, rank_size, n_dev)
    told = lax.all_to_all(part, "ad", split_axis=0, concat_axis=0, tiled=True)

    chips = half_size // 2
    order = [2 * at for at in range(chips)] + [2 * at + 1 for at in range(chips)]
    near_flips = spot ^ jnp.array(order, dtype=jnp.int32)
    far_flips = spot ^ jnp.arange(half_size, dtype=jnp.int32)
    pick = jnp.concatenate([to_half[near_flips, 0], to_half[far_flips, 1]])
    pick = pick.reshape(slots, rows).T
    landed_far = lax.optimization_barrier((landed_far, told))[0]
    landed = hand_over(landed_near) + landed_far
    row_marks = jnp.pad(row_seq.astype(F32), ((0, 0), (count, MARKS - count - seqs)))
    input_grad, grad_down, grad_up, losses = finish(
        me,
        told,
        got,
        hidden_rows,
        pulled_rows,
        row_marks,
        count,
        seqs,
        width,
        pick,
        landed,
        [capacity] * chips + [chips * capacity] + [2 * capacity] * chips,
    )
    return (
        input_grad,
        grad_down.reshape(count, rank_size, width),
        grad_up.reshape(count, rank_size, out_width),
        losses,
    )


def solution(mesh):
    placed = (
        P(("grp", "ad"), None),
        P(("grp", "ad"), None),
        P(("grp", "ad"), None),
        P(("grp", "ad")),
        P(("grp", "ad"), None),
        P(("grp", "ad"), None),
        P(("grp", "ad"), None),
        P("ad", None, None),
        P("ad", None, None),
    )
    return jax.shard_map(
        body,
        mesh=mesh,
        in_specs=placed,
        out_specs=(
            P(("grp", "ad"), None),
            P(("grp", "ad"), None, None),
            P(("grp", "ad"), None, None),
            P(("grp", "ad")),
        ),
        check_vma=False,
    )
```

time: 205 us -> 196 us (0.956)
  matrix products: 18.8 us -> 0 us
  Pallas kernels: 14.2 us -> 31.3 us
  other arithmetic: 12.2 us -> 5.75 us
  local copies, waits for them, and re-layouts: 21.2 us -> 15.7 us
  starting transfers between devices: 45.8 us -> 48.9 us
    all_to_all x1, waiting for transfers between devices: 2.86 us -> 27.9 us  [body(): lax.all_to_all(sent.reshape(n_dev, capacity, width + out_width + MARKS),...]
    ppermute x1, waiting for transfers between devices: 21.2 us -> 0.01 us  [other_grp(): return lax.ppermute(block, 'grp', [(0, 1), (1, 0)])]
    dot_general x7 -> x0, matrix products: 18.8 us -> none  [the longest x1 5.28 us: body(): jnp.dot(to_slot, jnp.concatenate([tokens, marked], axis=1), preferred_ele...]
    pallas_call x1 -> x6, Pallas kernels: 4.93 us -> 22 us  [the longest x1 6.25 us: finish(): pl.pallas_call(functools.partial(finish_kernel, count, seqs, slots // n_d...]
    squeeze x2 -> x0, local copies, waits for them, and re-layouts: 4.33 us -> none  [the longest x1 2.68 us: half(): lax.dynamic_index_in_dim(adapter_down_weight, which, keepdims=False)]
    ppermute x9, waiting for transfers between devices: 49.4 us -> 45.7 us  [flipped(): return lax.ppermute(block, 'ad', [(at, at ^ flip) for at in range(n_dev)])]
    unnamed x56 -> x42, local copies, waits for them, and re-layouts: 3.54 us -> 7.05 us
    all_to_all x2, starting transfers between devices: 23.4 us -> 26 us  [the longest x1 22 us: body(): told = lax.all_to_all(part, 'ad', split_axis=0, concat_axis=0, tiled=True)]
  transfers between devices with their start and end apart: 13 -> 13, of which waited for: 8 -> 7; matrix products, arithmetic and copies ran while one was open for 21% -> 7% of each run, Pallas kernels for 5% -> 10%
where the time goes in v4:
time: 196 us
  waiting for transfers between devices  93 us (47%)
  starting transfers between devices  48.9 us (25%)
  Pallas kernels  31.3 us (16%)
  local copies, waits for them, and re-layouts  15.7 us (8%)
  other arithmetic  5.75 us (3%)
    ppermute x9, waiting for transfers between devices, flipped(): return lax.ppermute(block, 'ad', [(at, at ^ flip) for at in range(n_dev)])  45.7 us
    all_to_all x1, waiting for transfers between devices, body(): lax.all_to_all(sent.reshape(n_dev, capacity, width + out_width + MARKS),...  27.9 us
    all_to_all x1, starting transfers between devices, body(): told = lax.all_to_all(part, 'ad', split_axis=0, concat_axis=0, tiled=True)  22 us
    ppermute x9, starting transfers between devices, flipped(): return lax.ppermute(block, 'ad', [(at, at ^ flip) for at in range(n_dev)])  16.9 us
    all_to_all x1, waiting for transfers between devices, body(): lax.all_to_all(sent_g.reshape(half_size, 2 * capacity, out_width + MARKS)...  13.9 us
    pallas_call x2, Pallas kernels, project(): pl.pallas_call(functools.partial(project_kernel, side, split, capacity, o...  9.28 us
    unnamed x42, local copies, waits for them, and re-layouts  7.05 us
    pallas_call x1, Pallas kernels, finish(): pl.pallas_call(functools.partial(finish_kernel, count, seqs, slots // n_d...  6.25 us
  transfers between devices with their start and end apart: 13, of which 7 were waited for; matrix products, arithmetic and copies ran while one was open for 7% of the time, Pallas kernels for 10%

profile of v4, /device:TPU:0, one launch (start us, length us, event | category | flops | bytes accessed | tf_op | source)
XLA Modules:
  0.0 195.6 jit_solution(16712952252116049604)
XLA Ops:
  0.6 2.3 %half.2.refs_0_ = bf16[64,9216]{1,0:T(8,128)(2,1)} custom-call(s32[1]{0:T(128)} %bitcast.4.which_ref, bf16[2,64,1024]{2,1,0:T(8,128)(2,1)} %up_hbm.3, bf16[2,64,8192]{2,1,0:T(8,128)(2,1)} %down_hbm.3), custom_call_target="tpu_custom_call" | custom-call | tf_op jit(solution)/shard_map/half/pallas_call | solution.py:503
  3.0 4.1 %collective-permute-start.4 = (bf16[64,9216]{1,0:T(8,128)(2,1)}, bf16[64,9216]{1,0:T(8,128)(2,1)}, u32[]{:S(2)}, u32[]{:S(2)}) collective-permute-start(bf16[64,9216]{1,0:T(8,128)(2,1)} %half.2.refs_0_), channel_id=1, source_target_pairs={{0,8},{1,9},{2,10},{3,11},{4,12},{5,13},{6,14},{7,15},{8,0},{9,1},... | collective-permute-start | bytes 3538952 | tf_op jit(solution)/shard_map/ppermute | solution.py:539
  7.8 2.5 %slots.1 = (bf16[256,128]{1,0:T(8,128)(2,1)}, bf16[256,128]{1,0:T(8,128)(2,1)}, bf16[128,128]{1,0:T(8,128)(2,1)}, bf16[256,1152]{1,0:T(8,128)(2,1)}) custom-call(s32[1]{0:T(128)} %bitcast.3.half_ref, s32[128,1]{1,0:T(8,128)} %gate.3.owner_ref, s32[1,128]{1,0:T(1,128)} %bitcast.34, s32[1,128]{1,0:T(1,128)} %segment_ref.1, bf16[128,1024]{1,0:T(8,128)(2,1)} %g_ref.3), custom_call_target="tpu_custom_call" | custom-call | tf_op jit(solution)/shard_map/slots/pallas_call | solution.py:407
  10.3 4.0 %all-to-all-start = ((bf16[8,32,1152]{2,1,0:T(8,128)(2,1)}), bf16[8,32,1152]{2,1,0:T(8,128)(2,1)S(1)}, u32[]{:S(2)}, u32[]{:S(2)}) async-start(bf16[8,32,1152]{2,1,0:T(8,128)(2,1)} %bitcast.27), calls=%async_computation | async-start | bytes 1179648 | tf_op jit(solution)/shard_map/all_to_all | solution.py:557
  14.3 2.5 %half.3.refs_1_ = bf16[64,9216]{1,0:T(8,128)(2,1)} custom-call(s32[1]{0:T(128)} %bitcast.8.which_ref, bf16[2,64,1024]{2,1,0:T(8,128)(2,1)} %up_hbm.3, bf16[2,64,8192]{2,1,0:T(8,128)(2,1)} %down_hbm.3), custom_call_target="tpu_custom_call" | custom-call | tf_op jit(solution)/shard_map/half/pallas_call | solution.py:503
  18.6 3.2 %send.1.refs_0_ = bf16[256,9344]{1,0:T(8,128)(2,1)S(1)} custom-call(bf16[256,128]{1,0:T(8,128)(2,1)S(1)} %copy-done.7, bf16[128,128]{1,0:T(8,128)(2,1)S(1)} %copy-done.12, bf16[128,1024]{1,0:T(8,128)(2,1)S(1)} %copy-done.6, bf16[128,8192]{1,0:T(8,128)(2,1)S(1)} %copy-done.3), custom_call_target="tpu_custom_call" | custom-call | flops 612368384 | bytes 7176192 | tf_op jit(solution)/shard_map/send/pallas_call | solution.py:464
  21.9 2.2 %copy-done = bf16[256,9344]{1,0:T(8,128)(2,1)} copy-done((bf16[256,9344]{1,0:T(8,128)(2,1)}, bf16[256,9344]{1,0:T(8,128)(2,1)S(1)}, u32[]{:S(2)}) %copy-start) | copy-done | bytes 4784152
  25.1 13.9 %all-to-all-done.g_ref = bf16[8,32,1152]{2,1,0:T(8,128)(2,1)S(1)} async-done(((bf16[8,32,1152]{2,1,0:T(8,128)(2,1)}), bf16[8,32,1152]{2,1,0:T(8,128)(2,1)S(1)}, u32[]{:S(2)}, u32[]{:S(2)}) %all-to-all-start) | async-done | bytes 589856 | tf_op jit(solution)/shard_map/all_to_all | solution.py:557
  39.8 4.7 %project.2 = (bf16[32,8192]{1,0:T(8,128)(2,1)}, bf16[32,8192]{1,0:T(8,128)(2,1)}, bf16[32,8192]{1,0:T(8,128)(2,1)}, bf16[32,8192]{1,0:T(8,128)(2,1)}) custom-call(s32[1]{0:T(128)} %bitcast.6.spot_ref, bf16[8,32,1152]{2,1,0:T(8,128)(2,1)} %copy-done.13, f32[2,128]{1,0:T(2,128)} %compare_convert_fusion.which.refs_0_, bf16[64,9216]{1,0:T(8,128)(2,1)} %half.2.refs_0_, ...), custom_call_target="tpu_custom_call" | custom-call | flops 1000 | bytes 1000 | tf_op jit(solution)/shard_map/project/pallas_call | solution.py:75
  44.5 1.5 collective-permute-start
  46.0 2.4 %collective-permute-start.1 = (bf16[32,8192]{1,0:T(8,128)(2,1)}, bf16[32,8192]{1,0:T(8,128)(2,1)}, u32[]{:S(2)}, u32[]{:S(2)}) collective-permute-start(bf16[32,8192]{1,0:T(8,128)(2,1)} %get-tuple-element.34), channel_id=1, source_target_pairs={{0,4},{1,5},{2,6},{3,7},{4,0},{5,1},{6,2},{7,3},{8,12},{9,13},{10,... | collective-permute-start | bytes 1572872 | tf_op jit(solution)/shard_map/ppermute | solution.py:539
  48.4 1.0 copy-done.4
  50.2 4.6 %all-to-all-start.1 = ((bf16[16,16,9344]{2,1,0:T(8,128)(2,1)}), bf16[16,16,9344]{2,1,0:T(8,128)(2,1)}, u32[]{:S(2)}, u32[]{:S(2)}) async-start(bf16[16,16,9344]{2,1,0:T(8,128)(2,1)} %bitcast.23), calls=%async_computation.1 | async-start | bytes 9568256 | tf_op jit(solution)/shard_map/all_to_all | solution.py:580
  54.7 4.0 %collective-permute-done.4.refs_0_ = bf16[64,9216]{1,0:T(8,128)(2,1)} collective-permute-done((bf16[64,9216]{1,0:T(8,128)(2,1)}, bf16[64,9216]{1,0:T(8,128)(2,1)}, u32[]{:S(2)}, u32[]{:S(2)}) %collective-permute-start.4) | collective-permute-done | bytes 1179680 | tf_op jit(solution)/shard_map/ppermute | solution.py:539
  58.8 1.5 collective-permute-start.5
  60.3 35.3 %collective-permute-done.1.refs_7_ = bf16[32,8192]{1,0:T(8,128)(2,1)} collective-permute-done((bf16[32,8192]{1,0:T(8,128)(2,1)}, bf16[32,8192]{1,0:T(8,128)(2,1)}, u32[]{:S(2)}, u32[]{:S(2)}) %collective-permute-start.1) | collective-permute-done | bytes 524320 | tf_op jit(solution)/shard_map/ppermute | solution.py:539
  95.6 5.8 %collective-permute-done.2.refs_8_ = bf16[32,8192]{1,0:T(8,128)(2,1)} collective-permute-done((bf16[32,8192]{1,0:T(8,128)(2,1)}, bf16[32,8192]{1,0:T(8,128)(2,1)}, u32[]{:S(2)}, u32[]{:S(2)}) %collective-permute-start.2) | collective-permute-done | bytes 524320 | tf_op jit(solution)/shard_map/ppermute | solution.py:539
  101.5 1.0 slice.52
  102.5 1.0 slice.53
  103.4 1.0 slice.54
  104.4 1.0 pad_maximum_fusion
  105.5 4.6 %project.3 = (bf16[64,8192]{1,0:T(8,128)(2,1)}, bf16[64,8192]{1,0:T(8,128)(2,1)}) custom-call(s32[1]{0:T(128)} %bitcast.6.spot_ref, bf16[8,32,1152]{2,1,0:T(8,128)(2,1)} %copy-done.13, f32[2,128]{1,0:T(2,128)} %gate.5.which, bf16[64,9216]{1,0:T(8,128)(2,1)} %collective-permute-done.4.refs_0_, bf16[64,9216]{1,0:T(8,128)(2,1)} %collective-permute-done.5.refs_1_), custom_call_target="tpu_custom_call" | custom-call | flops 1000 | bytes 1000 | tf_op jit(solution)/shard_map/project/pallas_call | solution.py:75
  110.6 2.0 fusion.10
  113.9 0.8 pad_maximum_fusion.4
  114.7 0.8 pad_maximum_fusion.3
  115.6 8.3 %collective-permute-start.8 = (bf16[32,8192]{1,0:T(8,128)(2,1)}, bf16[32,8192]{1,0:T(8,128)(2,1)}, u32[]{:S(2)}, u32[]{:S(2)}) collective-permute-start(bf16[32,8192]{1,0:T(8,128)(2,1)} %pad_maximum_fusion.3), channel_id=1, source_target_pairs={{0,4},{1,5},{2,6},{3,7},{4,0},{5,1},{6,2},{7,3},{8,12},{9,13},{10,... | collective-permute-start | bytes 1572872 | tf_op jit(solution)/shard_map/ppermute | solution.py:539
  124.7 27.9 %all-to-all-done.1 = bf16[16,16,9344]{2,1,0:T(8,128)(2,1)} async-done(((bf16[16,16,9344]{2,1,0:T(8,128)(2,1)}), bf16[16,16,9344]{2,1,0:T(8,128)(2,1)}, u32[]{:S(2)}, u32[]{:S(2)}) %all-to-all-start.1) | async-done | bytes 4784160 | tf_op jit(solution)/shard_map/all_to_all | solution.py:580
  152.6 5.3 %score.1 = (bf16[256,128]{1,0:T(8,128)(2,1)S(1)}, bf16[256,128]{1,0:T(8,128)(2,1)S(1)}, f32[16,1,256]{2,1,0:T(1,128)}) custom-call(f32[1,256]{1,0:T(1,128)S(1)} %fusion.3.own_ref, bf16[256,9344]{1,0:T(8,128)(2,1)} %bitcast.10.got_hbm.refs_3_, bf16[128,8192]{1,0:T(8,128)(2,1)S(1)} %bitcast.24, bf16[128,1024]{1,0:T(8,128)(2,1)S(1)} %bitcast.25), custom_call_target="tpu_custom_call" | custom-call | flops 603979776 | bytes 7077888 | tf_op jit(solution)/shard_map/score/pallas_call | solution.py:177
  159.1 22.0 %all-to-all-start.2 = ((f32[16,1,256]{2,1,0:T(1,128)}), f32[16,1,256]{2,1,0:T(1,128)S(1)}, u32[]{:S(2)}, u32[]{:S(2)}) async-start(f32[16,1,256]{2,1,0:T(1,128)} %get-tuple-element.37), calls=%async_computation.2 | async-start | bytes 32768 | tf_op jit(solution)/shard_map/all_to_all | solution.py:613
  181.2 1.1 pad_maximum_fusion.1.refs_10_
  182.3 5.4 %all-to-all-done.2.told_ref = f32[16,1,256]{2,1,0:T(1,128)S(1)} async-done(((f32[16,1,256]{2,1,0:T(1,128)}), f32[16,1,256]{2,1,0:T(1,128)S(1)}, u32[]{:S(2)}, u32[]{:S(2)}) %all-to-all-start.2) | async-done | bytes 16416 | tf_op jit(solution)/shard_map/all_to_all | solution.py:613
  189.4 6.2 %finish.1 = (f32[2]{0:T(128)}, f32[128,1]{1,0:T(8,128)}, bf16[128,1024]{1,0:T(8,128)(2,1)}, bf16[128,8192]{1,0:T(8,128)(2,1)}, bf16[128,8192]{1,0:T(8,128)(2,1)}) custom-call(s32[1]{0:T(128)} %bitcast.me_ref, f32[16,1,256]{2,1,0:T(1,128)S(1)} %all-to-all-done.2.told_ref, bf16[256,128]{1,0:T(8,128)(2,1)S(1)} %copy-done.9, bf16[256,128]{1,0:T(8,128)(2,1)S(1)} %copy-done.11, ...), custom_call_target="tpu_custom_call" | custom-call | flops 1073741824 | bytes 12582912 | tf_op jit(solution)/shard_map/finish/pallas_call | solution.py:347
  (79 shorter events, 10.6 us)
Async XLA Ops:
  0.6 6.5 %copy-start.17 = (s32[128,1]{0,1:T(1,128)S(1)}, s32[128,1]{0,1:T(1,128)}, u32[]{:S(2)}) copy-start(s32[128,1]{0,1:T(1,128)} %param.12) | copy-start | bytes 1540
  3.0 55.8 %collective-permute-start.4 = (bf16[64,9216]{1,0:T(8,128)(2,1)}, bf16[64,9216]{1,0:T(8,128)(2,1)}, u32[]{:S(2)}, u32[]{:S(2)}) collective-permute-start(bf16[64,9216]{1,0:T(8,128)(2,1)} %half.2.refs_0_), channel_id=1, source_target_pairs={{0,8},{1,9},{2,10},{3,11},{4,12},{5,13},{6,14},{7,15},{8,0},{9,1},... | collective-permute-start | bytes 3538952 | tf_op jit(solution)/shard_map/ppermute | solution.py:539
  10.3 6.5 %copy-start.18 = (f32[1,4]{1,0:T(1,128)S(1)}, f32[1,4]{1,0:T(1,128)}, u32[]{:S(2)}) copy-start(f32[1,4]{1,0:T(1,128)} %param.16) | copy-start | bytes 52
  10.3 6.7 %copy-start.19 = (s32[1,4]{1,0:T(1,128)S(1)}, s32[1,4]{1,0:T(1,128)}, u32[]{:S(2)}) copy-start(s32[1,4]{1,0:T(1,128)} %param.15) | copy-start | bytes 52
  10.3 7.0 %copy-start.20 = (s32[8]{0:T(128)S(1)}, s32[8]{0:T(128)}, u32[]{:S(2)}) copy-start(s32[8]{0:T(128)} %constant.50.clone) | copy-start | bytes 100
  10.3 7.0 %copy-start.15 = (bf16[256,128]{1,0:T(8,128)(2,1)S(1)}, bf16[256,128]{1,0:T(8,128)(2,1)}, u32[]{:S(2)}) copy-start(bf16[256,128]{1,0:T(8,128)(2,1)} %get-tuple-element.40) | copy-start | bytes 196612
  10.3 28.7 %all-to-all-start = ((bf16[8,32,1152]{2,1,0:T(8,128)(2,1)}), bf16[8,32,1152]{2,1,0:T(8,128)(2,1)S(1)}, u32[]{:S(2)}, u32[]{:S(2)}) async-start(bf16[8,32,1152]{2,1,0:T(8,128)(2,1)} %bitcast.27), calls=%async_computation | async-start | bytes 1179648 | tf_op jit(solution)/shard_map/all_to_all | solution.py:557
  14.3 4.3 %copy-start.3 = (bf16[128,8192]{1,0:T(8,128)(2,1)S(1)}, bf16[128,8192]{1,0:T(8,128)(2,1)}, u32[]{:S(2)}) copy-start(bf16[128,8192]{1,0:T(8,128)(2,1)} %tokens_hbm.1) | copy-start | bytes 6291460
  14.3 4.3 %copy-start.6 = (bf16[128,1024]{1,0:T(8,128)(2,1)S(1)}, bf16[128,1024]{1,0:T(8,128)(2,1)}, u32[]{:S(2)}) copy-start(bf16[128,1024]{1,0:T(8,128)(2,1)} %g_ref.3) | copy-start | bytes 786436
  14.3 4.3 %copy-start.7 = (bf16[256,128]{1,0:T(8,128)(2,1)S(1)}, bf16[256,128]{1,0:T(8,128)(2,1)}, u32[]{:S(2)}) copy-start(bf16[256,128]{1,0:T(8,128)(2,1)} %get-tuple-element.29.to_slot) | copy-start | bytes 196612
  14.3 4.3 %copy-start.12 = (bf16[128,128]{1,0:T(8,128)(2,1)S(1)}, bf16[128,128]{1,0:T(8,128)(2,1)}, u32[]{:S(2)}) copy-start(bf16[128,128]{1,0:T(8,128)(2,1)} %get-tuple-element.30.marks) | copy-start | bytes 98308
  18.6 5.5 %copy-start.16 = (s32[1,128]{1,0:T(1,128)S(1)}, s32[1,128]{1,0:T(1,128)}, u32[]{:S(2)}) copy-start(s32[1,128]{1,0:T(1,128)} %segment_ref.1) | copy-start | bytes 1540
  21.9 2.2 %copy-start = (bf16[256,9344]{1,0:T(8,128)(2,1)}, bf16[256,9344]{1,0:T(8,128)(2,1)S(1)}, u32[]{:S(2)}) copy-start(bf16[256,9344]{1,0:T(8,128)(2,1)S(1)} %send.1.refs_0_) | copy-start | bytes 14352388
  39.0 0.8 copy-start.13
  44.5 15.8 %collective-permute-start = (bf16[32,8192]{1,0:T(8,128)(2,1)}, bf16[32,8192]{1,0:T(8,128)(2,1)}, u32[]{:S(2)}, u32[]{:S(2)}) collective-permute-start(bf16[32,8192]{1,0:T(8,128)(2,1)} %get-tuple-element.33), channel_id=1, source_target_pairs={{0,2},{1,3},{2,0},{3,1},{4,6},{5,7},{6,4},{7,5},{8,10},{9,11},{10,... | collective-permute-start | bytes 1572872 | tf_op jit(solution)/shard_map/ppermute | solution.py:539
  46.0 49.6 %collective-permute-start.1 = (bf16[32,8192]{1,0:T(8,128)(2,1)}, bf16[32,8192]{1,0:T(8,128)(2,1)}, u32[]{:S(2)}, u32[]{:S(2)}) collective-permute-start(bf16[32,8192]{1,0:T(8,128)(2,1)} %get-tuple-element.34), channel_id=1, source_target_pairs={{0,4},{1,5},{2,6},{3,7},{4,0},{5,1},{6,2},{7,3},{8,12},{9,13},{10,... | collective-permute-start | bytes 1572872 | tf_op jit(solution)/shard_map/ppermute | solution.py:539
  48.4 53.1 %collective-permute-start.2 = (bf16[32,8192]{1,0:T(8,128)(2,1)}, bf16[32,8192]{1,0:T(8,128)(2,1)}, u32[]{:S(2)}, u32[]{:S(2)}) collective-permute-start(bf16[32,8192]{1,0:T(8,128)(2,1)} %get-tuple-element.35), channel_id=1, source_target_pairs={{0,6},{1,7},{2,4},{3,5},{4,2},{5,3},{6,0},{7,1},{8,14},{9,15},{10,... | collective-permute-start | bytes 1572872 | tf_op jit(solution)/shard_map/ppermute | solution.py:539
  48.4 1.0 copy-start.4
  50.2 102.5 %all-to-all-start.1 = ((bf16[16,16,9344]{2,1,0:T(8,128)(2,1)}), bf16[16,16,9344]{2,1,0:T(8,128)(2,1)}, u32[]{:S(2)}, u32[]{:S(2)}) async-start(bf16[16,16,9344]{2,1,0:T(8,128)(2,1)} %bitcast.23), calls=%async_computation.1 | async-start | bytes 9568256 | tf_op jit(solution)/shard_map/all_to_all | solution.py:580
  58.8 46.7 %collective-permute-start.5 = (bf16[64,9216]{1,0:T(8,128)(2,1)}, bf16[64,9216]{1,0:T(8,128)(2,1)}, u32[]{:S(2)}, u32[]{:S(2)}) collective-permute-start(bf16[64,9216]{1,0:T(8,128)(2,1)} %collective-permute-done.4.refs_0_), channel_id=1, source_target_pairs={{0,16},{16,0},{1,17},{17,1},{2,18},{18,2},{3,19},{19,3},{4,20},{20... | collective-permute-start | bytes 3538952 | tf_op jit(solution)/shard_map/ppermute | solution.py:542
  101.4 3.0 %copy-start.14 = (bf16[16,8192]{1,0:T(8,128)(2,1)S(1)}, bf16[16,8192]{1,0:T(8,128)(2,1)}, u32[]{:S(2)}) copy-start(bf16[16,8192]{1,0:T(8,128)(2,1)} %slice.36) | copy-start | bytes 786436
  105.5 82.2 %collective-permute-start.3 = (bf16[64,8192]{1,0:T(8,128)(2,1)}, bf16[64,8192]{1,0:T(8,128)(2,1)}, u32[]{:S(2)}, u32[]{:S(2)}) collective-permute-start(bf16[64,8192]{1,0:T(8,128)(2,1)} %pad_maximum_fusion), channel_id=1, source_target_pairs={{0,1},{1,0},{2,3},{3,2},{4,5},{5,4},{6,7},{7,6},{8,9},{9,8},{10,11... | collective-permute-start | bytes 3145736 | tf_op jit(solution)/shard_map/ppermute | solution.py:539
  110.1 3.0 %collective-permute-start.6 = (bf16[64,8192]{1,0:T(8,128)(2,1)}, bf16[64,8192]{1,0:T(8,128)(2,1)S(1)}, u32[]{:S(2)}, u32[]{:S(2)}) collective-permute-start(bf16[64,8192]{1,0:T(8,128)(2,1)} %get-tuple-element.43), channel_id=1, source_target_pairs={{0,1},{1,0},{2,3},{3,2},{4,5},{5,4},{6,7},{7,6},{8,9},{9,8},{10,11... | collective-permute-start | bytes 3145736 | tf_op jit(solution)/shard_map/ppermute | solution.py:539
  113.9 38.8 %copy-start.1 = (bf16[2,64,8192]{2,1,0:T(8,128)(2,1)S(1)}, bf16[2,64,8192]{2,1,0:T(8,128)(2,1)}, u32[]{:S(2)}) copy-start(bf16[2,64,8192]{2,1,0:T(8,128)(2,1)} %down_hbm.3) | copy-start | bytes 6291460
  113.9 38.8 %copy-start.2 = (bf16[2,64,1024]{2,1,0:T(8,128)(2,1)S(1)}, bf16[2,64,1024]{2,1,0:T(8,128)(2,1)}, u32[]{:S(2)}) copy-start(bf16[2,64,1024]{2,1,0:T(8,128)(2,1)} %up_hbm.3) | copy-start | bytes 786436
  114.7 67.5 %collective-permute-start.9 = (bf16[32,8192]{1,0:T(8,128)(2,1)}, bf16[32,8192]{1,0:T(8,128)(2,1)S(1)}, u32[]{:S(2)}, u32[]{:S(2)}) collective-permute-start(bf16[32,8192]{1,0:T(8,128)(2,1)} %pad_maximum_fusion.4), channel_id=1, source_target_pairs={{0,6},{1,7},{2,4},{3,5},{4,2},{5,3},{6,0},{7,1},{8,14},{9,15},{10,... | collective-permute-start | bytes 1572872 | tf_op jit(solution)/shard_map/ppermute | solution.py:539
  115.6 66.7 %collective-permute-start.8 = (bf16[32,8192]{1,0:T(8,128)(2,1)}, bf16[32,8192]{1,0:T(8,128)(2,1)}, u32[]{:S(2)}, u32[]{:S(2)}) collective-permute-start(bf16[32,8192]{1,0:T(8,128)(2,1)} %pad_maximum_fusion.3), channel_id=1, source_target_pairs={{0,4},{1,5},{2,6},{3,7},{4,0},{5,1},{6,2},{7,3},{8,12},{9,13},{10,... | collective-permute-start | bytes 1572872 | tf_op jit(solution)/shard_map/ppermute | solution.py:539
  124.7 57.5 %collective-permute-start.7 = (bf16[32,8192]{1,0:T(8,128)(2,1)}, bf16[32,8192]{1,0:T(8,128)(2,1)}, u32[]{:S(2)}, u32[]{:S(2)}) collective-permute-start(bf16[32,8192]{1,0:T(8,128)(2,1)} %pad_maximum_fusion.2), channel_id=1, source_target_pairs={{0,2},{1,3},{2,0},{3,1},{4,6},{5,7},{6,4},{7,5},{8,10},{9,11},{10,... | collective-permute-start | bytes 1572872 | tf_op jit(solution)/shard_map/ppermute | solution.py:539
  152.6 35.1 %copy-start.5 = (bf16[32,8192]{1,0:T(8,128)(2,1)S(1)}, bf16[32,8192]{1,0:T(8,128)(2,1)}, u32[]{:S(2)}) copy-start(bf16[32,8192]{1,0:T(8,128)(2,1)} %get-tuple-element.32.refs_5_) | copy-start | bytes 1572868
  159.1 28.5 %all-to-all-start.2 = ((f32[16,1,256]{2,1,0:T(1,128)}), f32[16,1,256]{2,1,0:T(1,128)S(1)}, u32[]{:S(2)}, u32[]{:S(2)}) async-start(f32[16,1,256]{2,1,0:T(1,128)} %get-tuple-element.37), calls=%async_computation.2 | async-start | bytes 32768 | tf_op jit(solution)/shard_map/all_to_all | solution.py:613
  187.7 0.8 copy-start.9
  188.5 0.8 copy-start.11
  (2 other events, 1.2 us)

commit v5 on v4

--- a/solution.py
+++ b/solution.py
@@ -113,32 +113,26 @@
 
 
 def score_kernel(
-    count, seqs, rank_size, capacity, columns, own_ref, got_hbm, down_hbm, up_hbm, *refs
+    count, seqs, rank_size, capacity, columns, own_ref, got_hbm, down, up, *refs
 ):
-    hidden_ref, pulled_ref, told_ref, got, down, up, got_sems, down_sems, up_sem = refs
+    told_ref, rows_hbm, got, rank_rows, got_sems, rows_sem = refs
     width, out_width = down.shape[1], up.shape[1]
     parts = column_parts(width, columns)
     tail = slice(width, got.shape[1])
     copies = []
     for at, part in enumerate(parts):
         copies.append(
-            (
-                pltpu.make_async_copy(got_hbm.at[:, part], got.at[:, part], got_sems.at[at]),
-                pltpu.make_async_copy(down_hbm.at[:, part], down.at[:, part], down_sems.at[at]),
-            )
+            (pltpu.make_async_copy(got_hbm.at[:, part], got.at[:, part], got_sems.at[at]),)
         )
     tail_copy = pltpu.make_async_copy(got_hbm.at[:, tail], got.at[:, tail], got_sems.at[len(parts)])
-    up_copy = pltpu.make_async_copy(up_hbm, up, up_sem)
     tail_copy.start()
-    up_copy.start()
     for pair in copies:
         for copy in pair:
             copy.start()
     contract = (((1,), (1,)), ((), ()))
     tail_copy.wait()
-    up_copy.wait()
     marks = got[:, width + out_width :].astype(F32)
-    slots, lanes = hidden_ref.shape
+    slots, lanes = got.shape[0], down.shape[0]
     lane = iota((slots, lanes), 1) // rank_size
     member = jnp.zeros((slots, lanes), F32)
     for which in range(count):
@@ -146,7 +140,7 @@
     pulled = member * lax.dot_general(
         got[:, width : width + out_width], up[...], contract, preferred_element_type=F32
     )
-    pulled_ref[...] = pulled.astype(BF16)
+    rank_rows[:, lanes:] = pulled.astype(BF16)
     total = jnp.zeros((slots, lanes), F32)
     for pair, part in zip(copies, parts):
         for copy in pair:
@@ -155,7 +149,9 @@
             got[:, part], down[:, part], contract, preferred_element_type=F32
         )
     hidden = (member * total).astype(BF16)
-    hidden_ref[...] = hidden
+    rank_rows[:, :lanes] = hidden
+    rows_copy = pltpu.make_async_copy(rank_rows, rows_hbm, rows_sem)
+    rows_copy.start()
     inner = SCALE * jnp.sum(hidden.astype(F32) * pulled, axis=1, keepdims=True)
     n_dev, _, all_lanes = told_ref.shape
     hot = iota((n_dev, slots), 1) // capacity == iota((n_dev, slots), 0)
@@ -166,6 +162,7 @@
     row = jnp.sum(jnp.where(at_device, spread, 0.0), axis=0, keepdims=True)
     row = jnp.concatenate([row, jnp.zeros((1, MARKS), F32)], axis=1) + own_ref[...]
     told_ref[...] = jnp.broadcast_to(row[None], told_ref.shape)
+    rows_copy.wait()
 
 
 def score(own, got, down, up, count, seqs, rank_size, n_dev):
@@ -177,18 +174,15 @@
     return pl.pallas_call(
         functools.partial(score_kernel, count, seqs, rank_size, slots // n_dev, columns),
         out_shape=[
-            jax.ShapeDtypeStruct((slots, lanes), BF16),
-            jax.ShapeDtypeStruct((slots, lanes), BF16),
             jax.ShapeDtypeStruct((n_dev,) + own.shape, F32),
+            pltpu.HBM((slots, 2 * lanes), BF16),
         ],
-        in_specs=[vmem, hbm, hbm, hbm],
-        out_specs=[vmem] * 3,
+        in_specs=[vmem, hbm, vmem, vmem],
+        out_specs=[vmem, pl.BlockSpec(memory_space=pltpu.HBM)],
         scratch_shapes=[
             pltpu.VMEM(got.shape, BF16),
-            pltpu.VMEM(down.shape, BF16),
-            pltpu.VMEM(up.shape, BF16),
+            pltpu.VMEM((slots, 2 * lanes), BF16),
             pltpu.SemaphoreType.DMA((n_parts + 1,)),
-            pltpu.SemaphoreType.DMA((n_parts,)),
             pltpu.SemaphoreType.DMA,
         ],
         compiler_params=pltpu.CompilerParams(vmem_limit_bytes=16 * 2**20),
@@ -224,16 +218,16 @@
 
 
 def finish_kernel(count, seqs, capacity, columns, used, me_ref, told_ref, *refs):
-    hidden_ref, pulled_ref, row_marks, got_hbm, *refs = refs
+    row_marks, rank_hbm, got_hbm, *refs = refs
     if used:
         pick, *refs = refs
     block_hbms, refs = refs[: len(used)], refs[len(used) :]
     losses_ref, row_weight, up_hbm, down_hbm, *refs = refs
     if used:
-        input_hbm, got, grad_up, grad_down, rows, input_grad, *sems = refs
-        got_sems, up_sem, down_sems, block_sems, input_sems = sems
+        input_hbm, rank_rows, got, grad_up, grad_down, rows, input_grad, *sems = refs
+        rank_sem, got_sems, up_sem, down_sems, block_sems, input_sems = sems
     else:
-        got, grad_up, grad_down, got_sems, up_sem, down_sems = refs
+        rank_rows, got, grad_up, grad_down, rank_sem, got_sems, up_sem, down_sems = refs
     width, out_width = grad_down.shape[1], grad_up.shape[1]
     parts = column_parts(width, columns)
     tail = slice(width, got.shape[1])
@@ -250,6 +244,8 @@
             )
         )
         first += size
+    rank_copy = pltpu.make_async_copy(rank_hbm, rank_rows, rank_sem)
+    rank_copy.start()
     tail_copy.start()
     for copy in copies + block_copies:
         copy.start()
@@ -280,8 +276,10 @@
     tail_copy.wait()
     marks = got[:, width + out_width :].astype(F32)
     weight = jnp.sum(marks * slot_table, axis=1, keepdims=True)
-    lower = (weight * pulled_ref[...].astype(F32)).astype(BF16)
-    upper = (weight * hidden_ref[...].astype(F32)).astype(BF16)
+    rank_copy.wait()
+    lanes = grad_up.shape[0]
+    upper = (weight * rank_rows[:, :lanes].astype(F32)).astype(BF16)
+    lower = (weight * rank_rows[:, lanes:].astype(F32)).astype(BF16)
     contract = (((0,), (0,)), ((), ()))
     made = lax.dot_general(
         upper, got[:, width : width + out_width], contract, preferred_element_type=F32
@@ -314,15 +312,15 @@
 
 
 def finish(
-    me, told, got, hidden_rows, pulled_rows, row_marks, count, seqs, width, pick, blocks, used
+    me, told, got, rank_rows, row_marks, count, seqs, width, pick, blocks, used
 ):
-    slots, lanes = hidden_rows.shape
+    slots, lanes = rank_rows.shape[0], rank_rows.shape[1] // 2
     rows = row_marks.shape[0]
     n_dev = told.shape[0]
     columns = got.shape[1] - width - MARKS
     n_parts = len(column_parts(width, columns))
     together = not any(size % 16 for size in used)
-    vmem, hbm = pl.BlockSpec(memory_space=pltpu.VMEM), pl.BlockSpec(memory_space=pl.ANY)
+    vmem, hbm = pl.BlockSpec(memory_space=pltpu.VMEM), pl.BlockSpec(memory_space=pltpu.HBM)
     sems = pltpu.SemaphoreType.DMA
     out_shape = [
         jax.ShapeDtypeStruct((seqs // 2,), F32),
@@ -330,14 +328,16 @@
         jax.ShapeDtypeStruct((lanes, columns), BF16),
         jax.ShapeDtypeStruct((lanes, width), BF16),
     ]
-    in_specs = [pl.BlockSpec(memory_space=pltpu.SMEM)] + [vmem] * 4 + [hbm]
-    operands = [me.reshape(1), told, hidden_rows, pulled_rows, row_marks, got]
+    in_specs = [pl.BlockSpec(memory_space=pltpu.SMEM)] + [vmem] * 2 + [hbm] * 2
+    rank_rows = pltpu.with_memory_space_constraint(rank_rows, pltpu.HBM)
+    operands = [me.reshape(1), told, row_marks, rank_rows, got]
     scratch = [
+        pltpu.VMEM(rank_rows.shape, BF16),
         pltpu.VMEM(got.shape, BF16),
         pltpu.VMEM((lanes, columns), BF16),
         pltpu.VMEM((lanes, width), BF16),
     ]
-    scratch_sems = [sems((n_parts + 1,)), sems, sems((n_parts,))]
+    scratch_sems = [sems, sems((n_parts + 1,)), sems, sems((n_parts,))]
     if together:
         out_shape.append(jax.ShapeDtypeStruct((rows, width), BF16))
         in_specs += [vmem] + [hbm] * len(blocks)
@@ -609,7 +609,7 @@
         ],
         axis=1,
     )
-    hidden_rows, pulled_rows, part = score(own, got, down, up, count, seqs, rank_size, n_dev)
+    part, rank_rows = score(own, got, down, up, count, seqs, rank_size, n_dev)
     told = lax.all_to_all(part, "ad", split_axis=0, concat_axis=0, tiled=True)
 
     chips = half_size // 2
@@ -625,8 +625,7 @@
         me,
         told,
         got,
-        hidden_rows,
-        pulled_rows,
+        rank_rows,
         row_marks,
         count,
         seqs,

time: 196 us -> 194 us (0.990)
  local copies, waits for them, and re-layouts: 15.7 us -> 12.8 us
    unnamed x42 -> x34, local copies, waits for them, and re-layouts: 7.05 us -> 4.11 us
where the time goes in v5:
time: 194 us
  waiting for transfers between devices  92.9 us (48%)
  starting transfers between devices  49 us (25%)
  Pallas kernels  32.3 us (17%)
  local copies, waits for them, and re-layouts  12.8 us (7%)
  other arithmetic  5.76 us (3%)
    ppermute x9, waiting for transfers between devices, flipped(): return lax.ppermute(block, 'ad', [(at, at ^ flip) for at in range(n_dev)])  45.7 us
    all_to_all x1, waiting for transfers between devices, body(): lax.all_to_all(sent.reshape(n_dev, capacity, width + out_width + MARKS),...  27.9 us
    all_to_all x1, starting transfers between devices, body(): told = lax.all_to_all(part, 'ad', split_axis=0, concat_axis=0, tiled=True)  22.1 us
    ppermute x9, starting transfers between devices, flipped(): return lax.ppermute(block, 'ad', [(at, at ^ flip) for at in range(n_dev)])  16.9 us
    all_to_all x1, waiting for transfers between devices, body(): lax.all_to_all(sent_g.reshape(half_size, 2 * capacity, out_width + MARKS)...  14 us
    pallas_call x2, Pallas kernels, project(): pl.pallas_call(functools.partial(project_kernel, side, split, capacity, o...  9.28 us
    pallas_call x1, Pallas kernels, finish(): pl.pallas_call(functools.partial(finish_kernel, count, seqs, slots // n_d...  7.11 us
    pallas_call x1, Pallas kernels, score(): pl.pallas_call(functools.partial(score_kernel, count, seqs, rank_size, sl...  5.41 us
  transfers between devices with their start and end apart: 13, of which 7 were waited for; matrix products, arithmetic and copies ran while one was open for 7% of the time, Pallas kernels for 10%

profile of v5, /device:TPU:0, one launch (start us, length us, event | category | flops | bytes accessed | tf_op | source)
XLA Modules:
  0.0 193.7 jit_solution(18062182146180726254)
XLA Ops:
  0.6 2.3 %half.2.refs_0_ = bf16[64,9216]{1,0:T(8,128)(2,1)} custom-call(s32[1]{0:T(128)} %bitcast.4.which_ref, bf16[2,64,1024]{2,1,0:T(8,128)(2,1)} %up_hbm.3, bf16[2,64,8192]{2,1,0:T(8,128)(2,1)} %down_hbm.3), custom_call_target="tpu_custom_call" | custom-call | tf_op jit(solution)/shard_map/half/pallas_call | solution.py:503
  3.0 4.1 %collective-permute-start.4 = (bf16[64,9216]{1,0:T(8,128)(2,1)}, bf16[64,9216]{1,0:T(8,128)(2,1)}, u32[]{:S(2)}, u32[]{:S(2)}) collective-permute-start(bf16[64,9216]{1,0:T(8,128)(2,1)} %half.2.refs_0_), channel_id=1, source_target_pairs={{0,8},{1,9},{2,10},{3,11},{4,12},{5,13},{6,14},{7,15},{8,0},{9,1},... | collective-permute-start | bytes 3538952 | tf_op jit(solution)/shard_map/ppermute | solution.py:539
  7.8 2.5 %slots.1 = (bf16[256,128]{1,0:T(8,128)(2,1)}, bf16[256,128]{1,0:T(8,128)(2,1)}, bf16[128,128]{1,0:T(8,128)(2,1)}, bf16[256,1152]{1,0:T(8,128)(2,1)}) custom-call(s32[1]{0:T(128)} %bitcast.3.half_ref, s32[128,1]{1,0:T(8,128)} %gate.3.owner_ref, s32[1,128]{1,0:T(1,128)} %bitcast.34, s32[1,128]{1,0:T(1,128)} %segment_ref.1, bf16[128,1024]{1,0:T(8,128)(2,1)} %g_ref.3), custom_call_target="tpu_custom_call" | custom-call | tf_op jit(solution)/shard_map/slots/pallas_call | solution.py:407
  10.3 4.0 %all-to-all-start = ((bf16[8,32,1152]{2,1,0:T(8,128)(2,1)}), bf16[8,32,1152]{2,1,0:T(8,128)(2,1)S(1)}, u32[]{:S(2)}, u32[]{:S(2)}) async-start(bf16[8,32,1152]{2,1,0:T(8,128)(2,1)} %bitcast.27), calls=%async_computation | async-start | bytes 1179648 | tf_op jit(solution)/shard_map/all_to_all | solution.py:557
  14.3 2.5 %half.3.refs_1_ = bf16[64,9216]{1,0:T(8,128)(2,1)} custom-call(s32[1]{0:T(128)} %bitcast.8.which_ref, bf16[2,64,1024]{2,1,0:T(8,128)(2,1)} %up_hbm.3, bf16[2,64,8192]{2,1,0:T(8,128)(2,1)} %down_hbm.3), custom_call_target="tpu_custom_call" | custom-call | tf_op jit(solution)/shard_map/half/pallas_call | solution.py:503
  18.6 3.2 %send.1.refs_0_ = bf16[256,9344]{1,0:T(8,128)(2,1)S(1)} custom-call(bf16[256,128]{1,0:T(8,128)(2,1)S(1)} %copy-done.7, bf16[128,128]{1,0:T(8,128)(2,1)S(1)} %copy-done.8, bf16[128,1024]{1,0:T(8,128)(2,1)S(1)} %copy-done.6, bf16[128,8192]{1,0:T(8,128)(2,1)S(1)} %copy-done.3), custom_call_target="tpu_custom_call" | custom-call | flops 612368384 | bytes 7176192 | tf_op jit(solution)/shard_map/send/pallas_call | solution.py:464
  21.9 2.2 %copy-done = bf16[256,9344]{1,0:T(8,128)(2,1)} copy-done((bf16[256,9344]{1,0:T(8,128)(2,1)}, bf16[256,9344]{1,0:T(8,128)(2,1)S(1)}, u32[]{:S(2)}) %copy-start) | copy-done | bytes 4784152
  25.0 14.0 %all-to-all-done.g_ref = bf16[8,32,1152]{2,1,0:T(8,128)(2,1)S(1)} async-done(((bf16[8,32,1152]{2,1,0:T(8,128)(2,1)}), bf16[8,32,1152]{2,1,0:T(8,128)(2,1)S(1)}, u32[]{:S(2)}, u32[]{:S(2)}) %all-to-all-start) | async-done | bytes 589856 | tf_op jit(solution)/shard_map/all_to_all | solution.py:557
  39.8 4.7 %project.2 = (bf16[32,8192]{1,0:T(8,128)(2,1)}, bf16[32,8192]{1,0:T(8,128)(2,1)}, bf16[32,8192]{1,0:T(8,128)(2,1)}, bf16[32,8192]{1,0:T(8,128)(2,1)}) custom-call(s32[1]{0:T(128)} %bitcast.6.spot_ref, bf16[8,32,1152]{2,1,0:T(8,128)(2,1)} %copy-done.9, f32[2,128]{1,0:T(2,128)} %compare_convert_fusion.which.refs_0_, bf16[64,9216]{1,0:T(8,128)(2,1)} %half.2.refs_0_, ...), custom_call_target="tpu_custom_call" | custom-call | flops 1000 | bytes 1000 | tf_op jit(solution)/shard_map/project/pallas_call | solution.py:75
  44.5 1.5 collective-permute-start
  46.0 2.4 %collective-permute-start.1 = (bf16[32,8192]{1,0:T(8,128)(2,1)}, bf16[32,8192]{1,0:T(8,128)(2,1)}, u32[]{:S(2)}, u32[]{:S(2)}) collective-permute-start(bf16[32,8192]{1,0:T(8,128)(2,1)} %get-tuple-element.33), channel_id=1, source_target_pairs={{0,4},{1,5},{2,6},{3,7},{4,0},{5,1},{6,2},{7,3},{8,12},{9,13},{10,... | collective-permute-start | bytes 1572872 | tf_op jit(solution)/shard_map/ppermute | solution.py:539
  48.4 1.0 copy-done.4
  50.2 4.6 %all-to-all-start.1 = ((bf16[16,16,9344]{2,1,0:T(8,128)(2,1)}), bf16[16,16,9344]{2,1,0:T(8,128)(2,1)}, u32[]{:S(2)}, u32[]{:S(2)}) async-start(bf16[16,16,9344]{2,1,0:T(8,128)(2,1)} %bitcast.23), calls=%async_computation.1 | async-start | bytes 9568256 | tf_op jit(solution)/shard_map/all_to_all | solution.py:580
  54.7 4.0 %collective-permute-done.4.refs_0_ = bf16[64,9216]{1,0:T(8,128)(2,1)} collective-permute-done((bf16[64,9216]{1,0:T(8,128)(2,1)}, bf16[64,9216]{1,0:T(8,128)(2,1)}, u32[]{:S(2)}, u32[]{:S(2)}) %collective-permute-start.4) | collective-permute-done | bytes 1179680 | tf_op jit(solution)/shard_map/ppermute | solution.py:539
  58.8 1.5 collective-permute-start.5
  60.3 35.3 %collective-permute-done.1.refs_6_ = bf16[32,8192]{1,0:T(8,128)(2,1)} collective-permute-done((bf16[32,8192]{1,0:T(8,128)(2,1)}, bf16[32,8192]{1,0:T(8,128)(2,1)}, u32[]{:S(2)}, u32[]{:S(2)}) %collective-permute-start.1) | collective-permute-done | bytes 524320 | tf_op jit(solution)/shard_map/ppermute | solution.py:539
  95.6 5.8 %collective-permute-done.2.refs_7_ = bf16[32,8192]{1,0:T(8,128)(2,1)} collective-permute-done((bf16[32,8192]{1,0:T(8,128)(2,1)}, bf16[32,8192]{1,0:T(8,128)(2,1)}, u32[]{:S(2)}, u32[]{:S(2)}) %collective-permute-start.2) | collective-permute-done | bytes 524320 | tf_op jit(solution)/shard_map/ppermute | solution.py:539
  101.5 1.0 slice.52
  102.5 1.0 slice.53
  103.4 1.0 slice.54
  104.4 1.0 pad_maximum_fusion
  105.5 4.6 %project.3 = (bf16[64,8192]{1,0:T(8,128)(2,1)}, bf16[64,8192]{1,0:T(8,128)(2,1)}) custom-call(s32[1]{0:T(128)} %bitcast.6.spot_ref, bf16[8,32,1152]{2,1,0:T(8,128)(2,1)} %copy-done.9, f32[2,128]{1,0:T(2,128)} %gate.5.which, bf16[64,9216]{1,0:T(8,128)(2,1)} %collective-permute-done.4.refs_0_, bf16[64,9216]{1,0:T(8,128)(2,1)} %collective-permute-done.5.refs_1_), custom_call_target="tpu_custom_call" | custom-call | flops 1000 | bytes 1000 | tf_op jit(solution)/shard_map/project/pallas_call | solution.py:75
  110.6 2.0 %fusion.10 = (bf16[16,8192]{1,0:T(8,128)(2,1)S(1)}, bf16[16,8192]{1,0:T(8,128)(2,1)S(1)}, bf16[16,8192]{1,0:T(8,128)(2,1)S(1)}, bf16[16,8192]{1,0:T(8,128)(2,1)}) fusion(bf16[64,8192]{1,0:T(8,128)(2,1)} %get-tuple-element.40), kind=kLoop, calls=%fused_computation.28 | loop fusion | bytes 2097152 | tf_op jit(solution)/shard_map/slice | solution.py:596
  113.9 0.8 pad_maximum_fusion.4
  114.7 0.8 pad_maximum_fusion.3
  115.6 8.3 %collective-permute-start.8 = (bf16[32,8192]{1,0:T(8,128)(2,1)}, bf16[32,8192]{1,0:T(8,128)(2,1)}, u32[]{:S(2)}, u32[]{:S(2)}) collective-permute-start(bf16[32,8192]{1,0:T(8,128)(2,1)} %pad_maximum_fusion.3), channel_id=1, source_target_pairs={{0,4},{1,5},{2,6},{3,7},{4,0},{5,1},{6,2},{7,3},{8,12},{9,13},{10,... | collective-permute-start | bytes 1572872 | tf_op jit(solution)/shard_map/ppermute | solution.py:539
  124.7 27.9 %all-to-all-done.1 = bf16[16,16,9344]{2,1,0:T(8,128)(2,1)} async-done(((bf16[16,16,9344]{2,1,0:T(8,128)(2,1)}), bf16[16,16,9344]{2,1,0:T(8,128)(2,1)}, u32[]{:S(2)}, u32[]{:S(2)}) %all-to-all-start.1) | async-done | bytes 4784160 | tf_op jit(solution)/shard_map/all_to_all | solution.py:580
  152.6 5.4 %score.1 = (f32[16,1,256]{2,1,0:T(1,128)}, bf16[256,256]{1,0:T(8,128)(2,1)}) custom-call(f32[1,256]{1,0:T(1,128)S(1)} %fusion.3.own_ref, bf16[256,9344]{1,0:T(8,128)(2,1)} %bitcast.10.got_hbm.refs_2_, bf16[128,8192]{1,0:T(8,128)(2,1)S(1)} %bitcast.24, bf16[128,1024]{1,0:T(8,128)(2,1)S(1)} %bitcast.25), custom_call_target="tpu_custom_call" | custom-call | flops 603979776 | bytes 7077888 | tf_op jit(solution)/shard_map/score/pallas_call | solution.py:174
  158.0 22.1 %all-to-all-start.2 = ((f32[16,1,256]{2,1,0:T(1,128)}), f32[16,1,256]{2,1,0:T(1,128)S(1)}, u32[]{:S(2)}, u32[]{:S(2)}) async-start(f32[16,1,256]{2,1,0:T(1,128)} %get-tuple-element.36), calls=%async_computation.2 | async-start | bytes 32768 | tf_op jit(solution)/shard_map/all_to_all | solution.py:613
  180.1 1.1 pad_maximum_fusion.1.refs_9_
  181.2 5.4 %all-to-all-done.2.told_ref = f32[16,1,256]{2,1,0:T(1,128)S(1)} async-done(((f32[16,1,256]{2,1,0:T(1,128)}), f32[16,1,256]{2,1,0:T(1,128)S(1)}, u32[]{:S(2)}, u32[]{:S(2)}) %all-to-all-start.2) | async-done | bytes 16416 | tf_op jit(solution)/shard_map/all_to_all | solution.py:613
  186.6 7.1 %finish.1 = (f32[2]{0:T(128)}, f32[128,1]{1,0:T(8,128)}, bf16[128,1024]{1,0:T(8,128)(2,1)}, bf16[128,8192]{1,0:T(8,128)(2,1)}, bf16[128,8192]{1,0:T(8,128)(2,1)}) custom-call(s32[1]{0:T(128)} %bitcast.me_ref, f32[16,1,256]{2,1,0:T(1,128)S(1)} %all-to-all-done.2.told_ref, f32[128,128]{1,0:T(8,128)S(1)} %pad_convert_fusion.refs_0_, ...), custom_call_target="tpu_custom_call" | custom-call | flops 1073741824 | bytes 12582912 | tf_op jit(solution)/shard_map/finish/pallas_call | solution.py:347
  (71 shorter events, 7.7 us)
Async XLA Ops:
  0.6 6.5 %copy-start.13 = (s32[128,1]{0,1:T(1,128)S(1)}, s32[128,1]{0,1:T(1,128)}, u32[]{:S(2)}) copy-start(s32[128,1]{0,1:T(1,128)} %param.12) | copy-start | bytes 1540
  3.0 55.8 %collective-permute-start.4 = (bf16[64,9216]{1,0:T(8,128)(2,1)}, bf16[64,9216]{1,0:T(8,128)(2,1)}, u32[]{:S(2)}, u32[]{:S(2)}) collective-permute-start(bf16[64,9216]{1,0:T(8,128)(2,1)} %half.2.refs_0_), channel_id=1, source_target_pairs={{0,8},{1,9},{2,10},{3,11},{4,12},{5,13},{6,14},{7,15},{8,0},{9,1},... | collective-permute-start | bytes 3538952 | tf_op jit(solution)/shard_map/ppermute | solution.py:539
  10.3 6.5 %copy-start.14 = (f32[1,4]{1,0:T(1,128)S(1)}, f32[1,4]{1,0:T(1,128)}, u32[]{:S(2)}) copy-start(f32[1,4]{1,0:T(1,128)} %param.16) | copy-start | bytes 52
  10.3 6.7 %copy-start.15 = (s32[1,4]{1,0:T(1,128)S(1)}, s32[1,4]{1,0:T(1,128)}, u32[]{:S(2)}) copy-start(s32[1,4]{1,0:T(1,128)} %param.15) | copy-start | bytes 52
  10.3 7.0 %copy-start.16 = (s32[8]{0:T(128)S(1)}, s32[8]{0:T(128)}, u32[]{:S(2)}) copy-start(s32[8]{0:T(128)} %constant.50.clone) | copy-start | bytes 100
  10.3 7.0 %copy-start.11 = (bf16[256,128]{1,0:T(8,128)(2,1)S(1)}, bf16[256,128]{1,0:T(8,128)(2,1)}, u32[]{:S(2)}) copy-start(bf16[256,128]{1,0:T(8,128)(2,1)} %get-tuple-element.38) | copy-start | bytes 196612
  10.3 28.7 %all-to-all-start = ((bf16[8,32,1152]{2,1,0:T(8,128)(2,1)}), bf16[8,32,1152]{2,1,0:T(8,128)(2,1)S(1)}, u32[]{:S(2)}, u32[]{:S(2)}) async-start(bf16[8,32,1152]{2,1,0:T(8,128)(2,1)} %bitcast.27), calls=%async_computation | async-start | bytes 1179648 | tf_op jit(solution)/shard_map/all_to_all | solution.py:557
  14.3 4.3 %copy-start.3 = (bf16[128,8192]{1,0:T(8,128)(2,1)S(1)}, bf16[128,8192]{1,0:T(8,128)(2,1)}, u32[]{:S(2)}) copy-start(bf16[128,8192]{1,0:T(8,128)(2,1)} %tokens_hbm.1) | copy-start | bytes 6291460
  14.3 4.3 %copy-start.6 = (bf16[128,1024]{1,0:T(8,128)(2,1)S(1)}, bf16[128,1024]{1,0:T(8,128)(2,1)}, u32[]{:S(2)}) copy-start(bf16[128,1024]{1,0:T(8,128)(2,1)} %g_ref.3) | copy-start | bytes 786436
  14.3 4.3 %copy-start.7 = (bf16[256,128]{1,0:T(8,128)(2,1)S(1)}, bf16[256,128]{1,0:T(8,128)(2,1)}, u32[]{:S(2)}) copy-start(bf16[256,128]{1,0:T(8,128)(2,1)} %get-tuple-element.28.to_slot) | copy-start | bytes 196612
  14.3 4.3 %copy-start.8 = (bf16[128,128]{1,0:T(8,128)(2,1)S(1)}, bf16[128,128]{1,0:T(8,128)(2,1)}, u32[]{:S(2)}) copy-start(bf16[128,128]{1,0:T(8,128)(2,1)} %get-tuple-element.29.marks) | copy-start | bytes 98308
  18.6 5.5 %copy-start.12 = (s32[1,128]{1,0:T(1,128)S(1)}, s32[1,128]{1,0:T(1,128)}, u32[]{:S(2)}) copy-start(s32[1,128]{1,0:T(1,128)} %segment_ref.1) | copy-start | bytes 1540
  21.9 2.2 %copy-start = (bf16[256,9344]{1,0:T(8,128)(2,1)}, bf16[256,9344]{1,0:T(8,128)(2,1)S(1)}, u32[]{:S(2)}) copy-start(bf16[256,9344]{1,0:T(8,128)(2,1)S(1)} %send.1.refs_0_) | copy-start | bytes 14352388
  39.0 0.8 copy-start.9
  44.5 15.8 %collective-permute-start = (bf16[32,8192]{1,0:T(8,128)(2,1)}, bf16[32,8192]{1,0:T(8,128)(2,1)}, u32[]{:S(2)}, u32[]{:S(2)}) collective-permute-start(bf16[32,8192]{1,0:T(8,128)(2,1)} %get-tuple-element.32), channel_id=1, source_target_pairs={{0,2},{1,3},{2,0},{3,1},{4,6},{5,7},{6,4},{7,5},{8,10},{9,11},{10,... | collective-permute-start | bytes 1572872 | tf_op jit(solution)/shard_map/ppermute | solution.py:539
  46.0 49.6 %collective-permute-start.1 = (bf16[32,8192]{1,0:T(8,128)(2,1)}, bf16[32,8192]{1,0:T(8,128)(2,1)}, u32[]{:S(2)}, u32[]{:S(2)}) collective-permute-start(bf16[32,8192]{1,0:T(8,128)(2,1)} %get-tuple-element.33), channel_id=1, source_target_pairs={{0,4},{1,5},{2,6},{3,7},{4,0},{5,1},{6,2},{7,3},{8,12},{9,13},{10,... | collective-permute-start | bytes 1572872 | tf_op jit(solution)/shard_map/ppermute | solution.py:539
  48.4 53.1 %collective-permute-start.2 = (bf16[32,8192]{1,0:T(8,128)(2,1)}, bf16[32,8192]{1,0:T(8,128)(2,1)}, u32[]{:S(2)}, u32[]{:S(2)}) collective-permute-start(bf16[32,8192]{1,0:T(8,128)(2,1)} %get-tuple-element.34), channel_id=1, source_target_pairs={{0,6},{1,7},{2,4},{3,5},{4,2},{5,3},{6,0},{7,1},{8,14},{9,15},{10,... | collective-permute-start | bytes 1572872 | tf_op jit(solution)/shard_map/ppermute | solution.py:539
  48.4 1.0 copy-start.4
  50.2 102.5 %all-to-all-start.1 = ((bf16[16,16,9344]{2,1,0:T(8,128)(2,1)}), bf16[16,16,9344]{2,1,0:T(8,128)(2,1)}, u32[]{:S(2)}, u32[]{:S(2)}) async-start(bf16[16,16,9344]{2,1,0:T(8,128)(2,1)} %bitcast.23), calls=%async_computation.1 | async-start | bytes 9568256 | tf_op jit(solution)/shard_map/all_to_all | solution.py:580
  58.8 46.7 %collective-permute-start.5 = (bf16[64,9216]{1,0:T(8,128)(2,1)}, bf16[64,9216]{1,0:T(8,128)(2,1)}, u32[]{:S(2)}, u32[]{:S(2)}) collective-permute-start(bf16[64,9216]{1,0:T(8,128)(2,1)} %collective-permute-done.4.refs_0_), channel_id=1, source_target_pairs={{0,16},{16,0},{1,17},{17,1},{2,18},{18,2},{3,19},{19,3},{4,20},{20... | collective-permute-start | bytes 3538952 | tf_op jit(solution)/shard_map/ppermute | solution.py:542
  101.4 3.0 %copy-start.10 = (bf16[16,8192]{1,0:T(8,128)(2,1)S(1)}, bf16[16,8192]{1,0:T(8,128)(2,1)}, u32[]{:S(2)}) copy-start(bf16[16,8192]{1,0:T(8,128)(2,1)} %slice.36) | copy-start | bytes 786436
  105.5 81.1 %collective-permute-start.3 = (bf16[64,8192]{1,0:T(8,128)(2,1)}, bf16[64,8192]{1,0:T(8,128)(2,1)}, u32[]{:S(2)}, u32[]{:S(2)}) collective-permute-start(bf16[64,8192]{1,0:T(8,128)(2,1)} %pad_maximum_fusion), channel_id=1, source_target_pairs={{0,1},{1,0},{2,3},{3,2},{4,5},{5,4},{6,7},{7,6},{8,9},{9,8},{10,11... | collective-permute-start | bytes 3145736 | tf_op jit(solution)/shard_map/ppermute | solution.py:539
  110.1 3.0 %collective-permute-start.6 = (bf16[64,8192]{1,0:T(8,128)(2,1)}, bf16[64,8192]{1,0:T(8,128)(2,1)S(1)}, u32[]{:S(2)}, u32[]{:S(2)}) collective-permute-start(bf16[64,8192]{1,0:T(8,128)(2,1)} %get-tuple-element.41), channel_id=1, source_target_pairs={{0,1},{1,0},{2,3},{3,2},{4,5},{5,4},{6,7},{7,6},{8,9},{9,8},{10,11... | collective-permute-start | bytes 3145736 | tf_op jit(solution)/shard_map/ppermute | solution.py:539
  113.9 38.8 %copy-start.1 = (bf16[2,64,8192]{2,1,0:T(8,128)(2,1)S(1)}, bf16[2,64,8192]{2,1,0:T(8,128)(2,1)}, u32[]{:S(2)}) copy-start(bf16[2,64,8192]{2,1,0:T(8,128)(2,1)} %down_hbm.3) | copy-start | bytes 6291460
  113.9 38.8 %copy-start.2 = (bf16[2,64,1024]{2,1,0:T(8,128)(2,1)S(1)}, bf16[2,64,1024]{2,1,0:T(8,128)(2,1)}, u32[]{:S(2)}) copy-start(bf16[2,64,1024]{2,1,0:T(8,128)(2,1)} %up_hbm.3) | copy-start | bytes 786436
  114.7 66.5 %collective-permute-start.9 = (bf16[32,8192]{1,0:T(8,128)(2,1)}, bf16[32,8192]{1,0:T(8,128)(2,1)S(1)}, u32[]{:S(2)}, u32[]{:S(2)}) collective-permute-start(bf16[32,8192]{1,0:T(8,128)(2,1)} %pad_maximum_fusion.4), channel_id=1, source_target_pairs={{0,6},{1,7},{2,4},{3,5},{4,2},{5,3},{6,0},{7,1},{8,14},{9,15},{10,... | collective-permute-start | bytes 1572872 | tf_op jit(solution)/shard_map/ppermute | solution.py:539
  115.6 65.6 %collective-permute-start.8 = (bf16[32,8192]{1,0:T(8,128)(2,1)}, bf16[32,8192]{1,0:T(8,128)(2,1)}, u32[]{:S(2)}, u32[]{:S(2)}) collective-permute-start(bf16[32,8192]{1,0:T(8,128)(2,1)} %pad_maximum_fusion.3), channel_id=1, source_target_pairs={{0,4},{1,5},{2,6},{3,7},{4,0},{5,1},{6,2},{7,3},{8,12},{9,13},{10,... | collective-permute-start | bytes 1572872 | tf_op jit(solution)/shard_map/ppermute | solution.py:539
  124.7 56.5 %collective-permute-start.7 = (bf16[32,8192]{1,0:T(8,128)(2,1)}, bf16[32,8192]{1,0:T(8,128)(2,1)}, u32[]{:S(2)}, u32[]{:S(2)}) collective-permute-start(bf16[32,8192]{1,0:T(8,128)(2,1)} %pad_maximum_fusion.2), channel_id=1, source_target_pairs={{0,2},{1,3},{2,0},{3,1},{4,6},{5,7},{6,4},{7,5},{8,10},{9,11},{10,... | collective-permute-start | bytes 1572872 | tf_op jit(solution)/shard_map/ppermute | solution.py:539
  152.6 34.0 %copy-start.5 = (bf16[32,8192]{1,0:T(8,128)(2,1)S(1)}, bf16[32,8192]{1,0:T(8,128)(2,1)}, u32[]{:S(2)}) copy-start(bf16[32,8192]{1,0:T(8,128)(2,1)} %get-tuple-element.31.refs_4_) | copy-start | bytes 1572868
  158.0 28.6 %all-to-all-start.2 = ((f32[16,1,256]{2,1,0:T(1,128)}), f32[16,1,256]{2,1,0:T(1,128)S(1)}, u32[]{:S(2)}, u32[]{:S(2)}) async-start(f32[16,1,256]{2,1,0:T(1,128)} %get-tuple-element.36), calls=%async_computation.2 | async-start | bytes 32768 | tf_op jit(solution)/shard_map/all_to_all | solution.py:613

commit v6 on v5

--- a/solution.py
+++ b/solution.py
@@ -117,7 +117,7 @@
 ):
     told_ref, rows_hbm, got, rank_rows, got_sems, rows_sem = refs
     width, out_width = down.shape[1], up.shape[1]
-    parts = column_parts(width, columns)
+    parts = column_parts(width, 4 * columns)
     tail = slice(width, got.shape[1])
     copies = []
     for at, part in enumerate(parts):
@@ -169,7 +169,7 @@
     slots = got.shape[0]
     lanes, width = down.shape
     columns = up.shape[1]
-    n_parts = len(column_parts(width, columns))
+    n_parts = len(column_parts(width, 4 * columns))
     vmem, hbm = pl.BlockSpec(memory_space=pltpu.VMEM), pl.BlockSpec(memory_space=pl.ANY)
     return pl.pallas_call(
         functools.partial(score_kernel, count, seqs, rank_size, slots // n_dev, columns),
@@ -229,7 +229,7 @@
     else:
         rank_rows, got, grad_up, grad_down, rank_sem, got_sems, up_sem, down_sems = refs
     width, out_width = grad_down.shape[1], grad_up.shape[1]
-    parts = column_parts(width, columns)
+    parts = column_parts(width, 2 * columns)
     tail = slice(width, got.shape[1])
     tail_copy = pltpu.make_async_copy(got_hbm.at[:, tail], got.at[:, tail], got_sems.at[len(parts)])
     copies = [
@@ -318,7 +318,7 @@
     rows = row_marks.shape[0]
     n_dev = told.shape[0]
     columns = got.shape[1] - width - MARKS
-    n_parts = len(column_parts(width, columns))
+    n_parts = len(column_parts(width, 2 * columns))
     together = not any(size % 16 for size in used)
     vmem, hbm = pl.BlockSpec(memory_space=pltpu.VMEM), pl.BlockSpec(memory_space=pltpu.HBM)
     sems = pltpu.SemaphoreType.DMA

time: 194 us -> 193 us (level)
  no operation moved by 1% of the time
where the time goes in v6:
time: 193 us
  waiting for transfers between devices  92.9 us (48%)
  starting transfers between devices  49 us (25%)
  Pallas kernels  31.4 us (16%)
  local copies, waits for them, and re-layouts  12.8 us (7%)
  other arithmetic  5.76 us (3%)
    ppermute x9, waiting for transfers between devices, flipped(): return lax.ppermute(block, 'ad', [(at, at ^ flip) for at in range(n_dev)])  45.7 us
    all_to_all x1, waiting for transfers between devices, body(): lax.all_to_all(sent.reshape(n_dev, capacity, width + out_width + MARKS),...  27.9 us
    all_to_all x1, starting transfers between devices, body(): told = lax.all_to_all(part, 'ad', split_axis=0, concat_axis=0, tiled=True)  22.1 us
    ppermute x9, starting transfers between devices, flipped(): return lax.ppermute(block, 'ad', [(at, at ^ flip) for at in range(n_dev)])  16.9 us
    all_to_all x1, waiting for transfers between devices, body(): lax.all_to_all(sent_g.reshape(half_size, 2 * capacity, out_width + MARKS)...  14 us
    pallas_call x2, Pallas kernels, project(): pl.pallas_call(functools.partial(project_kernel, side, split, capacity, o...  9.28 us
    pallas_call x1, Pallas kernels, finish(): pl.pallas_call(functools.partial(finish_kernel, count, seqs, slots // n_d...  6.42 us
    all_to_all x1, waiting for transfers between devices, body(): told = lax.all_to_all(part, 'ad', split_axis=0, concat_axis=0, tiled=True)  5.4 us
  transfers between devices with their start and end apart: 13, of which 7 were waited for; matrix products, arithmetic and copies ran while one was open for 7% of the time, Pallas kernels for 10%

profile of v6, /device:TPU:0, one launch (start us, length us, event | category | flops | bytes accessed | tf_op | source)
XLA Modules:
  0.0 192.8 jit_solution(7986945095795015287)
XLA Ops:
  0.6 2.3 %half.2.refs_0_ = bf16[64,9216]{1,0:T(8,128)(2,1)} custom-call(s32[1]{0:T(128)} %bitcast.4.which_ref, bf16[2,64,1024]{2,1,0:T(8,128)(2,1)} %up_hbm.3, bf16[2,64,8192]{2,1,0:T(8,128)(2,1)} %down_hbm.3), custom_call_target="tpu_custom_call" | custom-call | tf_op jit(solution)/shard_map/half/pallas_call | solution.py:503
  3.0 4.1 %collective-permute-start.4 = (bf16[64,9216]{1,0:T(8,128)(2,1)}, bf16[64,9216]{1,0:T(8,128)(2,1)}, u32[]{:S(2)}, u32[]{:S(2)}) collective-permute-start(bf16[64,9216]{1,0:T(8,128)(2,1)} %half.2.refs_0_), channel_id=1, source_target_pairs={{0,8},{1,9},{2,10},{3,11},{4,12},{5,13},{6,14},{7,15},{8,0},{9,1},... | collective-permute-start | bytes 3538952 | tf_op jit(solution)/shard_map/ppermute | solution.py:539
  7.8 2.5 %slots.1 = (bf16[256,128]{1,0:T(8,128)(2,1)}, bf16[256,128]{1,0:T(8,128)(2,1)}, bf16[128,128]{1,0:T(8,128)(2,1)}, bf16[256,1152]{1,0:T(8,128)(2,1)}) custom-call(s32[1]{0:T(128)} %bitcast.3.half_ref, s32[128,1]{1,0:T(8,128)} %gate.3.owner_ref, s32[1,128]{1,0:T(1,128)} %bitcast.34, s32[1,128]{1,0:T(1,128)} %segment_ref.1, bf16[128,1024]{1,0:T(8,128)(2,1)} %g_ref.3), custom_call_target="tpu_custom_call" | custom-call | tf_op jit(solution)/shard_map/slots/pallas_call | solution.py:407
  10.3 4.0 %all-to-all-start = ((bf16[8,32,1152]{2,1,0:T(8,128)(2,1)}), bf16[8,32,1152]{2,1,0:T(8,128)(2,1)S(1)}, u32[]{:S(2)}, u32[]{:S(2)}) async-start(bf16[8,32,1152]{2,1,0:T(8,128)(2,1)} %bitcast.27), calls=%async_computation | async-start | bytes 1179648 | tf_op jit(solution)/shard_map/all_to_all | solution.py:557
  14.3 2.5 %half.3.refs_1_ = bf16[64,9216]{1,0:T(8,128)(2,1)} custom-call(s32[1]{0:T(128)} %bitcast.8.which_ref, bf16[2,64,1024]{2,1,0:T(8,128)(2,1)} %up_hbm.3, bf16[2,64,8192]{2,1,0:T(8,128)(2,1)} %down_hbm.3), custom_call_target="tpu_custom_call" | custom-call | tf_op jit(solution)/shard_map/half/pallas_call | solution.py:503
  18.6 3.2 %send.1.refs_0_ = bf16[256,9344]{1,0:T(8,128)(2,1)S(1)} custom-call(bf16[256,128]{1,0:T(8,128)(2,1)S(1)} %copy-done.7, bf16[128,128]{1,0:T(8,128)(2,1)S(1)} %copy-done.8, bf16[128,1024]{1,0:T(8,128)(2,1)S(1)} %copy-done.6, bf16[128,8192]{1,0:T(8,128)(2,1)S(1)} %copy-done.3), custom_call_target="tpu_custom_call" | custom-call | flops 612368384 | bytes 7176192 | tf_op jit(solution)/shard_map/send/pallas_call | solution.py:464
  21.9 2.2 %copy-done = bf16[256,9344]{1,0:T(8,128)(2,1)} copy-done((bf16[256,9344]{1,0:T(8,128)(2,1)}, bf16[256,9344]{1,0:T(8,128)(2,1)S(1)}, u32[]{:S(2)}) %copy-start) | copy-done | bytes 4784152
  25.0 14.0 %all-to-all-done.g_ref = bf16[8,32,1152]{2,1,0:T(8,128)(2,1)S(1)} async-done(((bf16[8,32,1152]{2,1,0:T(8,128)(2,1)}), bf16[8,32,1152]{2,1,0:T(8,128)(2,1)S(1)}, u32[]{:S(2)}, u32[]{:S(2)}) %all-to-all-start) | async-done | bytes 589856 | tf_op jit(solution)/shard_map/all_to_all | solution.py:557
  39.8 4.7 %project.2 = (bf16[32,8192]{1,0:T(8,128)(2,1)}, bf16[32,8192]{1,0:T(8,128)(2,1)}, bf16[32,8192]{1,0:T(8,128)(2,1)}, bf16[32,8192]{1,0:T(8,128)(2,1)}) custom-call(s32[1]{0:T(128)} %bitcast.6.spot_ref, bf16[8,32,1152]{2,1,0:T(8,128)(2,1)} %copy-done.9, f32[2,128]{1,0:T(2,128)} %compare_convert_fusion.which.refs_0_, bf16[64,9216]{1,0:T(8,128)(2,1)} %half.2.refs_0_, ...), custom_call_target="tpu_custom_call" | custom-call | flops 1000 | bytes 1000 | tf_op jit(solution)/shard_map/project/pallas_call | solution.py:75
  44.5 1.5 collective-permute-start
  46.0 2.4 %collective-permute-start.1 = (bf16[32,8192]{1,0:T(8,128)(2,1)}, bf16[32,8192]{1,0:T(8,128)(2,1)}, u32[]{:S(2)}, u32[]{:S(2)}) collective-permute-start(bf16[32,8192]{1,0:T(8,128)(2,1)} %get-tuple-element.33), channel_id=1, source_target_pairs={{0,4},{1,5},{2,6},{3,7},{4,0},{5,1},{6,2},{7,3},{8,12},{9,13},{10,... | collective-permute-start | bytes 1572872 | tf_op jit(solution)/shard_map/ppermute | solution.py:539
  48.4 1.0 copy-done.4
  50.2 4.6 %all-to-all-start.1 = ((bf16[16,16,9344]{2,1,0:T(8,128)(2,1)}), bf16[16,16,9344]{2,1,0:T(8,128)(2,1)}, u32[]{:S(2)}, u32[]{:S(2)}) async-start(bf16[16,16,9344]{2,1,0:T(8,128)(2,1)} %bitcast.23), calls=%async_computation.1 | async-start | bytes 9568256 | tf_op jit(solution)/shard_map/all_to_all | solution.py:580
  54.7 4.0 %collective-permute-done.4.refs_0_ = bf16[64,9216]{1,0:T(8,128)(2,1)} collective-permute-done((bf16[64,9216]{1,0:T(8,128)(2,1)}, bf16[64,9216]{1,0:T(8,128)(2,1)}, u32[]{:S(2)}, u32[]{:S(2)}) %collective-permute-start.4) | collective-permute-done | bytes 1179680 | tf_op jit(solution)/shard_map/ppermute | solution.py:539
  58.8 1.5 collective-permute-start.5
  60.3 35.3 %collective-permute-done.1.refs_6_ = bf16[32,8192]{1,0:T(8,128)(2,1)} collective-permute-done((bf16[32,8192]{1,0:T(8,128)(2,1)}, bf16[32,8192]{1,0:T(8,128)(2,1)}, u32[]{:S(2)}, u32[]{:S(2)}) %collective-permute-start.1) | collective-permute-done | bytes 524320 | tf_op jit(solution)/shard_map/ppermute | solution.py:539
  95.6 5.8 %collective-permute-done.2.refs_7_ = bf16[32,8192]{1,0:T(8,128)(2,1)} collective-permute-done((bf16[32,8192]{1,0:T(8,128)(2,1)}, bf16[32,8192]{1,0:T(8,128)(2,1)}, u32[]{:S(2)}, u32[]{:S(2)}) %collective-permute-start.2) | collective-permute-done | bytes 524320 | tf_op jit(solution)/shard_map/ppermute | solution.py:539
  101.5 1.0 slice.52
  102.5 1.0 slice.53
  103.4 1.0 slice.54
  104.4 1.0 pad_maximum_fusion
  105.5 4.6 %project.3 = (bf16[64,8192]{1,0:T(8,128)(2,1)}, bf16[64,8192]{1,0:T(8,128)(2,1)}) custom-call(s32[1]{0:T(128)} %bitcast.6.spot_ref, bf16[8,32,1152]{2,1,0:T(8,128)(2,1)} %copy-done.9, f32[2,128]{1,0:T(2,128)} %gate.5.which, bf16[64,9216]{1,0:T(8,128)(2,1)} %collective-permute-done.4.refs_0_, bf16[64,9216]{1,0:T(8,128)(2,1)} %collective-permute-done.5.refs_1_), custom_call_target="tpu_custom_call" | custom-call | flops 1000 | bytes 1000 | tf_op jit(solution)/shard_map/project/pallas_call | solution.py:75
  110.6 2.0 %fusion.10 = (bf16[16,8192]{1,0:T(8,128)(2,1)S(1)}, bf16[16,8192]{1,0:T(8,128)(2,1)S(1)}, bf16[16,8192]{1,0:T(8,128)(2,1)S(1)}, bf16[16,8192]{1,0:T(8,128)(2,1)}) fusion(bf16[64,8192]{1,0:T(8,128)(2,1)} %get-tuple-element.40), kind=kLoop, calls=%fused_computation.28 | loop fusion | bytes 2097152 | tf_op jit(solution)/shard_map/slice | solution.py:596
  113.9 0.8 pad_maximum_fusion.4
  114.7 0.8 pad_maximum_fusion.3
  115.6 8.3 %collective-permute-start.8 = (bf16[32,8192]{1,0:T(8,128)(2,1)}, bf16[32,8192]{1,0:T(8,128)(2,1)}, u32[]{:S(2)}, u32[]{:S(2)}) collective-permute-start(bf16[32,8192]{1,0:T(8,128)(2,1)} %pad_maximum_fusion.3), channel_id=1, source_target_pairs={{0,4},{1,5},{2,6},{3,7},{4,0},{5,1},{6,2},{7,3},{8,12},{9,13},{10,... | collective-permute-start | bytes 1572872 | tf_op jit(solution)/shard_map/ppermute | solution.py:539
  124.7 27.9 %all-to-all-done.1 = bf16[16,16,9344]{2,1,0:T(8,128)(2,1)} async-done(((bf16[16,16,9344]{2,1,0:T(8,128)(2,1)}), bf16[16,16,9344]{2,1,0:T(8,128)(2,1)}, u32[]{:S(2)}, u32[]{:S(2)}) %all-to-all-start.1) | async-done | bytes 4784160 | tf_op jit(solution)/shard_map/all_to_all | solution.py:580
  152.6 5.2 %score.1 = (f32[16,1,256]{2,1,0:T(1,128)}, bf16[256,256]{1,0:T(8,128)(2,1)}) custom-call(f32[1,256]{1,0:T(1,128)S(1)} %fusion.3.own_ref, bf16[256,9344]{1,0:T(8,128)(2,1)} %bitcast.10.got_hbm.refs_2_, bf16[128,8192]{1,0:T(8,128)(2,1)S(1)} %bitcast.24, bf16[128,1024]{1,0:T(8,128)(2,1)S(1)} %bitcast.25), custom_call_target="tpu_custom_call" | custom-call | flops 603979776 | bytes 7077888 | tf_op jit(solution)/shard_map/score/pallas_call | solution.py:174
  157.8 22.1 %all-to-all-start.2 = ((f32[16,1,256]{2,1,0:T(1,128)}), f32[16,1,256]{2,1,0:T(1,128)S(1)}, u32[]{:S(2)}, u32[]{:S(2)}) async-start(f32[16,1,256]{2,1,0:T(1,128)} %get-tuple-element.36), calls=%async_computation.2 | async-start | bytes 32768 | tf_op jit(solution)/shard_map/all_to_all | solution.py:613
  179.9 1.1 pad_maximum_fusion.1.refs_9_
  181.0 5.4 %all-to-all-done.2.told_ref = f32[16,1,256]{2,1,0:T(1,128)S(1)} async-done(((f32[16,1,256]{2,1,0:T(1,128)}), f32[16,1,256]{2,1,0:T(1,128)S(1)}, u32[]{:S(2)}, u32[]{:S(2)}) %all-to-all-start.2) | async-done | bytes 16416 | tf_op jit(solution)/shard_map/all_to_all | solution.py:613
  186.4 6.4 %finish.1 = (f32[2]{0:T(128)}, f32[128,1]{1,0:T(8,128)}, bf16[128,1024]{1,0:T(8,128)(2,1)}, bf16[128,8192]{1,0:T(8,128)(2,1)}, bf16[128,8192]{1,0:T(8,128)(2,1)}) custom-call(s32[1]{0:T(128)} %bitcast.me_ref, f32[16,1,256]{2,1,0:T(1,128)S(1)} %all-to-all-done.2.told_ref, f32[128,128]{1,0:T(8,128)S(1)} %pad_convert_fusion.refs_0_, ...), custom_call_target="tpu_custom_call" | custom-call | flops 1073741824 | bytes 12582912 | tf_op jit(solution)/shard_map/finish/pallas_call | solution.py:347
  (71 shorter events, 7.7 us)
Async XLA Ops:
  0.6 6.5 %copy-start.13 = (s32[128,1]{0,1:T(1,128)S(1)}, s32[128,1]{0,1:T(1,128)}, u32[]{:S(2)}) copy-start(s32[128,1]{0,1:T(1,128)} %param.12) | copy-start | bytes 1540
  3.0 55.8 %collective-permute-start.4 = (bf16[64,9216]{1,0:T(8,128)(2,1)}, bf16[64,9216]{1,0:T(8,128)(2,1)}, u32[]{:S(2)}, u32[]{:S(2)}) collective-permute-start(bf16[64,9216]{1,0:T(8,128)(2,1)} %half.2.refs_0_), channel_id=1, source_target_pairs={{0,8},{1,9},{2,10},{3,11},{4,12},{5,13},{6,14},{7,15},{8,0},{9,1},... | collective-permute-start | bytes 3538952 | tf_op jit(solution)/shard_map/ppermute | solution.py:539
  10.3 6.5 %copy-start.14 = (f32[1,4]{1,0:T(1,128)S(1)}, f32[1,4]{1,0:T(1,128)}, u32[]{:S(2)}) copy-start(f32[1,4]{1,0:T(1,128)} %param.16) | copy-start | bytes 52
  10.3 6.7 %copy-start.15 = (s32[1,4]{1,0:T(1,128)S(1)}, s32[1,4]{1,0:T(1,128)}, u32[]{:S(2)}) copy-start(s32[1,4]{1,0:T(1,128)} %param.15) | copy-start | bytes 52
  10.3 7.0 %copy-start.16 = (s32[8]{0:T(128)S(1)}, s32[8]{0:T(128)}, u32[]{:S(2)}) copy-start(s32[8]{0:T(128)} %constant.50.clone) | copy-start | bytes 100
  10.3 7.0 %copy-start.11 = (bf16[256,128]{1,0:T(8,128)(2,1)S(1)}, bf16[256,128]{1,0:T(8,128)(2,1)}, u32[]{:S(2)}) copy-start(bf16[256,128]{1,0:T(8,128)(2,1)} %get-tuple-element.38) | copy-start | bytes 196612
  10.3 28.7 %all-to-all-start = ((bf16[8,32,1152]{2,1,0:T(8,128)(2,1)}), bf16[8,32,1152]{2,1,0:T(8,128)(2,1)S(1)}, u32[]{:S(2)}, u32[]{:S(2)}) async-start(bf16[8,32,1152]{2,1,0:T(8,128)(2,1)} %bitcast.27), calls=%async_computation | async-start | bytes 1179648 | tf_op jit(solution)/shard_map/all_to_all | solution.py:557
  14.3 4.3 %copy-start.3 = (bf16[128,8192]{1,0:T(8,128)(2,1)S(1)}, bf16[128,8192]{1,0:T(8,128)(2,1)}, u32[]{:S(2)}) copy-start(bf16[128,8192]{1,0:T(8,128)(2,1)} %tokens_hbm.1) | copy-start | bytes 6291460
  14.3 4.3 %copy-start.6 = (bf16[128,1024]{1,0:T(8,128)(2,1)S(1)}, bf16[128,1024]{1,0:T(8,128)(2,1)}, u32[]{:S(2)}) copy-start(bf16[128,1024]{1,0:T(8,128)(2,1)} %g_ref.3) | copy-start | bytes 786436
  14.3 4.3 %copy-start.7 = (bf16[256,128]{1,0:T(8,128)(2,1)S(1)}, bf16[256,128]{1,0:T(8,128)(2,1)}, u32[]{:S(2)}) copy-start(bf16[256,128]{1,0:T(8,128)(2,1)} %get-tuple-element.28.to_slot) | copy-start | bytes 196612
  14.3 4.3 %copy-start.8 = (bf16[128,128]{1,0:T(8,128)(2,1)S(1)}, bf16[128,128]{1,0:T(8,128)(2,1)}, u32[]{:S(2)}) copy-start(bf16[128,128]{1,0:T(8,128)(2,1)} %get-tuple-element.29.marks) | copy-start | bytes 98308
  18.6 5.5 %copy-start.12 = (s32[1,128]{1,0:T(1,128)S(1)}, s32[1,128]{1,0:T(1,128)}, u32[]{:S(2)}) copy-start(s32[1,128]{1,0:T(1,128)} %segment_ref.1) | copy-start | bytes 1540
  21.9 2.2 %copy-start = (bf16[256,9344]{1,0:T(8,128)(2,1)}, bf16[256,9344]{1,0:T(8,128)(2,1)S(1)}, u32[]{:S(2)}) copy-start(bf16[256,9344]{1,0:T(8,128)(2,1)S(1)} %send.1.refs_0_) | copy-start | bytes 14352388
  39.0 0.8 copy-start.9
  44.5 15.8 %collective-permute-start = (bf16[32,8192]{1,0:T(8,128)(2,1)}, bf16[32,8192]{1,0:T(8,128)(2,1)}, u32[]{:S(2)}, u32[]{:S(2)}) collective-permute-start(bf16[32,8192]{1,0:T(8,128)(2,1)} %get-tuple-element.32), channel_id=1, source_target_pairs={{0,2},{1,3},{2,0},{3,1},{4,6},{5,7},{6,4},{7,5},{8,10},{9,11},{10,... | collective-permute-start | bytes 1572872 | tf_op jit(solution)/shard_map/ppermute | solution.py:539
  46.0 49.6 %collective-permute-start.1 = (bf16[32,8192]{1,0:T(8,128)(2,1)}, bf16[32,8192]{1,0:T(8,128)(2,1)}, u32[]{:S(2)}, u32[]{:S(2)}) collective-permute-start(bf16[32,8192]{1,0:T(8,128)(2,1)} %get-tuple-element.33), channel_id=1, source_target_pairs={{0,4},{1,5},{2,6},{3,7},{4,0},{5,1},{6,2},{7,3},{8,12},{9,13},{10,... | collective-permute-start | bytes 1572872 | tf_op jit(solution)/shard_map/ppermute | solution.py:539
  48.4 53.1 %collective-permute-start.2 = (bf16[32,8192]{1,0:T(8,128)(2,1)}, bf16[32,8192]{1,0:T(8,128)(2,1)}, u32[]{:S(2)}, u32[]{:S(2)}) collective-permute-start(bf16[32,8192]{1,0:T(8,128)(2,1)} %get-tuple-element.34), channel_id=1, source_target_pairs={{0,6},{1,7},{2,4},{3,5},{4,2},{5,3},{6,0},{7,1},{8,14},{9,15},{10,... | collective-permute-start | bytes 1572872 | tf_op jit(solution)/shard_map/ppermute | solution.py:539
  48.4 1.0 copy-start.4
  50.2 102.5 %all-to-all-start.1 = ((bf16[16,16,9344]{2,1,0:T(8,128)(2,1)}), bf16[16,16,9344]{2,1,0:T(8,128)(2,1)}, u32[]{:S(2)}, u32[]{:S(2)}) async-start(bf16[16,16,9344]{2,1,0:T(8,128)(2,1)} %bitcast.23), calls=%async_computation.1 | async-start | bytes 9568256 | tf_op jit(solution)/shard_map/all_to_all | solution.py:580
  58.8 46.7 %collective-permute-start.5 = (bf16[64,9216]{1,0:T(8,128)(2,1)}, bf16[64,9216]{1,0:T(8,128)(2,1)}, u32[]{:S(2)}, u32[]{:S(2)}) collective-permute-start(bf16[64,9216]{1,0:T(8,128)(2,1)} %collective-permute-done.4.refs_0_), channel_id=1, source_target_pairs={{0,16},{16,0},{1,17},{17,1},{2,18},{18,2},{3,19},{19,3},{4,20},{20... | collective-permute-start | bytes 3538952 | tf_op jit(solution)/shard_map/ppermute | solution.py:542
  101.4 3.0 %copy-start.10 = (bf16[16,8192]{1,0:T(8,128)(2,1)S(1)}, bf16[16,8192]{1,0:T(8,128)(2,1)}, u32[]{:S(2)}) copy-start(bf16[16,8192]{1,0:T(8,128)(2,1)} %slice.36) | copy-start | bytes 786436
  105.5 80.9 %collective-permute-start.3 = (bf16[64,8192]{1,0:T(8,128)(2,1)}, bf16[64,8192]{1,0:T(8,128)(2,1)}, u32[]{:S(2)}, u32[]{:S(2)}) collective-permute-start(bf16[64,8192]{1,0:T(8,128)(2,1)} %pad_maximum_fusion), channel_id=1, source_target_pairs={{0,1},{1,0},{2,3},{3,2},{4,5},{5,4},{6,7},{7,6},{8,9},{9,8},{10,11... | collective-permute-start | bytes 3145736 | tf_op jit(solution)/shard_map/ppermute | solution.py:539
  110.1 3.0 %collective-permute-start.6 = (bf16[64,8192]{1,0:T(8,128)(2,1)}, bf16[64,8192]{1,0:T(8,128)(2,1)S(1)}, u32[]{:S(2)}, u32[]{:S(2)}) collective-permute-start(bf16[64,8192]{1,0:T(8,128)(2,1)} %get-tuple-element.41), channel_id=1, source_target_pairs={{0,1},{1,0},{2,3},{3,2},{4,5},{5,4},{6,7},{7,6},{8,9},{9,8},{10,11... | collective-permute-start | bytes 3145736 | tf_op jit(solution)/shard_map/ppermute | solution.py:539
  113.9 38.8 %copy-start.1 = (bf16[2,64,8192]{2,1,0:T(8,128)(2,1)S(1)}, bf16[2,64,8192]{2,1,0:T(8,128)(2,1)}, u32[]{:S(2)}) copy-start(bf16[2,64,8192]{2,1,0:T(8,128)(2,1)} %down_hbm.3) | copy-start | bytes 6291460
  113.9 38.8 %copy-start.2 = (bf16[2,64,1024]{2,1,0:T(8,128)(2,1)S(1)}, bf16[2,64,1024]{2,1,0:T(8,128)(2,1)}, u32[]{:S(2)}) copy-start(bf16[2,64,1024]{2,1,0:T(8,128)(2,1)} %up_hbm.3) | copy-start | bytes 786436
  114.7 66.2 %collective-permute-start.9 = (bf16[32,8192]{1,0:T(8,128)(2,1)}, bf16[32,8192]{1,0:T(8,128)(2,1)S(1)}, u32[]{:S(2)}, u32[]{:S(2)}) collective-permute-start(bf16[32,8192]{1,0:T(8,128)(2,1)} %pad_maximum_fusion.4), channel_id=1, source_target_pairs={{0,6},{1,7},{2,4},{3,5},{4,2},{5,3},{6,0},{7,1},{8,14},{9,15},{10,... | collective-permute-start | bytes 1572872 | tf_op jit(solution)/shard_map/ppermute | solution.py:539
  115.6 65.4 %collective-permute-start.8 = (bf16[32,8192]{1,0:T(8,128)(2,1)}, bf16[32,8192]{1,0:T(8,128)(2,1)}, u32[]{:S(2)}, u32[]{:S(2)}) collective-permute-start(bf16[32,8192]{1,0:T(8,128)(2,1)} %pad_maximum_fusion.3), channel_id=1, source_target_pairs={{0,4},{1,5},{2,6},{3,7},{4,0},{5,1},{6,2},{7,3},{8,12},{9,13},{10,... | collective-permute-start | bytes 1572872 | tf_op jit(solution)/shard_map/ppermute | solution.py:539
  124.7 56.2 %collective-permute-start.7 = (bf16[32,8192]{1,0:T(8,128)(2,1)}, bf16[32,8192]{1,0:T(8,128)(2,1)}, u32[]{:S(2)}, u32[]{:S(2)}) collective-permute-start(bf16[32,8192]{1,0:T(8,128)(2,1)} %pad_maximum_fusion.2), channel_id=1, source_target_pairs={{0,2},{1,3},{2,0},{3,1},{4,6},{5,7},{6,4},{7,5},{8,10},{9,11},{10,... | collective-permute-start | bytes 1572872 | tf_op jit(solution)/shard_map/ppermute | solution.py:539
  152.6 33.8 %copy-start.5 = (bf16[32,8192]{1,0:T(8,128)(2,1)S(1)}, bf16[32,8192]{1,0:T(8,128)(2,1)}, u32[]{:S(2)}) copy-start(bf16[32,8192]{1,0:T(8,128)(2,1)} %get-tuple-element.31.refs_4_) | copy-start | bytes 1572868
  157.8 28.6 %all-to-all-start.2 = ((f32[16,1,256]{2,1,0:T(1,128)}), f32[16,1,256]{2,1,0:T(1,128)S(1)}, u32[]{:S(2)}, u32[]{:S(2)}) async-start(f32[16,1,256]{2,1,0:T(1,128)} %get-tuple-element.36), calls=%async_computation.2 | async-start | bytes 32768 | tf_op jit(solution)/shard_map/all_to_all | solution.py:613

commit v7 on v6

--- a/solution.py
+++ b/solution.py
@@ -154,8 +154,12 @@
     rows_copy.start()
     inner = SCALE * jnp.sum(hidden.astype(F32) * pulled, axis=1, keepdims=True)
     n_dev, _, all_lanes = told_ref.shape
-    hot = iota((n_dev, slots), 1) // capacity == iota((n_dev, slots), 0)
-    part = exact_dot(hot.astype(F32), marks * inner)
+    scored = marks * inner
+    if capacity % 8 == 0:
+        part = jnp.sum(scored.reshape(n_dev, capacity, MARKS), axis=1)
+    else:
+        hot = iota((n_dev, slots), 1) // capacity == iota((n_dev, slots), 0)
+        part = exact_dot(hot.astype(F32), scored)
     score_lanes = all_lanes - MARKS
     spread = exact_dot(part, sequence_lanes(score_lanes, count, seqs))
     at_device = iota((n_dev, score_lanes), 0) == iota((n_dev, score_lanes), 1) // seqs
@@ -206,9 +210,10 @@
     losses, by_order = jnp.zeros(total.shape, F32), []
     for pair in range(seqs // 2):
         margin = BETA * (ordered[2 * pair] - ordered[2 * pair + 1])
-        loss = jnp.maximum(-margin, 0.0) + jnp.log1p(jnp.exp(-jnp.abs(margin)))
+        small = jnp.exp(-jnp.abs(margin))
+        loss = jnp.maximum(-margin, 0.0) + jnp.log1p(small)
         losses = jnp.where(lane == pair, loss, losses)
-        lean = 1.0 / (1.0 + jnp.exp(margin))
+        lean = jnp.where(margin > 0.0, small, 1.0) / (1.0 + small)
         by_order += [-BETA * lean, BETA * lean]
     table = jnp.zeros(total.shape, F32)
     for s in range(seqs):

time: 193 us -> 193 us (level)
  no operation moved by 1% of the time
where the time goes in v7:
time: 193 us
  waiting for transfers between devices  92.9 us (48%)
  starting transfers between devices  49 us (25%)
  Pallas kernels  31.4 us (16%)
  local copies, waits for them, and re-layouts  12.8 us (7%)
  other arithmetic  5.76 us (3%)
    ppermute x9, waiting for transfers between devices, flipped(): return lax.ppermute(block, 'ad', [(at, at ^ flip) for at in range(n_dev)])  45.7 us
    all_to_all x1, waiting for transfers between devices, body(): lax.all_to_all(sent.reshape(n_dev, capacity, width + out_width + MARKS),...  27.9 us
    all_to_all x1, starting transfers between devices, body(): told = lax.all_to_all(part, 'ad', split_axis=0, concat_axis=0, tiled=True)  22.1 us
    ppermute x9, starting transfers between devices, flipped(): return lax.ppermute(block, 'ad', [(at, at ^ flip) for at in range(n_dev)])  16.9 us
    all_to_all x1, waiting for transfers between devices, body(): lax.all_to_all(sent_g.reshape(half_size, 2 * capacity, out_width + MARKS)...  14 us
    pallas_call x2, Pallas kernels, project(): pl.pallas_call(functools.partial(project_kernel, side, split, capacity, o...  9.28 us
    pallas_call x1, Pallas kernels, finish(): pl.pallas_call(functools.partial(finish_kernel, count, seqs, slots // n_d...  6.43 us
    all_to_all x1, waiting for transfers between devices, body(): told = lax.all_to_all(part, 'ad', split_axis=0, concat_axis=0, tiled=True)  5.4 us
  transfers between devices with their start and end apart: 13, of which 7 were waited for; matrix products, arithmetic and copies ran while one was open for 7% of the time, Pallas kernels for 10%

profile of v7, /device:TPU:0, one launch (start us, length us, event | category | flops | bytes accessed | tf_op | source)
XLA Modules:
  0.0 192.8 jit_solution(4168895337856917340)
XLA Ops:
  0.6 2.3 %half.2.refs_0_ = bf16[64,9216]{1,0:T(8,128)(2,1)} custom-call(s32[1]{0:T(128)} %bitcast.4.which_ref, bf16[2,64,1024]{2,1,0:T(8,128)(2,1)} %up_hbm.3, bf16[2,64,8192]{2,1,0:T(8,128)(2,1)} %down_hbm.3), custom_call_target="tpu_custom_call" | custom-call | tf_op jit(solution)/shard_map/half/pallas_call | solution.py:508
  3.0 4.1 %collective-permute-start.4 = (bf16[64,9216]{1,0:T(8,128)(2,1)}, bf16[64,9216]{1,0:T(8,128)(2,1)}, u32[]{:S(2)}, u32[]{:S(2)}) collective-permute-start(bf16[64,9216]{1,0:T(8,128)(2,1)} %half.2.refs_0_), channel_id=1, source_target_pairs={{0,8},{1,9},{2,10},{3,11},{4,12},{5,13},{6,14},{7,15},{8,0},{9,1},... | collective-permute-start | bytes 3538952 | tf_op jit(solution)/shard_map/ppermute | solution.py:544
  7.8 2.5 %slots.1 = (bf16[256,128]{1,0:T(8,128)(2,1)}, bf16[256,128]{1,0:T(8,128)(2,1)}, bf16[128,128]{1,0:T(8,128)(2,1)}, bf16[256,1152]{1,0:T(8,128)(2,1)}) custom-call(s32[1]{0:T(128)} %bitcast.3.half_ref, s32[128,1]{1,0:T(8,128)} %gate.3.owner_ref, s32[1,128]{1,0:T(1,128)} %bitcast.34, s32[1,128]{1,0:T(1,128)} %segment_ref.1, bf16[128,1024]{1,0:T(8,128)(2,1)} %g_ref.3), custom_call_target="tpu_custom_call" | custom-call | tf_op jit(solution)/shard_map/slots/pallas_call | solution.py:412
  10.3 4.0 %all-to-all-start = ((bf16[8,32,1152]{2,1,0:T(8,128)(2,1)}), bf16[8,32,1152]{2,1,0:T(8,128)(2,1)S(1)}, u32[]{:S(2)}, u32[]{:S(2)}) async-start(bf16[8,32,1152]{2,1,0:T(8,128)(2,1)} %bitcast.27), calls=%async_computation | async-start | bytes 1179648 | tf_op jit(solution)/shard_map/all_to_all | solution.py:562
  14.3 2.5 %half.3.refs_1_ = bf16[64,9216]{1,0:T(8,128)(2,1)} custom-call(s32[1]{0:T(128)} %bitcast.8.which_ref, bf16[2,64,1024]{2,1,0:T(8,128)(2,1)} %up_hbm.3, bf16[2,64,8192]{2,1,0:T(8,128)(2,1)} %down_hbm.3), custom_call_target="tpu_custom_call" | custom-call | tf_op jit(solution)/shard_map/half/pallas_call | solution.py:508
  18.6 3.2 %send.1.refs_0_ = bf16[256,9344]{1,0:T(8,128)(2,1)S(1)} custom-call(bf16[256,128]{1,0:T(8,128)(2,1)S(1)} %copy-done.7, bf16[128,128]{1,0:T(8,128)(2,1)S(1)} %copy-done.8, bf16[128,1024]{1,0:T(8,128)(2,1)S(1)} %copy-done.6, bf16[128,8192]{1,0:T(8,128)(2,1)S(1)} %copy-done.3), custom_call_target="tpu_custom_call" | custom-call | flops 612368384 | bytes 7176192 | tf_op jit(solution)/shard_map/send/pallas_call | solution.py:469
  21.9 2.2 %copy-done = bf16[256,9344]{1,0:T(8,128)(2,1)} copy-done((bf16[256,9344]{1,0:T(8,128)(2,1)}, bf16[256,9344]{1,0:T(8,128)(2,1)S(1)}, u32[]{:S(2)}) %copy-start) | copy-done | bytes 4784152
  25.0 14.0 %all-to-all-done.g_ref = bf16[8,32,1152]{2,1,0:T(8,128)(2,1)S(1)} async-done(((bf16[8,32,1152]{2,1,0:T(8,128)(2,1)}), bf16[8,32,1152]{2,1,0:T(8,128)(2,1)S(1)}, u32[]{:S(2)}, u32[]{:S(2)}) %all-to-all-start) | async-done | bytes 589856 | tf_op jit(solution)/shard_map/all_to_all | solution.py:562
  39.8 4.7 %project.2 = (bf16[32,8192]{1,0:T(8,128)(2,1)}, bf16[32,8192]{1,0:T(8,128)(2,1)}, bf16[32,8192]{1,0:T(8,128)(2,1)}, bf16[32,8192]{1,0:T(8,128)(2,1)}) custom-call(s32[1]{0:T(128)} %bitcast.6.spot_ref, bf16[8,32,1152]{2,1,0:T(8,128)(2,1)} %copy-done.9, f32[2,128]{1,0:T(2,128)} %compare_convert_fusion.which.refs_0_, bf16[64,9216]{1,0:T(8,128)(2,1)} %half.2.refs_0_, ...), custom_call_target="tpu_custom_call" | custom-call | flops 1000 | bytes 1000 | tf_op jit(solution)/shard_map/project/pallas_call | solution.py:75
  44.5 1.5 collective-permute-start
  46.0 2.4 %collective-permute-start.1 = (bf16[32,8192]{1,0:T(8,128)(2,1)}, bf16[32,8192]{1,0:T(8,128)(2,1)}, u32[]{:S(2)}, u32[]{:S(2)}) collective-permute-start(bf16[32,8192]{1,0:T(8,128)(2,1)} %get-tuple-element.33), channel_id=1, source_target_pairs={{0,4},{1,5},{2,6},{3,7},{4,0},{5,1},{6,2},{7,3},{8,12},{9,13},{10,... | collective-permute-start | bytes 1572872 | tf_op jit(solution)/shard_map/ppermute | solution.py:544
  48.4 1.0 copy-done.4
  50.2 4.6 %all-to-all-start.1 = ((bf16[16,16,9344]{2,1,0:T(8,128)(2,1)}), bf16[16,16,9344]{2,1,0:T(8,128)(2,1)}, u32[]{:S(2)}, u32[]{:S(2)}) async-start(bf16[16,16,9344]{2,1,0:T(8,128)(2,1)} %bitcast.23), calls=%async_computation.1 | async-start | bytes 9568256 | tf_op jit(solution)/shard_map/all_to_all | solution.py:585
  54.7 4.0 %collective-permute-done.4.refs_0_ = bf16[64,9216]{1,0:T(8,128)(2,1)} collective-permute-done((bf16[64,9216]{1,0:T(8,128)(2,1)}, bf16[64,9216]{1,0:T(8,128)(2,1)}, u32[]{:S(2)}, u32[]{:S(2)}) %collective-permute-start.4) | collective-permute-done | bytes 1179680 | tf_op jit(solution)/shard_map/ppermute | solution.py:544
  58.8 1.5 collective-permute-start.5
  60.3 35.3 %collective-permute-done.1.refs_6_ = bf16[32,8192]{1,0:T(8,128)(2,1)} collective-permute-done((bf16[32,8192]{1,0:T(8,128)(2,1)}, bf16[32,8192]{1,0:T(8,128)(2,1)}, u32[]{:S(2)}, u32[]{:S(2)}) %collective-permute-start.1) | collective-permute-done | bytes 524320 | tf_op jit(solution)/shard_map/ppermute | solution.py:544
  95.6 5.8 %collective-permute-done.2.refs_7_ = bf16[32,8192]{1,0:T(8,128)(2,1)} collective-permute-done((bf16[32,8192]{1,0:T(8,128)(2,1)}, bf16[32,8192]{1,0:T(8,128)(2,1)}, u32[]{:S(2)}, u32[]{:S(2)}) %collective-permute-start.2) | collective-permute-done | bytes 524320 | tf_op jit(solution)/shard_map/ppermute | solution.py:544
  101.5 1.0 slice.52
  102.5 1.0 slice.53
  103.4 1.0 slice.54
  104.4 1.0 pad_maximum_fusion
  105.5 4.6 %project.3 = (bf16[64,8192]{1,0:T(8,128)(2,1)}, bf16[64,8192]{1,0:T(8,128)(2,1)}) custom-call(s32[1]{0:T(128)} %bitcast.6.spot_ref, bf16[8,32,1152]{2,1,0:T(8,128)(2,1)} %copy-done.9, f32[2,128]{1,0:T(2,128)} %gate.5.which, bf16[64,9216]{1,0:T(8,128)(2,1)} %collective-permute-done.4.refs_0_, bf16[64,9216]{1,0:T(8,128)(2,1)} %collective-permute-done.5.refs_1_), custom_call_target="tpu_custom_call" | custom-call | flops 1000 | bytes 1000 | tf_op jit(solution)/shard_map/project/pallas_call | solution.py:75
  110.6 2.0 %fusion.10 = (bf16[16,8192]{1,0:T(8,128)(2,1)S(1)}, bf16[16,8192]{1,0:T(8,128)(2,1)S(1)}, bf16[16,8192]{1,0:T(8,128)(2,1)S(1)}, bf16[16,8192]{1,0:T(8,128)(2,1)}) fusion(bf16[64,8192]{1,0:T(8,128)(2,1)} %get-tuple-element.40), kind=kLoop, calls=%fused_computation.28 | loop fusion | bytes 2097152 | tf_op jit(solution)/shard_map/slice | solution.py:601
  113.9 0.8 pad_maximum_fusion.4
  114.7 0.8 pad_maximum_fusion.3
  115.6 8.3 %collective-permute-start.8 = (bf16[32,8192]{1,0:T(8,128)(2,1)}, bf16[32,8192]{1,0:T(8,128)(2,1)}, u32[]{:S(2)}, u32[]{:S(2)}) collective-permute-start(bf16[32,8192]{1,0:T(8,128)(2,1)} %pad_maximum_fusion.3), channel_id=1, source_target_pairs={{0,4},{1,5},{2,6},{3,7},{4,0},{5,1},{6,2},{7,3},{8,12},{9,13},{10,... | collective-permute-start | bytes 1572872 | tf_op jit(solution)/shard_map/ppermute | solution.py:544
  124.7 27.9 %all-to-all-done.1 = bf16[16,16,9344]{2,1,0:T(8,128)(2,1)} async-done(((bf16[16,16,9344]{2,1,0:T(8,128)(2,1)}), bf16[16,16,9344]{2,1,0:T(8,128)(2,1)}, u32[]{:S(2)}, u32[]{:S(2)}) %all-to-all-start.1) | async-done | bytes 4784160 | tf_op jit(solution)/shard_map/all_to_all | solution.py:585
  152.6 5.2 %score.1 = (f32[16,1,256]{2,1,0:T(1,128)}, bf16[256,256]{1,0:T(8,128)(2,1)}) custom-call(f32[1,256]{1,0:T(1,128)S(1)} %fusion.3.own_ref, bf16[256,9344]{1,0:T(8,128)(2,1)} %bitcast.10.got_hbm.refs_2_, bf16[128,8192]{1,0:T(8,128)(2,1)S(1)} %bitcast.24, bf16[128,1024]{1,0:T(8,128)(2,1)S(1)} %bitcast.25), custom_call_target="tpu_custom_call" | custom-call | flops 603979776 | bytes 7077888 | tf_op jit(solution)/shard_map/score/pallas_call | solution.py:178
  157.8 22.1 %all-to-all-start.2 = ((f32[16,1,256]{2,1,0:T(1,128)}), f32[16,1,256]{2,1,0:T(1,128)S(1)}, u32[]{:S(2)}, u32[]{:S(2)}) async-start(f32[16,1,256]{2,1,0:T(1,128)} %get-tuple-element.36), calls=%async_computation.2 | async-start | bytes 32768 | tf_op jit(solution)/shard_map/all_to_all | solution.py:618
  179.8 1.1 pad_maximum_fusion.1.refs_9_
  180.9 5.4 %all-to-all-done.2.told_ref = f32[16,1,256]{2,1,0:T(1,128)S(1)} async-done(((f32[16,1,256]{2,1,0:T(1,128)}), f32[16,1,256]{2,1,0:T(1,128)S(1)}, u32[]{:S(2)}, u32[]{:S(2)}) %all-to-all-start.2) | async-done | bytes 16416 | tf_op jit(solution)/shard_map/all_to_all | solution.py:618
  186.4 6.4 %finish.1 = (f32[2]{0:T(128)}, f32[128,1]{1,0:T(8,128)}, bf16[128,1024]{1,0:T(8,128)(2,1)}, bf16[128,8192]{1,0:T(8,128)(2,1)}, bf16[128,8192]{1,0:T(8,128)(2,1)}) custom-call(s32[1]{0:T(128)} %bitcast.me_ref, f32[16,1,256]{2,1,0:T(1,128)S(1)} %all-to-all-done.2.told_ref, f32[128,128]{1,0:T(8,128)S(1)} %pad_convert_fusion.refs_0_, ...), custom_call_target="tpu_custom_call" | custom-call | flops 1073741824 | bytes 12582912 | tf_op jit(solution)/shard_map/finish/pallas_call | solution.py:352
  (71 shorter events, 7.7 us)
Async XLA Ops:
  0.6 6.5 %copy-start.13 = (s32[128,1]{0,1:T(1,128)S(1)}, s32[128,1]{0,1:T(1,128)}, u32[]{:S(2)}) copy-start(s32[128,1]{0,1:T(1,128)} %param.12) | copy-start | bytes 1540
  3.0 55.8 %collective-permute-start.4 = (bf16[64,9216]{1,0:T(8,128)(2,1)}, bf16[64,9216]{1,0:T(8,128)(2,1)}, u32[]{:S(2)}, u32[]{:S(2)}) collective-permute-start(bf16[64,9216]{1,0:T(8,128)(2,1)} %half.2.refs_0_), channel_id=1, source_target_pairs={{0,8},{1,9},{2,10},{3,11},{4,12},{5,13},{6,14},{7,15},{8,0},{9,1},... | collective-permute-start | bytes 3538952 | tf_op jit(solution)/shard_map/ppermute | solution.py:544
  10.3 6.5 %copy-start.14 = (f32[1,4]{1,0:T(1,128)S(1)}, f32[1,4]{1,0:T(1,128)}, u32[]{:S(2)}) copy-start(f32[1,4]{1,0:T(1,128)} %param.16) | copy-start | bytes 52
  10.3 6.7 %copy-start.15 = (s32[1,4]{1,0:T(1,128)S(1)}, s32[1,4]{1,0:T(1,128)}, u32[]{:S(2)}) copy-start(s32[1,4]{1,0:T(1,128)} %param.15) | copy-start | bytes 52
  10.3 7.0 %copy-start.16 = (s32[8]{0:T(128)S(1)}, s32[8]{0:T(128)}, u32[]{:S(2)}) copy-start(s32[8]{0:T(128)} %constant.50.clone) | copy-start | bytes 100
  10.3 7.0 %copy-start.11 = (bf16[256,128]{1,0:T(8,128)(2,1)S(1)}, bf16[256,128]{1,0:T(8,128)(2,1)}, u32[]{:S(2)}) copy-start(bf16[256,128]{1,0:T(8,128)(2,1)} %get-tuple-element.38) | copy-start | bytes 196612
  10.3 28.7 %all-to-all-start = ((bf16[8,32,1152]{2,1,0:T(8,128)(2,1)}), bf16[8,32,1152]{2,1,0:T(8,128)(2,1)S(1)}, u32[]{:S(2)}, u32[]{:S(2)}) async-start(bf16[8,32,1152]{2,1,0:T(8,128)(2,1)} %bitcast.27), calls=%async_computation | async-start | bytes 1179648 | tf_op jit(solution)/shard_map/all_to_all | solution.py:562
  14.3 4.3 %copy-start.3 = (bf16[128,8192]{1,0:T(8,128)(2,1)S(1)}, bf16[128,8192]{1,0:T(8,128)(2,1)}, u32[]{:S(2)}) copy-start(bf16[128,8192]{1,0:T(8,128)(2,1)} %tokens_hbm.1) | copy-start | bytes 6291460
  14.3 4.3 %copy-start.6 = (bf16[128,1024]{1,0:T(8,128)(2,1)S(1)}, bf16[128,1024]{1,0:T(8,128)(2,1)}, u32[]{:S(2)}) copy-start(bf16[128,1024]{1,0:T(8,128)(2,1)} %g_ref.3) | copy-start | bytes 786436
  14.3 4.3 %copy-start.7 = (bf16[256,128]{1,0:T(8,128)(2,1)S(1)}, bf16[256,128]{1,0:T(8,128)(2,1)}, u32[]{:S(2)}) copy-start(bf16[256,128]{1,0:T(8,128)(2,1)} %get-tuple-element.28.to_slot) | copy-start | bytes 196612
  14.3 4.3 %copy-start.8 = (bf16[128,128]{1,0:T(8,128)(2,1)S(1)}, bf16[128,128]{1,0:T(8,128)(2,1)}, u32[]{:S(2)}) copy-start(bf16[128,128]{1,0:T(8,128)(2,1)} %get-tuple-element.29.marks) | copy-start | bytes 98308
  18.6 5.5 %copy-start.12 = (s32[1,128]{1,0:T(1,128)S(1)}, s32[1,128]{1,0:T(1,128)}, u32[]{:S(2)}) copy-start(s32[1,128]{1,0:T(1,128)} %segment_ref.1) | copy-start | bytes 1540
  21.9 2.2 %copy-start = (bf16[256,9344]{1,0:T(8,128)(2,1)}, bf16[256,9344]{1,0:T(8,128)(2,1)S(1)}, u32[]{:S(2)}) copy-start(bf16[256,9344]{1,0:T(8,128)(2,1)S(1)} %send.1.refs_0_) | copy-start | bytes 14352388
  39.0 0.8 copy-start.9
  44.5 15.8 %collective-permute-start = (bf16[32,8192]{1,0:T(8,128)(2,1)}, bf16[32,8192]{1,0:T(8,128)(2,1)}, u32[]{:S(2)}, u32[]{:S(2)}) collective-permute-start(bf16[32,8192]{1,0:T(8,128)(2,1)} %get-tuple-element.32), channel_id=1, source_target_pairs={{0,2},{1,3},{2,0},{3,1},{4,6},{5,7},{6,4},{7,5},{8,10},{9,11},{10,... | collective-permute-start | bytes 1572872 | tf_op jit(solution)/shard_map/ppermute | solution.py:544
  46.0 49.6 %collective-permute-start.1 = (bf16[32,8192]{1,0:T(8,128)(2,1)}, bf16[32,8192]{1,0:T(8,128)(2,1)}, u32[]{:S(2)}, u32[]{:S(2)}) collective-permute-start(bf16[32,8192]{1,0:T(8,128)(2,1)} %get-tuple-element.33), channel_id=1, source_target_pairs={{0,4},{1,5},{2,6},{3,7},{4,0},{5,1},{6,2},{7,3},{8,12},{9,13},{10,... | collective-permute-start | bytes 1572872 | tf_op jit(solution)/shard_map/ppermute | solution.py:544
  48.4 53.1 %collective-permute-start.2 = (bf16[32,8192]{1,0:T(8,128)(2,1)}, bf16[32,8192]{1,0:T(8,128)(2,1)}, u32[]{:S(2)}, u32[]{:S(2)}) collective-permute-start(bf16[32,8192]{1,0:T(8,128)(2,1)} %get-tuple-element.34), channel_id=1, source_target_pairs={{0,6},{1,7},{2,4},{3,5},{4,2},{5,3},{6,0},{7,1},{8,14},{9,15},{10,... | collective-permute-start | bytes 1572872 | tf_op jit(solution)/shard_map/ppermute | solution.py:544
  48.4 1.0 copy-start.4
  50.2 102.5 %all-to-all-start.1 = ((bf16[16,16,9344]{2,1,0:T(8,128)(2,1)}), bf16[16,16,9344]{2,1,0:T(8,128)(2,1)}, u32[]{:S(2)}, u32[]{:S(2)}) async-start(bf16[16,16,9344]{2,1,0:T(8,128)(2,1)} %bitcast.23), calls=%async_computation.1 | async-start | bytes 9568256 | tf_op jit(solution)/shard_map/all_to_all | solution.py:585
  58.8 46.7 %collective-permute-start.5 = (bf16[64,9216]{1,0:T(8,128)(2,1)}, bf16[64,9216]{1,0:T(8,128)(2,1)}, u32[]{:S(2)}, u32[]{:S(2)}) collective-permute-start(bf16[64,9216]{1,0:T(8,128)(2,1)} %collective-permute-done.4.refs_0_), channel_id=1, source_target_pairs={{0,16},{16,0},{1,17},{17,1},{2,18},{18,2},{3,19},{19,3},{4,20},{20... | collective-permute-start | bytes 3538952 | tf_op jit(solution)/shard_map/ppermute | solution.py:547
  101.4 3.0 %copy-start.10 = (bf16[16,8192]{1,0:T(8,128)(2,1)S(1)}, bf16[16,8192]{1,0:T(8,128)(2,1)}, u32[]{:S(2)}) copy-start(bf16[16,8192]{1,0:T(8,128)(2,1)} %slice.36) | copy-start | bytes 786436
  105.5 80.9 %collective-permute-start.3 = (bf16[64,8192]{1,0:T(8,128)(2,1)}, bf16[64,8192]{1,0:T(8,128)(2,1)}, u32[]{:S(2)}, u32[]{:S(2)}) collective-permute-start(bf16[64,8192]{1,0:T(8,128)(2,1)} %pad_maximum_fusion), channel_id=1, source_target_pairs={{0,1},{1,0},{2,3},{3,2},{4,5},{5,4},{6,7},{7,6},{8,9},{9,8},{10,11... | collective-permute-start | bytes 3145736 | tf_op jit(solution)/shard_map/ppermute | solution.py:544
  110.1 3.0 %collective-permute-start.6 = (bf16[64,8192]{1,0:T(8,128)(2,1)}, bf16[64,8192]{1,0:T(8,128)(2,1)S(1)}, u32[]{:S(2)}, u32[]{:S(2)}) collective-permute-start(bf16[64,8192]{1,0:T(8,128)(2,1)} %get-tuple-element.41), channel_id=1, source_target_pairs={{0,1},{1,0},{2,3},{3,2},{4,5},{5,4},{6,7},{7,6},{8,9},{9,8},{10,11... | collective-permute-start | bytes 3145736 | tf_op jit(solution)/shard_map/ppermute | solution.py:544
  113.9 38.8 %copy-start.1 = (bf16[2,64,8192]{2,1,0:T(8,128)(2,1)S(1)}, bf16[2,64,8192]{2,1,0:T(8,128)(2,1)}, u32[]{:S(2)}) copy-start(bf16[2,64,8192]{2,1,0:T(8,128)(2,1)} %down_hbm.3) | copy-start | bytes 6291460
  113.9 38.8 %copy-start.2 = (bf16[2,64,1024]{2,1,0:T(8,128)(2,1)S(1)}, bf16[2,64,1024]{2,1,0:T(8,128)(2,1)}, u32[]{:S(2)}) copy-start(bf16[2,64,1024]{2,1,0:T(8,128)(2,1)} %up_hbm.3) | copy-start | bytes 786436
  114.7 66.2 %collective-permute-start.9 = (bf16[32,8192]{1,0:T(8,128)(2,1)}, bf16[32,8192]{1,0:T(8,128)(2,1)S(1)}, u32[]{:S(2)}, u32[]{:S(2)}) collective-permute-start(bf16[32,8192]{1,0:T(8,128)(2,1)} %pad_maximum_fusion.4), channel_id=1, source_target_pairs={{0,6},{1,7},{2,4},{3,5},{4,2},{5,3},{6,0},{7,1},{8,14},{9,15},{10,... | collective-permute-start | bytes 1572872 | tf_op jit(solution)/shard_map/ppermute | solution.py:544
  115.6 65.4 %collective-permute-start.8 = (bf16[32,8192]{1,0:T(8,128)(2,1)}, bf16[32,8192]{1,0:T(8,128)(2,1)}, u32[]{:S(2)}, u32[]{:S(2)}) collective-permute-start(bf16[32,8192]{1,0:T(8,128)(2,1)} %pad_maximum_fusion.3), channel_id=1, source_target_pairs={{0,4},{1,5},{2,6},{3,7},{4,0},{5,1},{6,2},{7,3},{8,12},{9,13},{10,... | collective-permute-start | bytes 1572872 | tf_op jit(solution)/shard_map/ppermute | solution.py:544
  124.7 56.2 %collective-permute-start.7 = (bf16[32,8192]{1,0:T(8,128)(2,1)}, bf16[32,8192]{1,0:T(8,128)(2,1)}, u32[]{:S(2)}, u32[]{:S(2)}) collective-permute-start(bf16[32,8192]{1,0:T(8,128)(2,1)} %pad_maximum_fusion.2), channel_id=1, source_target_pairs={{0,2},{1,3},{2,0},{3,1},{4,6},{5,7},{6,4},{7,5},{8,10},{9,11},{10,... | collective-permute-start | bytes 1572872 | tf_op jit(solution)/shard_map/ppermute | solution.py:544
  152.6 33.7 %copy-start.5 = (bf16[32,8192]{1,0:T(8,128)(2,1)S(1)}, bf16[32,8192]{1,0:T(8,128)(2,1)}, u32[]{:S(2)}) copy-start(bf16[32,8192]{1,0:T(8,128)(2,1)} %get-tuple-element.31.refs_4_) | copy-start | bytes 1572868
  157.8 28.6 %all-to-all-start.2 = ((f32[16,1,256]{2,1,0:T(1,128)}), f32[16,1,256]{2,1,0:T(1,128)S(1)}, u32[]{:S(2)}, u32[]{:S(2)}) async-start(f32[16,1,256]{2,1,0:T(1,128)} %get-tuple-element.36), calls=%async_computation.2 | async-start | bytes 32768 | tf_op jit(solution)/shard_map/all_to_all | solution.py:618

commit v8 on v7

--- a/solution.py
+++ b/solution.py
@@ -112,45 +112,66 @@
     return (iota(shape, 0) == count + iota(shape, 1) % seqs).astype(F32)
 
 
+def pull_kernel(count, rank_size, g_ref, up, out):
+    lanes, out_width = up.shape
+    marks = g_ref[:, out_width:]
+    lane = iota((g_ref.shape[0], lanes), 1) // rank_size
+    member = jnp.zeros((g_ref.shape[0], lanes), F32)
+    for which in range(count):
+        member = jnp.where(lane == which, marks[:, which : which + 1].astype(F32), member)
+    pull = member * lax.dot_general(
+        g_ref[:, :out_width], up[...], (((1,), (1,)), ((), ())), preferred_element_type=F32
+    )
+    out[:, :lanes] = pull.astype(BF16)
+    out[:, lanes:] = marks
+
+
+def pull_rows(g_rows, up, count, rank_size):
+    vmem = pl.BlockSpec(memory_space=pltpu.VMEM)
+    return pl.pallas_call(
+        functools.partial(pull_kernel, count, rank_size),
+        out_shape=jax.ShapeDtypeStruct((g_rows.shape[0], up.shape[0] + MARKS), BF16),
+        in_specs=[vmem] * 2,
+        out_specs=vmem,
+        cost_estimate=pl.CostEstimate(flops=1000, bytes_accessed=1000, transcendentals=0),
+        name="pull",
+    )(g_rows, up)
+
+
+def in_slots(here, near, across):
+    first = jnp.where(here == 0, near, across)
+    return jnp.concatenate([first, jnp.where(here == 0, across, near)], axis=0)
+
+
 def score_kernel(
-    count, seqs, rank_size, capacity, columns, own_ref, got_hbm, down, up, *refs
+    count, seqs, capacity, here_ref, own_ref, near_ref, across_ref, down, got_hbm, *refs
 ):
-    told_ref, rows_hbm, got, rank_rows, got_sems, rows_sem = refs
-    width, out_width = down.shape[1], up.shape[1]
-    parts = column_parts(width, 4 * columns)
-    tail = slice(width, got.shape[1])
-    copies = []
-    for at, part in enumerate(parts):
-        copies.append(
-            (pltpu.make_async_copy(got_hbm.at[:, part], got.at[:, part], got_sems.at[at]),)
-        )
-    tail_copy = pltpu.make_async_copy(got_hbm.at[:, tail], got.at[:, tail], got_sems.at[len(parts)])
-    tail_copy.start()
-    for pair in copies:
-        for copy in pair:
-            copy.start()
+    told_ref, rows_hbm, got, hidden_rows, got_sems, rows_sem = refs
+    lanes, width = down.shape
+    parts = column_parts(width, 4096)
+    copies = [
+        pltpu.make_async_copy(got_hbm.at[:, part], got.at[:, part], got_sems.at[at])
+        for at, part in enumerate(parts)
+    ]
+    for copy in copies:
+        copy.start()
     contract = (((1,), (1,)), ((), ()))
-    tail_copy.wait()
-    marks = got[:, width + out_width :].astype(F32)
-    slots, lanes = got.shape[0], down.shape[0]
-    lane = iota((slots, lanes), 1) // rank_size
+    both = in_slots(here_ref[0], near_ref[...].astype(F32), across_ref[...].astype(F32))
+    pulled, marks = both[:, :lanes], both[:, lanes:]
+    slots = got.shape[0]
+    lane = iota((slots, lanes), 1) // (lanes // count)
     member = jnp.zeros((slots, lanes), F32)
     for which in range(count):
         member = jnp.where(lane == which, marks[:, which : which + 1], member)
-    pulled = member * lax.dot_general(
-        got[:, width : width + out_width], up[...], contract, preferred_element_type=F32
-    )
-    rank_rows[:, lanes:] = pulled.astype(BF16)
     total = jnp.zeros((slots, lanes), F32)
-    for pair, part in zip(copies, parts):
-        for copy in pair:
-            copy.wait()
+    for copy, part in zip(copies, parts):
+        copy.wait()
         total = total + lax.dot_general(
             got[:, part], down[:, part], contract, preferred_element_type=F32
         )
     hidden = (member * total).astype(BF16)
-    rank_rows[:, :lanes] = hidden
-    rows_copy = pltpu.make_async_copy(rank_rows, rows_hbm, rows_sem)
+    hidden_rows[...] = hidden
+    rows_copy = pltpu.make_async_copy(hidden_rows, rows_hbm, rows_sem)
     rows_copy.start()
     inner = SCALE * jnp.sum(hidden.astype(F32) * pulled, axis=1, keepdims=True)
     n_dev, _, all_lanes = told_ref.shape
@@ -169,34 +190,33 @@
     rows_copy.wait()
 
 
-def score(own, got, down, up, count, seqs, rank_size, n_dev):
+def score(here, own, near, across, got, down, count, seqs, n_dev):
     slots = got.shape[0]
     lanes, width = down.shape
-    columns = up.shape[1]
-    n_parts = len(column_parts(width, 4 * columns))
+    n_parts = len(column_parts(width, 4096))
     vmem, hbm = pl.BlockSpec(memory_space=pltpu.VMEM), pl.BlockSpec(memory_space=pl.ANY)
     return pl.pallas_call(
-        functools.partial(score_kernel, count, seqs, rank_size, slots // n_dev, columns),
+        functools.partial(score_kernel, count, seqs, slots // n_dev),
         out_shape=[
             jax.ShapeDtypeStruct((n_dev,) + own.shape, F32),
-            pltpu.HBM((slots, 2 * lanes), BF16),
+            pltpu.HBM((slots, lanes), BF16),
         ],
-        in_specs=[vmem, hbm, vmem, vmem],
+        in_specs=[pl.BlockSpec(memory_space=pltpu.SMEM)] + [vmem] * 4 + [hbm],
         out_specs=[vmem, pl.BlockSpec(memory_space=pltpu.HBM)],
         scratch_shapes=[
             pltpu.VMEM(got.shape, BF16),
-            pltpu.VMEM((slots, 2 * lanes), BF16),
-            pltpu.SemaphoreType.DMA((n_parts + 1,)),
+            pltpu.VMEM((slots, lanes), BF16),
+            pltpu.SemaphoreType.DMA((n_parts,)),
             pltpu.SemaphoreType.DMA,
         ],
         compiler_params=pltpu.CompilerParams(vmem_limit_bytes=16 * 2**20),
         cost_estimate=pl.CostEstimate(
-            flops=2 * slots * lanes * (width + columns),
-            bytes_accessed=2 * (slots + lanes) * (width + columns),
+            flops=2 * slots * lanes * width,
+            bytes_accessed=2 * (slots + lanes) * width,
             transcendentals=0,
         ),
         name="score",
-    )(own, got, down, up)
+    )(here.reshape(1), own, near, across, down, got)
 
 
 def weights(total, count, seqs):
@@ -222,21 +242,22 @@
     return losses, table
 
 
-def finish_kernel(count, seqs, capacity, columns, used, me_ref, told_ref, *refs):
-    row_marks, rank_hbm, got_hbm, *refs = refs
+def finish_kernel(count, seqs, capacity, used, place_ref, told_ref, *refs):
+    row_marks, *small_hbms, got_hbm = refs[:5]
+    refs = refs[5:]
     if used:
         pick, *refs = refs
     block_hbms, refs = refs[: len(used)], refs[len(used) :]
-    losses_ref, row_weight, up_hbm, down_hbm, *refs = refs
+    losses_ref, row_weight, upper_ref, down_hbm, *refs = refs
     if used:
-        input_hbm, rank_rows, got, grad_up, grad_down, rows, input_grad, *sems = refs
-        rank_sem, got_sems, up_sem, down_sems, block_sems, input_sems = sems
+        input_hbm, *smalls = refs[:4]
+        got, grad_down, rows, input_grad, *sems = refs[4:]
+        small_sems, got_sems, down_sems, block_sems, input_sems = sems
     else:
-        rank_rows, got, grad_up, grad_down, rank_sem, got_sems, up_sem, down_sems = refs
-    width, out_width = grad_down.shape[1], grad_up.shape[1]
-    parts = column_parts(width, 2 * columns)
-    tail = slice(width, got.shape[1])
-    tail_copy = pltpu.make_async_copy(got_hbm.at[:, tail], got.at[:, tail], got_sems.at[len(parts)])
+        smalls, refs = refs[:3], refs[3:]
+        got, grad_down, small_sems, got_sems, down_sems = refs
+    lanes, width = grad_down.shape
+    parts = column_parts(width, 2048)
     copies = [
         pltpu.make_async_copy(got_hbm.at[:, part], got.at[:, part], got_sems.at[at])
         for at, part in enumerate(parts)
@@ -249,10 +270,11 @@
             )
         )
         first += size
-    rank_copy = pltpu.make_async_copy(rank_hbm, rank_rows, rank_sem)
-    rank_copy.start()
-    tail_copy.start()
-    for copy in copies + block_copies:
+    small_copies = [
+        pltpu.make_async_copy(hbm, small, small_sems.at[at])
+        for at, (hbm, small) in enumerate(zip(small_hbms, smalls))
+    ]
+    for copy in small_copies + copies + block_copies:
         copy.start()
 
     told = jnp.concatenate([told_ref[at] for at in range(told_ref.shape[0])], axis=0)
@@ -268,8 +290,8 @@
         preferred_element_type=F32,
     )
     losses, table = weights(total, count, seqs)
-    n_dev, slots = total.shape[0], got.shape[0]
-    mine = iota(total.shape, 0) == me_ref[0]
+    n_dev, slots, here = total.shape[0], got.shape[0], place_ref[1]
+    mine = iota(total.shape, 0) == place_ref[0]
     pair_lane = iota(losses.shape, 1)
     for pair in range(seqs // 2):
         losses_ref[pair] = jnp.sum(jnp.where(mine & (pair_lane == pair), losses, 0.0))
@@ -278,20 +300,16 @@
     row_weight[...] = my_weight
     hot = iota((slots, n_dev), 0) // capacity == iota((slots, n_dev), 1)
     slot_table = exact_dot(hot.astype(F32), table)
-    tail_copy.wait()
-    marks = got[:, width + out_width :].astype(F32)
+    for copy in small_copies:
+        copy.wait()
+    hidden, near_rank, across_rank = [small[...] for small in smalls]
+    both = in_slots(here, near_rank.astype(F32), across_rank.astype(F32))
+    pulled, marks = both[:, :lanes], both[:, lanes:]
     weight = jnp.sum(marks * slot_table, axis=1, keepdims=True)
-    rank_copy.wait()
-    lanes = grad_up.shape[0]
-    upper = (weight * rank_rows[:, :lanes].astype(F32)).astype(BF16)
-    lower = (weight * rank_rows[:, lanes:].astype(F32)).astype(BF16)
+    upper_ref[...] = (weight * hidden.astype(F32)).astype(BF16)
+    lower = (weight * pulled).astype(BF16)
     contract = (((0,), (0,)), ((), ()))
-    made = lax.dot_general(
-        upper, got[:, width : width + out_width], contract, preferred_element_type=F32
-    )
-    grad_up[...] = (SCALE * made).astype(BF16)
-    outs = [pltpu.make_async_copy(grad_up, up_hbm, up_sem)]
-    outs[0].start()
+    outs = []
     for at, part in enumerate(parts):
         copies[at].wait()
         made = lax.dot_general(lower, got[:, part], contract, preferred_element_type=F32)
@@ -316,46 +334,42 @@
         copy.wait()
 
 
-def finish(
-    me, told, got, rank_rows, row_marks, count, seqs, width, pick, blocks, used
-):
-    slots, lanes = rank_rows.shape[0], rank_rows.shape[1] // 2
+def finish(place, told, got, smalls, row_marks, count, seqs, pick, blocks, used):
+    (slots, width), lanes = got.shape, smalls[0].shape[1]
     rows = row_marks.shape[0]
     n_dev = told.shape[0]
-    columns = got.shape[1] - width - MARKS
-    n_parts = len(column_parts(width, 2 * columns))
+    n_parts = len(column_parts(width, 2048))
     together = not any(size % 16 for size in used)
     vmem, hbm = pl.BlockSpec(memory_space=pltpu.VMEM), pl.BlockSpec(memory_space=pltpu.HBM)
     sems = pltpu.SemaphoreType.DMA
     out_shape = [
         jax.ShapeDtypeStruct((seqs // 2,), F32),
         jax.ShapeDtypeStruct((rows, 1), F32),
-        jax.ShapeDtypeStruct((lanes, columns), BF16),
+        jax.ShapeDtypeStruct((slots, lanes), BF16),
         jax.ShapeDtypeStruct((lanes, width), BF16),
     ]
-    in_specs = [pl.BlockSpec(memory_space=pltpu.SMEM)] + [vmem] * 2 + [hbm] * 2
-    rank_rows = pltpu.with_memory_space_constraint(rank_rows, pltpu.HBM)
-    operands = [me.reshape(1), told, row_marks, rank_rows, got]
+    in_specs = [pl.BlockSpec(memory_space=pltpu.SMEM)] + [vmem] * 2 + [hbm] * 4
+    smalls = [pltpu.with_memory_space_constraint(small, pltpu.HBM) for small in smalls]
+    operands = [place, told, row_marks, *smalls, got]
     scratch = [
-        pltpu.VMEM(rank_rows.shape, BF16),
+        *[pltpu.VMEM(small.shape, BF16) for small in smalls],
         pltpu.VMEM(got.shape, BF16),
-        pltpu.VMEM((lanes, columns), BF16),
         pltpu.VMEM((lanes, width), BF16),
     ]
-    scratch_sems = [sems, sems((n_parts + 1,)), sems, sems((n_parts,))]
+    scratch_sems = [sems((3,)), sems((n_parts,)), sems((n_parts,))]
     if together:
         out_shape.append(jax.ShapeDtypeStruct((rows, width), BF16))
         in_specs += [vmem] + [hbm] * len(blocks)
         operands += [pick, *blocks]
         scratch += [pltpu.VMEM((slots, width), BF16), pltpu.VMEM((rows, width), BF16)]
         scratch_sems += [sems((len(blocks),)), sems((n_parts,))]
-    losses, row_weight, grad_up, grad_down, *input_grad = pl.pallas_call(
+    losses, row_weight, upper, grad_down, *input_grad = pl.pallas_call(
         functools.partial(
-            finish_kernel, count, seqs, slots // n_dev, columns, used if together else []
+            finish_kernel, count, seqs, slots // n_dev, used if together else []
         ),
         out_shape=out_shape,
         in_specs=in_specs,
-        out_specs=[pl.BlockSpec(memory_space=pltpu.SMEM), vmem] + [hbm] * (len(out_shape) - 2),
+        out_specs=[pl.BlockSpec(memory_space=pltpu.SMEM), vmem, vmem] + [hbm] * (len(out_shape) - 3),
         scratch_shapes=scratch + scratch_sems,
         compiler_params=pltpu.CompilerParams(vmem_limit_bytes=24 * 2**20),
         cost_estimate=pl.CostEstimate(
@@ -369,13 +383,37 @@
         blocks = jnp.concatenate([block[:size] for block, size in zip(blocks, used)])
         picked = jnp.dot(pick, blocks, preferred_element_type=F32)
         input_grad = [(row_weight * picked).astype(BF16)]
-    return input_grad[0], grad_down, grad_up, losses
+    return input_grad[0], grad_down, upper, losses
+
+
+def up_kernel(here_ref, upper, near_g, across_g, out):
+    out_width = out.shape[1]
+    contract = (((0,), (0,)), ((), ()))
+    g_rows = in_slots(here_ref[0], near_g[:, :out_width], across_g[:, :out_width])
+    made = lax.dot_general(upper[...], g_rows, contract, preferred_element_type=F32)
+    out[...] = (SCALE * made).astype(BF16)
+
+
+def up_gradient(here, upper, near_g, across_g):
+    vmem = pl.BlockSpec(memory_space=pltpu.VMEM)
+    return pl.pallas_call(
+        up_kernel,
+        out_shape=jax.ShapeDtypeStruct((upper.shape[1], near_g.shape[1] - MARKS), BF16),
+        in_specs=[pl.BlockSpec(memory_space=pltpu.SMEM)] + [vmem] * 3,
+        out_specs=vmem,
+        cost_estimate=pl.CostEstimate(
+            flops=2 * upper.shape[0] * upper.shape[1] * near_g.shape[1],
+            bytes_accessed=4 * near_g.shape[0] * near_g.shape[1],
+            transcendentals=0,
+        ),
+        name="up",
+    )(here.reshape(1), upper, near_g, across_g)
 
 
 def slots_kernel(
     count, capacity, half_size, half_ref, owner_ref, adapter_ref, segment_ref, g_ref, *refs
 ):
-    to_slot, to_half, marks_ref, sent_g = refs
+    to_slot, to_half, sent_g = refs
     slots, rows = to_slot.shape
     out_width = g_ref.shape[1]
     eye = (iota((rows, rows), 0) == iota((rows, rows), 1)).astype(BF16)
@@ -398,7 +436,6 @@
     to_half[...] = hot_half
     lane = iota((MARKS, rows), 0)
     marks = ((lane == adapter_ref[...]) | (lane == segment_ref[...] + count)).astype(BF16)
-    marks_ref[...] = marks
     sent_g[:, :out_width] = jnp.dot(hot_half, g_ref[...], preferred_element_type=F32).astype(BF16)
     sent_g[:, out_width:] = lax.dot_general(
         hot_half, marks, (((1,), (1,)), ((), ())), preferred_element_type=F32
@@ -414,19 +451,16 @@
         out_shape=[
             jax.ShapeDtypeStruct((slots, rows), BF16),
             jax.ShapeDtypeStruct((slots, rows), BF16),
-            jax.ShapeDtypeStruct((MARKS, rows), BF16),
             jax.ShapeDtypeStruct((slots, out_width + MARKS), BF16),
         ],
         in_specs=[pl.BlockSpec(memory_space=pltpu.SMEM)] + [vmem] * 4,
-        out_specs=[vmem] * 4,
+        out_specs=[vmem] * 3,
         name="slots",
     )(half_at.reshape(1), owner, adapter.reshape(1, rows), segment, cotangent)
 
 
-def send_kernel(columns, to_slot, marks, g_ref, tokens_hbm, sent_hbm, tokens, sent, *sems):
-    in_sems, out_sems = sems
-    width, out_width = tokens.shape[1], g_ref.shape[1]
-    parts = column_parts(width, columns)
+def send_kernel(to_slot, tokens_hbm, sent_hbm, tokens, sent, in_sems, out_sems):
+    parts = column_parts(tokens.shape[1], 1024)
     copies = [
         pltpu.make_async_copy(tokens_hbm.at[:, part], tokens.at[:, part], in_sems.at[at])
         for at, part in enumerate(parts)
@@ -434,57 +468,41 @@
     for copy in copies:
         copy.start()
     hot = to_slot[...]
-    last = slice(width + out_width, width + out_width + MARKS)
-    sent[:, width : width + out_width] = jnp.dot(
-        hot, g_ref[...], preferred_element_type=F32
-    ).astype(BF16)
-    sent[:, last] = lax.dot_general(
-        hot, marks[...], (((1,), (1,)), ((), ())), preferred_element_type=F32
-    ).astype(BF16)
     outs = []
-
-    def send(part):
+    for at, part in enumerate(parts):
+        copies[at].wait()
+        sent[:, part] = jnp.dot(hot, tokens[:, part], preferred_element_type=F32).astype(BF16)
         outs.append(
-            pltpu.make_async_copy(
-                sent.at[:, part], sent_hbm.at[:, part], out_sems.at[len(outs)]
-            )
+            pltpu.make_async_copy(sent.at[:, part], sent_hbm.at[:, part], out_sems.at[at])
         )
         outs[-1].start()
-
-    send(slice(width, width + out_width + MARKS))
-    for copy, part in zip(copies, parts):
-        copy.wait()
-        sent[:, part] = jnp.dot(hot, tokens[:, part], preferred_element_type=F32).astype(BF16)
-        send(part)
     for copy in outs:
         copy.wait()
 
 
-def send_rows(to_slot, marks, cotangent, tokens):
+def send_rows(to_slot, tokens):
     slots, (rows, width) = to_slot.shape[0], tokens.shape
-    columns = cotangent.shape[1]
-    full = width + columns + MARKS
-    n_parts = len(column_parts(width, columns))
+    n_parts = len(column_parts(width, 1024))
     vmem, hbm = pl.BlockSpec(memory_space=pltpu.VMEM), pl.BlockSpec(memory_space=pl.ANY)
     return pl.pallas_call(
-        functools.partial(send_kernel, columns),
-        out_shape=jax.ShapeDtypeStruct((slots, full), BF16),
-        in_specs=[vmem] * 3 + [hbm],
+        send_kernel,
+        out_shape=jax.ShapeDtypeStruct((slots, width), BF16),
+        in_specs=[vmem, hbm],
         out_specs=hbm,
         scratch_shapes=[
             pltpu.VMEM((rows, width), BF16),
-            pltpu.VMEM((slots, full), BF16),
+            pltpu.VMEM((slots, width), BF16),
             pltpu.SemaphoreType.DMA((n_parts,)),
-            pltpu.SemaphoreType.DMA((n_parts + 1,)),
+            pltpu.SemaphoreType.DMA((n_parts,)),
         ],
         compiler_params=pltpu.CompilerParams(vmem_limit_bytes=32 * 2**20),
         cost_estimate=pl.CostEstimate(
-            flops=2 * slots * rows * full,
-            bytes_accessed=2 * (slots + rows) * full,
+            flops=2 * slots * rows * width,
+            bytes_accessed=2 * (slots + rows) * width,
             transcendentals=0,
         ),
         name="send",
-    )(to_slot, marks, cotangent, tokens)
+    )(to_slot, tokens)
 
 
 def half_kernel(which_ref, up_hbm, down_hbm, out, sems):
@@ -552,10 +570,10 @@
 
     (owner,) = gate(lax.optimization_barrier((owner, half_mine))[0])
     row_seq = segment[0][:, None] == jnp.arange(seqs, dtype=jnp.int32)
-    to_slot, to_half, marks, sent_g = slot_rows(
+    to_slot, to_half, sent_g = slot_rows(
         me // half_size, owner, token_local_adapter, segment, cotangent, count, capacity, half_size
     )
-    sent = send_rows(to_slot, marks, cotangent, tokens)
+    sent = send_rows(to_slot, tokens)
 
     halves = [list(range(half_size)), list(range(half_size, n_dev))]
     to_half = to_half.reshape(half_size, 2, capacity, rows)
@@ -583,12 +601,12 @@
     landed_near = land(made_near)
     (sent,) = gate(lax.optimization_barrier((sent, made_near))[0])
     got = lax.all_to_all(
-        sent.reshape(n_dev, capacity, width + out_width + MARKS),
+        sent.reshape(n_dev, capacity, width),
         "ad",
         split_axis=0,
         concat_axis=0,
         tiled=True,
-    ).reshape(slots, width + out_width + MARKS)
+    ).reshape(slots, width)
 
     (which_far,) = gate(lax.optimization_barrier((which, sent, landed_near))[0])
     far_other = other_grp(far)
@@ -602,6 +620,17 @@
             for at in range(0, half_size // 2 * capacity, capacity)
         ]
     )
+    here = me // half_size
+    near_g = half_g[:, :capacity].reshape(-1, out_width + MARKS)
+    far_g = half_g[:, capacity:].reshape(-1, out_width + MARKS)
+    far_ups = far[:, :out_width], far_other[:, :out_width]
+    far_up = jnp.concatenate(
+        [jnp.where(grp == 0, *far_ups), jnp.where(grp == 0, *far_ups[::-1])]
+    )
+    near_rank = pull_rows(near_g, up, count, rank_size)
+    across_rank = flipped(pull_rows(far_g, far_up, count, rank_size), half_size)
+    across_g = flipped(lax.optimization_barrier((far_g, got))[0], half_size)
+
     pair_hot = pair_sequence_order[0][:, None] == jnp.arange(seqs, dtype=jnp.int32)
     at_me = (jnp.arange(n_dev, dtype=jnp.int32) == me)[:, None]
     own_scores = jnp.where(at_me, frozen_margin_score, 0.0).reshape(1, -1)
@@ -614,7 +643,9 @@
         ],
         axis=1,
     )
-    part, rank_rows = score(own, got, down, up, count, seqs, rank_size, n_dev)
+    part, hidden_rows = score(
+        here, own, near_rank, across_rank, got, down, count, seqs, n_dev
+    )
     told = lax.all_to_all(part, "ad", split_axis=0, concat_axis=0, tiled=True)
 
     chips = half_size // 2
@@ -626,19 +657,19 @@
     landed_far = lax.optimization_barrier((landed_far, told))[0]
     landed = hand_over(landed_near) + landed_far
     row_marks = jnp.pad(row_seq.astype(F32), ((0, 0), (count, MARKS - count - seqs)))
-    input_grad, grad_down, grad_up, losses = finish(
-        me,
+    input_grad, grad_down, upper, losses = finish(
+        jnp.stack([me, here]),
         told,
         got,
-        rank_rows,
+        [hidden_rows, near_rank, across_rank],
         row_marks,
         count,
         seqs,
-        width,
         pick,
         landed,
         [capacity] * chips + [chips * capacity] + [2 * capacity] * chips,
     )
+    grad_up = up_gradient(here, upper, near_g, across_g)
     return (
         input_grad,
         grad_down.reshape(count, rank_size, width),

time: 193 us -> 186 us (0.964)
  starting transfers between devices: 49 us -> 34.6 us
  Pallas kernels: 31.4 us -> 36.8 us
  waiting for transfers between devices: 92.9 us -> 88.7 us
  local copies, waits for them, and re-layouts: 12.8 us -> 16.4 us
    ppermute x9 -> x11, waiting for transfers between devices: 45.7 us -> 63.5 us  [flipped(): return lax.ppermute(block, 'ad', [(at, at ^ flip) for at in range(n_dev)])]
    all_to_all x1, waiting for transfers between devices: 27.9 us -> 14.6 us  [body(): lax.all_to_all(sent.reshape(n_dev, capacity, width), 'ad', split_axis=0,...]
    all_to_all x1, starting transfers between devices: 22.1 us -> 9.47 us  [body(): told = lax.all_to_all(part, 'ad', split_axis=0, concat_axis=0, tiled=True)]
    all_to_all x1, waiting for transfers between devices: 5.4 us -> 0.01 us  [body(): told = lax.all_to_all(part, 'ad', split_axis=0, concat_axis=0, tiled=True)]
    pallas_call x2 -> x5, Pallas kernels: 8.38 us -> 13.6 us  [the longest x1 4.8 us: score(): pl.pallas_call(functools.partial(score_kernel, count, seqs, slots // n_de...]
    all_to_all x1, waiting for transfers between devices: 14 us -> 10.5 us  [body(): lax.all_to_all(sent_g.reshape(half_size, 2 * capacity, out_width + MARKS)...]
    ppermute x9 -> x11, starting transfers between devices: 16.9 us -> 14.9 us  [flipped(): return lax.ppermute(block, 'ad', [(at, at ^ flip) for at in range(n_dev)])]
    unnamed x34 -> x32, local copies, waits for them, and re-layouts: 4.11 us -> 5.93 us
  transfers between devices with their start and end apart: 13 -> 15, of which waited for: 7 -> 9; matrix products, arithmetic and copies ran while one was open for 7% -> 10% of each run, Pallas kernels for 10% -> 16%
where the time goes in v8:
time: 186 us; the launch traced here: 185 us
  waiting for transfers between devices  88.7 us (48%)
  Pallas kernels  36.8 us (20%)
  starting transfers between devices  34.6 us (19%)
  local copies, waits for them, and re-layouts  16.4 us (9%)
  other arithmetic  7.56 us (4%)
    ppermute x11, waiting for transfers between devices, flipped(): return lax.ppermute(block, 'ad', [(at, at ^ flip) for at in range(n_dev)])  63.5 us
    ppermute x11, starting transfers between devices, flipped(): return lax.ppermute(block, 'ad', [(at, at ^ flip) for at in range(n_dev)])  14.9 us
    all_to_all x1, waiting for transfers between devices, body(): lax.all_to_all(sent.reshape(n_dev, capacity, width), 'ad', split_axis=0,...  14.6 us
    all_to_all x1, waiting for transfers between devices, body(): lax.all_to_all(sent_g.reshape(half_size, 2 * capacity, out_width + MARKS)...  10.5 us
    all_to_all x1, starting transfers between devices, body(): told = lax.all_to_all(part, 'ad', split_axis=0, concat_axis=0, tiled=True)  9.47 us
    pallas_call x2, Pallas kernels, project(): pl.pallas_call(functools.partial(project_kernel, side, split, capacity, o...  9.3 us
    pallas_call x1, Pallas kernels, finish(): pl.pallas_call(functools.partial(finish_kernel, count, seqs, slots // n_d...  6.64 us
    unnamed x32, local copies, waits for them, and re-layouts  5.93 us
  transfers between devices with their start and end apart: 15, of which 9 were waited for; matrix products, arithmetic and copies ran while one was open for 10% of the time, Pallas kernels for 16%

profile of v8, /device:TPU:0, one launch (start us, length us, event | category | flops | bytes accessed | tf_op | source)
XLA Modules:
  0.0 184.9 jit_solution(1652520536641936012)
XLA Ops:
  0.6 2.3 %half.2.refs_0_ = bf16[64,9216]{1,0:T(8,128)(2,1)} custom-call(s32[1]{0:T(128)} %bitcast.4.which_ref, bf16[2,64,1024]{2,1,0:T(8,128)(2,1)} %up_hbm.3, bf16[2,64,8192]{2,1,0:T(8,128)(2,1)} %down_hbm.3), custom_call_target="tpu_custom_call" | custom-call | tf_op jit(solution)/shard_map/half/pallas_call | solution.py:526
  3.0 4.1 %collective-permute-start = (bf16[64,9216]{1,0:T(8,128)(2,1)}, bf16[64,9216]{1,0:T(8,128)(2,1)}, u32[]{:S(2)}, u32[]{:S(2)}) collective-permute-start(bf16[64,9216]{1,0:T(8,128)(2,1)} %half.2.refs_0_), channel_id=1, source_target_pairs={{0,8},{1,9},{2,10},{3,11},{4,12},{5,13},{6,14},{7,15},{8,0},{9,1},... | collective-permute-start | bytes 3538952 | tf_op jit(solution)/shard_map/ppermute | solution.py:562
  7.8 2.5 %slots.1 = (bf16[256,128]{1,0:T(8,128)(2,1)}, bf16[256,128]{1,0:T(8,128)(2,1)}, bf16[256,1152]{1,0:T(8,128)(2,1)}) custom-call(s32[1]{0:T(128)} %bitcast.1.half_ref.here_ref, s32[128,1]{1,0:T(8,128)} %gate.3.owner_ref, s32[1,128]{1,0:T(1,128)} %bitcast.41, s32[1,128]{1,0:T(1,128)} %segment_ref.1, bf16[128,1024]{1,0:T(8,128)(2,1)} %g_ref.1), custom_call_target="tpu_custom_call" | custom-call | tf_op jit(solution)/shard_map/slots/pallas_call | solution.py:449
  10.4 3.8 %all-to-all-start = ((bf16[8,32,1152]{2,1,0:T(8,128)(2,1)}), bf16[8,32,1152]{2,1,0:T(8,128)(2,1)S(1)}, u32[]{:S(2)}, u32[]{:S(2)}) async-start(bf16[8,32,1152]{2,1,0:T(8,128)(2,1)} %bitcast.33), calls=%async_computation | async-start | bytes 1179648 | tf_op jit(solution)/shard_map/all_to_all | solution.py:580
  14.3 1.4 gather_fusion.1
  15.7 1.4 gather_fusion
  17.2 1.6 copy-done.2
  19.7 3.0 %send.1.refs_0_ = bf16[256,8192]{1,0:T(8,128)(2,1)S(1)} custom-call(bf16[256,128]{1,0:T(8,128)(2,1)S(1)} %copy-done.7, bf16[128,8192]{1,0:T(8,128)(2,1)S(1)} %copy-done.2), custom_call_target="tpu_custom_call" | custom-call | flops 536870912 | bytes 6291456 | tf_op jit(solution)/shard_map/send/pallas_call | solution.py:487
  22.7 2.0 %copy-done.1 = bf16[256,8192]{1,0:T(8,128)(2,1)} copy-done((bf16[256,8192]{1,0:T(8,128)(2,1)}, bf16[256,8192]{1,0:T(8,128)(2,1)S(1)}, u32[]{:S(2)}) %copy-start.1) | copy-done | bytes 4194328
  25.1 2.3 %half.3.refs_1_ = bf16[64,9216]{1,0:T(8,128)(2,1)} custom-call(s32[1]{0:T(128)} %bitcast.12.which_ref, bf16[2,64,1024]{2,1,0:T(8,128)(2,1)} %up_hbm.3, bf16[2,64,8192]{2,1,0:T(8,128)(2,1)} %down_hbm.3), custom_call_target="tpu_custom_call" | custom-call | tf_op jit(solution)/shard_map/half/pallas_call | solution.py:526
  28.5 10.5 %all-to-all-done.g_ref = bf16[8,32,1152]{2,1,0:T(8,128)(2,1)S(1)} async-done(((bf16[8,32,1152]{2,1,0:T(8,128)(2,1)}), bf16[8,32,1152]{2,1,0:T(8,128)(2,1)S(1)}, u32[]{:S(2)}, u32[]{:S(2)}) %all-to-all-start) | async-done | bytes 589856 | tf_op jit(solution)/shard_map/all_to_all | solution.py:580
  39.8 4.6 %project.2 = (bf16[32,8192]{1,0:T(8,128)(2,1)}, bf16[32,8192]{1,0:T(8,128)(2,1)}, bf16[32,8192]{1,0:T(8,128)(2,1)}, bf16[32,8192]{1,0:T(8,128)(2,1)}) custom-call(s32[1]{0:T(128)} %bitcast.11.spot_ref, bf16[8,32,1152]{2,1,0:T(8,128)(2,1)} %copy-done.9, f32[2,128]{1,0:T(2,128)} %compare_convert_fusion.which.refs_0_, bf16[64,9216]{1,0:T(8,128)(2,1)} %half.2.refs_0_, ...), custom_call_target="tpu_custom_call" | custom-call | flops 1000 | bytes 1000 | tf_op jit(solution)/shard_map/project/pallas_call | solution.py:75
  44.4 1.5 collective-permute-start.3
  46.0 2.4 %collective-permute-start.4 = (bf16[32,8192]{1,0:T(8,128)(2,1)}, bf16[32,8192]{1,0:T(8,128)(2,1)}, u32[]{:S(2)}, u32[]{:S(2)}) collective-permute-start(bf16[32,8192]{1,0:T(8,128)(2,1)} %get-tuple-element.32), channel_id=1, source_target_pairs={{0,4},{1,5},{2,6},{3,7},{4,0},{5,1},{6,2},{7,3},{8,12},{9,13},{10,... | collective-permute-start | bytes 1572872 | tf_op jit(solution)/shard_map/ppermute | solution.py:562
  48.3 4.7 %all-to-all-start.1 = ((bf16[16,16,8192]{2,1,0:T(8,128)(2,1)}), bf16[16,16,8192]{2,1,0:T(8,128)(2,1)}, u32[]{:S(2)}, u32[]{:S(2)}) async-start(bf16[16,16,8192]{2,1,0:T(8,128)(2,1)} %bitcast.26), calls=%async_computation.1 | async-start | bytes 8388608 | tf_op jit(solution)/shard_map/all_to_all | solution.py:603
  53.9 1.9 %pull.2.near_ref.refs_2_ = bf16[128,256]{1,0:T(8,128)(2,1)} custom-call(bf16[128,1152]{1,0:T(8,128)(2,1)} %bitcast.28, bf16[128,1024]{1,0:T(8,128)(2,1)} %bitcast.30), custom_call_target="tpu_custom_call" | custom-call | flops 1000 | bytes 1000 | tf_op jit(solution)/shard_map/pull/pallas_call | solution.py:131
  55.8 3.7 %collective-permute-done.refs_0_ = bf16[64,9216]{1,0:T(8,128)(2,1)} collective-permute-done((bf16[64,9216]{1,0:T(8,128)(2,1)}, bf16[64,9216]{1,0:T(8,128)(2,1)}, u32[]{:S(2)}, u32[]{:S(2)}) %collective-permute-start) | collective-permute-done | bytes 1179680 | tf_op jit(solution)/shard_map/ppermute | solution.py:562
  59.6 1.8 collective-permute-start.1
  62.4 30.1 %collective-permute-done.4.refs_8_ = bf16[32,8192]{1,0:T(8,128)(2,1)} collective-permute-done((bf16[32,8192]{1,0:T(8,128)(2,1)}, bf16[32,8192]{1,0:T(8,128)(2,1)}, u32[]{:S(2)}, u32[]{:S(2)}) %collective-permute-start.4) | collective-permute-done | bytes 524320 | tf_op jit(solution)/shard_map/ppermute | solution.py:562
  93.4 15.7 %collective-permute-done.5.refs_9_ = bf16[32,8192]{1,0:T(8,128)(2,1)} collective-permute-done((bf16[32,8192]{1,0:T(8,128)(2,1)}, bf16[32,8192]{1,0:T(8,128)(2,1)}, u32[]{:S(2)}, u32[]{:S(2)}) %collective-permute-start.5) | collective-permute-done | bytes 524320 | tf_op jit(solution)/shard_map/ppermute | solution.py:562
  112.8 1.9 %pull.3 = bf16[128,256]{1,0:T(8,128)(2,1)} custom-call(bf16[128,1152]{1,0:T(8,128)(2,1)} %bitcast.31, bf16[128,1024]{1,0:T(8,128)(2,1)} %pad_maximum_fusion.5.up), custom_call_target="tpu_custom_call" | custom-call | flops 1000 | bytes 1000 | tf_op jit(solution)/shard_map/pull/pallas_call | solution.py:131
  114.7 4.7 %project.3 = (bf16[64,8192]{1,0:T(8,128)(2,1)}, bf16[64,8192]{1,0:T(8,128)(2,1)}) custom-call(s32[1]{0:T(128)} %bitcast.11.spot_ref, bf16[8,32,1152]{2,1,0:T(8,128)(2,1)} %copy-done.9, f32[2,128]{1,0:T(2,128)} %gate.5.which, bf16[64,9216]{1,0:T(8,128)(2,1)} %collective-permute-done.refs_0_, bf16[64,9216]{1,0:T(8,128)(2,1)} %collective-permute-done.1.refs_1_), custom_call_target="tpu_custom_call" | custom-call | flops 1000 | bytes 1000 | tf_op jit(solution)/shard_map/project/pallas_call | solution.py:75
  119.9 2.0 %fusion.10 = (bf16[16,8192]{1,0:T(8,128)(2,1)S(1)}, bf16[16,8192]{1,0:T(8,128)(2,1)S(1)}, bf16[16,8192]{1,0:T(8,128)(2,1)S(1)}, bf16[16,8192]{1,0:T(8,128)(2,1)}) fusion(bf16[64,8192]{1,0:T(8,128)(2,1)} %get-tuple-element.39), kind=kLoop, calls=%fused_computation.32 | loop fusion | bytes 2097152 | tf_op jit(solution)/shard_map/slice | solution.py:619
  125.8 3.5 %collective-permute-start.10 = (bf16[32,8192]{1,0:T(8,128)(2,1)}, bf16[32,8192]{1,0:T(8,128)(2,1)}, u32[]{:S(2)}, u32[]{:S(2)}) collective-permute-start(bf16[32,8192]{1,0:T(8,128)(2,1)} %pad_maximum_fusion.4), channel_id=1, source_target_pairs={{0,6},{1,7},{2,4},{3,5},{4,2},{5,3},{6,0},{7,1},{8,14},{9,15},{10,... | collective-permute-start | bytes 1572872 | tf_op jit(solution)/shard_map/ppermute | solution.py:562
  129.3 14.6 %all-to-all-done.1 = bf16[16,16,8192]{2,1,0:T(8,128)(2,1)} async-done(((bf16[16,16,8192]{2,1,0:T(8,128)(2,1)}), bf16[16,16,8192]{2,1,0:T(8,128)(2,1)}, u32[]{:S(2)}, u32[]{:S(2)}) %all-to-all-start.1) | async-done | bytes 4194336 | tf_op jit(solution)/shard_map/all_to_all | solution.py:603
  143.9 7.6 %collective-permute-done.2.across_ref.refs_3_ = bf16[128,256]{1,0:T(8,128)(2,1)S(1)} collective-permute-done((bf16[128,256]{1,0:T(8,128)(2,1)}, bf16[128,256]{1,0:T(8,128)(2,1)S(1)}, u32[]{:S(2)}, u32[]{:S(2)}) %collective-permute-start.2) | collective-permute-done | bytes 65568 | tf_op jit(solution)/shard_map/ppermute | solution.py:562
  151.5 4.8 %score.1 = (f32[16,1,256]{2,1,0:T(1,128)}, bf16[256,128]{1,0:T(8,128)(2,1)}) custom-call(s32[1]{0:T(128)} %bitcast.1.half_ref.here_ref, f32[1,256]{1,0:T(1,128)S(1)} %fusion.3.own_ref, bf16[128,256]{1,0:T(8,128)(2,1)S(1)} %copy-done.5, bf16[128,256]{1,0:T(8,128)(2,1)S(1)} %collective-permute-done.2.across_ref.refs_3_, bf16[128,8192]{1,0:T(8,128)(2,1)S(1)} %bitcast.25, ...), custom_call_target="tpu_custom_call" | custom-call | flops 536870912 | bytes 6291456 | tf_op jit(solution)/shard_map/score/pallas_call | solution.py:198
  156.3 9.5 %all-to-all-start.2 = ((f32[16,1,256]{2,1,0:T(1,128)}), f32[16,1,256]{2,1,0:T(1,128)S(1)}, u32[]{:S(2)}, u32[]{:S(2)}) async-start(f32[16,1,256]{2,1,0:T(1,128)} %get-tuple-element.35), calls=%async_computation.2 | async-start | bytes 32768 | tf_op jit(solution)/shard_map/all_to_all | solution.py:649
  165.8 2.8 %collective-permute-start.11 = (bf16[128,1152]{1,0:T(8,128)(2,1)}, bf16[128,1152]{1,0:T(8,128)(2,1)}, u32[]{:S(2)}, u32[]{:S(2)}) collective-permute-start(bf16[128,1152]{1,0:T(8,128)(2,1)} %bitcast.32), channel_id=1, source_target_pairs={{0,8},{1,9},{2,10},{3,11},{4,12},{5,13},{6,14},{7,15},{8,0},{9,1},... | collective-permute-start | bytes 884744 | tf_op jit(solution)/shard_map/ppermute | solution.py:562
  169.7 4.7 %collective-permute-done.10.refs_14_ = bf16[32,8192]{1,0:T(8,128)(2,1)} collective-permute-done((bf16[32,8192]{1,0:T(8,128)(2,1)}, bf16[32,8192]{1,0:T(8,128)(2,1)}, u32[]{:S(2)}, u32[]{:S(2)}) %collective-permute-start.10) | collective-permute-done | bytes 524320 | tf_op jit(solution)/shard_map/ppermute | solution.py:562
  174.4 6.6 %finish.1 = (f32[2]{0:T(128)}, f32[128,1]{1,0:T(8,128)}, bf16[256,128]{1,0:T(8,128)(2,1)S(1)}, bf16[128,8192]{1,0:T(8,128)(2,1)}, bf16[128,8192]{1,0:T(8,128)(2,1)}) custom-call(s32[2]{0:T(128)S(1)} %pad_add_fusion.place_ref, f32[16,1,256]{2,1,0:T(1,128)S(1)} %all-to-all-done.2.told_ref, f32[128,128]{1,0:T(8,128)S(1)} %pad_convert_fusion.refs_0_, ...), custom_call_target="tpu_custom_call" | custom-call | flops 1073741824 | bytes 12582912 | tf_op jit(solution)/shard_map/finish/pallas_call | solution.py:366
  182.9 2.0 %up.1 = bf16[128,1024]{1,0:T(8,128)(2,1)} custom-call(s32[1]{0:T(128)} %bitcast.1.half_ref.here_ref, bf16[256,128]{1,0:T(8,128)(2,1)} %copy-done.8, bf16[128,1152]{1,0:T(8,128)(2,1)} %bitcast.29, bf16[128,1152]{1,0:T(8,128)(2,1)} %collective-permute-done.11.across_g), custom_call_target="tpu_custom_call" | custom-call | flops 75497472 | bytes 589824 | tf_op jit(solution)/shard_map/up/pallas_call | solution.py:399
  (80 shorter events, 17.8 us)
Async XLA Ops:
  0.6 6.5 %copy-start.12 = (s32[128,1]{0,1:T(1,128)S(1)}, s32[128,1]{0,1:T(1,128)}, u32[]{:S(2)}) copy-start(s32[128,1]{0,1:T(1,128)} %param.12) | copy-start | bytes 1540
  3.0 56.6 %collective-permute-start = (bf16[64,9216]{1,0:T(8,128)(2,1)}, bf16[64,9216]{1,0:T(8,128)(2,1)}, u32[]{:S(2)}, u32[]{:S(2)}) collective-permute-start(bf16[64,9216]{1,0:T(8,128)(2,1)} %half.2.refs_0_), channel_id=1, source_target_pairs={{0,8},{1,9},{2,10},{3,11},{4,12},{5,13},{6,14},{7,15},{8,0},{9,1},... | collective-permute-start | bytes 3538952 | tf_op jit(solution)/shard_map/ppermute | solution.py:562
  7.8 6.4 %copy-start.15 = (s32[8]{0:T(128)S(1)}, s32[8]{0:T(128)}, u32[]{:S(2)}) copy-start(s32[8]{0:T(128)} %constant.52.clone) | copy-start | bytes 100
  7.8 6.4 %copy-start.13 = (s32[1,4]{1,0:T(1,128)S(1)}, s32[1,4]{1,0:T(1,128)}, u32[]{:S(2)}) copy-start(s32[1,4]{1,0:T(1,128)} %param.15) | copy-start | bytes 52
  7.8 9.3 %copy-start.14 = (f32[1,4]{1,0:T(1,128)S(1)}, f32[1,4]{1,0:T(1,128)}, u32[]{:S(2)}) copy-start(f32[1,4]{1,0:T(1,128)} %param.16) | copy-start | bytes 52
  10.4 28.6 %all-to-all-start = ((bf16[8,32,1152]{2,1,0:T(8,128)(2,1)}), bf16[8,32,1152]{2,1,0:T(8,128)(2,1)S(1)}, u32[]{:S(2)}, u32[]{:S(2)}) async-start(bf16[8,32,1152]{2,1,0:T(8,128)(2,1)} %bitcast.33), calls=%async_computation | async-start | bytes 1179648 | tf_op jit(solution)/shard_map/all_to_all | solution.py:580
  17.2 1.6 copy-start.2
  18.8 0.8 copy-start.7
  22.7 2.0 %copy-start.1 = (bf16[256,8192]{1,0:T(8,128)(2,1)}, bf16[256,8192]{1,0:T(8,128)(2,1)S(1)}, u32[]{:S(2)}) copy-start(bf16[256,8192]{1,0:T(8,128)(2,1)S(1)} %send.1.refs_0_) | copy-start | bytes 12582916
  24.7 2.9 %copy-start.11 = (s32[1,128]{1,0:T(1,128)S(1)}, s32[1,128]{1,0:T(1,128)}, u32[]{:S(2)}) copy-start(s32[1,128]{1,0:T(1,128)} %segment_ref.1) | copy-start | bytes 1540
  39.0 0.8 copy-start.9
  44.4 17.0 %collective-permute-start.3 = (bf16[32,8192]{1,0:T(8,128)(2,1)}, bf16[32,8192]{1,0:T(8,128)(2,1)}, u32[]{:S(2)}, u32[]{:S(2)}) collective-permute-start(bf16[32,8192]{1,0:T(8,128)(2,1)} %get-tuple-element.31), channel_id=1, source_target_pairs={{0,2},{1,3},{2,0},{3,1},{4,6},{5,7},{6,4},{7,5},{8,10},{9,11},{10,... | collective-permute-start | bytes 1572872 | tf_op jit(solution)/shard_map/ppermute | solution.py:562
  46.0 46.5 %collective-permute-start.4 = (bf16[32,8192]{1,0:T(8,128)(2,1)}, bf16[32,8192]{1,0:T(8,128)(2,1)}, u32[]{:S(2)}, u32[]{:S(2)}) collective-permute-start(bf16[32,8192]{1,0:T(8,128)(2,1)} %get-tuple-element.32), channel_id=1, source_target_pairs={{0,4},{1,5},{2,6},{3,7},{4,0},{5,1},{6,2},{7,3},{8,12},{9,13},{10,... | collective-permute-start | bytes 1572872 | tf_op jit(solution)/shard_map/ppermute | solution.py:562
  48.3 60.8 %collective-permute-start.5 = (bf16[32,8192]{1,0:T(8,128)(2,1)}, bf16[32,8192]{1,0:T(8,128)(2,1)}, u32[]{:S(2)}, u32[]{:S(2)}) collective-permute-start(bf16[32,8192]{1,0:T(8,128)(2,1)} %get-tuple-element.33), channel_id=1, source_target_pairs={{0,6},{1,7},{2,4},{3,5},{4,2},{5,3},{6,0},{7,1},{8,14},{9,15},{10,... | collective-permute-start | bytes 1572872 | tf_op jit(solution)/shard_map/ppermute | solution.py:562
  48.3 4.7 %copy-start.10 = (bf16[8,32,1152]{2,1,0:T(8,128)(2,1)S(1)}, bf16[8,32,1152]{2,1,0:T(8,128)(2,1)}, u32[]{:S(2)}) copy-start(bf16[8,32,1152]{2,1,0:T(8,128)(2,1)} %copy-done.9) | copy-start | bytes 1769476
  48.3 7.5 %copy-start.3 = (bf16[32,8192]{1,0:T(8,128)(2,1)S(1)}, bf16[32,8192]{1,0:T(8,128)(2,1)}, u32[]{:S(2)}) copy-start(bf16[32,8192]{1,0:T(8,128)(2,1)} %get-tuple-element.30.refs_6_) | copy-start | bytes 1572868
  48.3 95.5 %all-to-all-start.1 = ((bf16[16,16,8192]{2,1,0:T(8,128)(2,1)}), bf16[16,16,8192]{2,1,0:T(8,128)(2,1)}, u32[]{:S(2)}, u32[]{:S(2)}) async-start(bf16[16,16,8192]{2,1,0:T(8,128)(2,1)} %bitcast.26), calls=%async_computation.1 | async-start | bytes 8388608 | tf_op jit(solution)/shard_map/all_to_all | solution.py:603
  59.6 51.5 %collective-permute-start.1 = (bf16[64,9216]{1,0:T(8,128)(2,1)}, bf16[64,9216]{1,0:T(8,128)(2,1)}, u32[]{:S(2)}, u32[]{:S(2)}) collective-permute-start(bf16[64,9216]{1,0:T(8,128)(2,1)} %collective-permute-done.refs_0_), channel_id=1, source_target_pairs={{0,16},{16,0},{1,17},{17,1},{2,18},{18,2},{3,19},{19,3},{4,20},{20... | collective-permute-start | bytes 3538952 | tf_op jit(solution)/shard_map/ppermute | solution.py:565
  111.1 63.3 %collective-permute-start.6 = (bf16[64,8192]{1,0:T(8,128)(2,1)}, bf16[64,8192]{1,0:T(8,128)(2,1)}, u32[]{:S(2)}, u32[]{:S(2)}) collective-permute-start(bf16[64,8192]{1,0:T(8,128)(2,1)} %pad_maximum_fusion), channel_id=1, source_target_pairs={{0,1},{1,0},{2,3},{3,2},{4,5},{5,4},{6,7},{7,6},{8,9},{9,8},{10,11... | collective-permute-start | bytes 3145736 | tf_op jit(solution)/shard_map/ppermute | solution.py:562
  114.7 36.7 %collective-permute-start.2 = (bf16[128,256]{1,0:T(8,128)(2,1)}, bf16[128,256]{1,0:T(8,128)(2,1)S(1)}, u32[]{:S(2)}, u32[]{:S(2)}) collective-permute-start(bf16[128,256]{1,0:T(8,128)(2,1)} %pull.3), channel_id=1, source_target_pairs={{0,8},{1,9},{2,10},{3,11},{4,12},{5,13},{6,14},{7,15},{8,0},{9,1},... | collective-permute-start | bytes 196616 | tf_op jit(solution)/shard_map/ppermute | solution.py:562
  119.4 3.0 %collective-permute-start.7 = (bf16[64,8192]{1,0:T(8,128)(2,1)}, bf16[64,8192]{1,0:T(8,128)(2,1)S(1)}, u32[]{:S(2)}, u32[]{:S(2)}) collective-permute-start(bf16[64,8192]{1,0:T(8,128)(2,1)} %get-tuple-element.40), channel_id=1, source_target_pairs={{0,1},{1,0},{2,3},{3,2},{4,5},{5,4},{6,7},{7,6},{8,9},{9,8},{10,11... | collective-permute-start | bytes 3145736 | tf_op jit(solution)/shard_map/ppermute | solution.py:562
  123.2 28.3 %copy-start = (bf16[2,64,8192]{2,1,0:T(8,128)(2,1)S(1)}, bf16[2,64,8192]{2,1,0:T(8,128)(2,1)}, u32[]{:S(2)}) copy-start(bf16[2,64,8192]{2,1,0:T(8,128)(2,1)} %down_hbm.3) | copy-start | bytes 6291460
  123.2 28.3 %copy-start.5 = (bf16[128,256]{1,0:T(8,128)(2,1)S(1)}, bf16[128,256]{1,0:T(8,128)(2,1)}, u32[]{:S(2)}) copy-start(bf16[128,256]{1,0:T(8,128)(2,1)} %pull.2.near_ref.refs_2_) | copy-start | bytes 196612
  124.0 45.6 %collective-permute-start.8 = (bf16[32,8192]{1,0:T(8,128)(2,1)}, bf16[32,8192]{1,0:T(8,128)(2,1)S(1)}, u32[]{:S(2)}, u32[]{:S(2)}) collective-permute-start(bf16[32,8192]{1,0:T(8,128)(2,1)} %pad_maximum_fusion.2), channel_id=1, source_target_pairs={{0,2},{1,3},{2,0},{3,1},{4,6},{5,7},{6,4},{7,5},{8,10},{9,11},{10,... | collective-permute-start | bytes 1572872 | tf_op jit(solution)/shard_map/ppermute | solution.py:562
  124.9 44.8 %collective-permute-start.9 = (bf16[32,8192]{1,0:T(8,128)(2,1)}, bf16[32,8192]{1,0:T(8,128)(2,1)}, u32[]{:S(2)}, u32[]{:S(2)}) collective-permute-start(bf16[32,8192]{1,0:T(8,128)(2,1)} %pad_maximum_fusion.3), channel_id=1, source_target_pairs={{0,4},{1,5},{2,6},{3,7},{4,0},{5,1},{6,2},{7,3},{8,12},{9,13},{10,... | collective-permute-start | bytes 1572872 | tf_op jit(solution)/shard_map/ppermute | solution.py:562
  125.8 48.6 %collective-permute-start.10 = (bf16[32,8192]{1,0:T(8,128)(2,1)}, bf16[32,8192]{1,0:T(8,128)(2,1)}, u32[]{:S(2)}, u32[]{:S(2)}) collective-permute-start(bf16[32,8192]{1,0:T(8,128)(2,1)} %pad_maximum_fusion.4), channel_id=1, source_target_pairs={{0,6},{1,7},{2,4},{3,5},{4,2},{5,3},{6,0},{7,1},{8,14},{9,15},{10,... | collective-permute-start | bytes 1572872 | tf_op jit(solution)/shard_map/ppermute | solution.py:562
  151.5 4.8 %copy-start.6 = (bf16[128,256]{1,0:T(8,128)(2,1)}, bf16[128,256]{1,0:T(8,128)(2,1)S(1)}, u32[]{:S(2)}) copy-start(bf16[128,256]{1,0:T(8,128)(2,1)S(1)} %collective-permute-done.2.across_ref.refs_3_) | copy-start | bytes 196612
  151.5 22.9 %copy-start.4 = (bf16[32,8192]{1,0:T(8,128)(2,1)S(1)}, bf16[32,8192]{1,0:T(8,128)(2,1)}, u32[]{:S(2)}) copy-start(bf16[32,8192]{1,0:T(8,128)(2,1)} %get-tuple-element.30.refs_6_) | copy-start | bytes 1572868
  156.3 18.1 %all-to-all-start.2 = ((f32[16,1,256]{2,1,0:T(1,128)}), f32[16,1,256]{2,1,0:T(1,128)S(1)}, u32[]{:S(2)}, u32[]{:S(2)}) async-start(f32[16,1,256]{2,1,0:T(1,128)} %get-tuple-element.35), calls=%async_computation.2 | async-start | bytes 32768 | tf_op jit(solution)/shard_map/all_to_all | solution.py:649
  165.8 17.1 %collective-permute-start.11 = (bf16[128,1152]{1,0:T(8,128)(2,1)}, bf16[128,1152]{1,0:T(8,128)(2,1)}, u32[]{:S(2)}, u32[]{:S(2)}) collective-permute-start(bf16[128,1152]{1,0:T(8,128)(2,1)} %bitcast.32), channel_id=1, source_target_pairs={{0,8},{1,9},{2,10},{3,11},{4,12},{5,13},{6,14},{7,15},{8,0},{9,1},... | collective-permute-start | bytes 884744 | tf_op jit(solution)/shard_map/ppermute | solution.py:562
  181.1 0.6 copy-start.8

commit v9 on v8

--- a/solution.py
+++ b/solution.py
@@ -248,7 +248,7 @@
     if used:
         pick, *refs = refs
     block_hbms, refs = refs[: len(used)], refs[len(used) :]
-    losses_ref, row_weight, upper_ref, down_hbm, *refs = refs
+    losses_ref, row_weight, upper_hbm, down_hbm, *refs, upper, upper_sem = refs
     if used:
         input_hbm, *smalls = refs[:4]
         got, grad_down, rows, input_grad, *sems = refs[4:]
@@ -306,10 +306,11 @@
     both = in_slots(here, near_rank.astype(F32), across_rank.astype(F32))
     pulled, marks = both[:, :lanes], both[:, lanes:]
     weight = jnp.sum(marks * slot_table, axis=1, keepdims=True)
-    upper_ref[...] = (weight * hidden.astype(F32)).astype(BF16)
+    upper[...] = (weight * hidden.astype(F32)).astype(BF16)
     lower = (weight * pulled).astype(BF16)
     contract = (((0,), (0,)), ((), ()))
-    outs = []
+    outs = [pltpu.make_async_copy(upper, upper_hbm, upper_sem)]
+    outs[0].start()
     for at, part in enumerate(parts):
         copies[at].wait()
         made = lax.dot_general(lower, got[:, part], contract, preferred_element_type=F32)
@@ -345,7 +346,7 @@
     out_shape = [
         jax.ShapeDtypeStruct((seqs // 2,), F32),
         jax.ShapeDtypeStruct((rows, 1), F32),
-        jax.ShapeDtypeStruct((slots, lanes), BF16),
+        pltpu.HBM((slots, lanes), BF16),
         jax.ShapeDtypeStruct((lanes, width), BF16),
     ]
     in_specs = [pl.BlockSpec(memory_space=pltpu.SMEM)] + [vmem] * 2 + [hbm] * 4
@@ -369,8 +370,8 @@
         ),
         out_shape=out_shape,
         in_specs=in_specs,
-        out_specs=[pl.BlockSpec(memory_space=pltpu.SMEM), vmem, vmem] + [hbm] * (len(out_shape) - 3),
-        scratch_shapes=scratch + scratch_sems,
+        out_specs=[pl.BlockSpec(memory_space=pltpu.SMEM), vmem] + [hbm] * (len(out_shape) - 2),
+        scratch_shapes=scratch + scratch_sems + [pltpu.VMEM((slots, lanes), BF16), sems],
         compiler_params=pltpu.CompilerParams(vmem_limit_bytes=24 * 2**20),
         cost_estimate=pl.CostEstimate(
             flops=4 * slots * lanes * width,
@@ -386,24 +387,49 @@
     return input_grad[0], grad_down, upper, losses
 
 
-def up_kernel(here_ref, upper, near_g, across_g, out):
-    out_width = out.shape[1]
+def up_kernel(here_ref, upper_hbm, near_hbm, across_hbm, out, upper, near, across, sems):
+    copies = [
+        pltpu.make_async_copy(near_hbm.at[:, pl.ds(0, out.shape[1])], near, sems.at[0]),
+        pltpu.make_async_copy(across_hbm, across, sems.at[1]),
+        pltpu.make_async_copy(upper_hbm, upper, sems.at[2]),
+    ]
+    for copy in copies:
+        copy.start()
+    size = near.shape[0]
+    copies[2].wait()
+    first, second = upper[:size, :].astype(F32), upper[size:, :].astype(F32)
+    here = here_ref[0]
+    near_upper = jnp.where(here == 0, first, second).astype(BF16)
+    across_upper = jnp.where(here == 0, second, first).astype(BF16)
     contract = (((0,), (0,)), ((), ()))
-    g_rows = in_slots(here_ref[0], near_g[:, :out_width], across_g[:, :out_width])
-    made = lax.dot_general(upper[...], g_rows, contract, preferred_element_type=F32)
+    copies[0].wait()
+    made = lax.dot_general(near_upper, near[...], contract, preferred_element_type=F32)
+    copies[1].wait()
+    made = made + lax.dot_general(
+        across_upper, across[...], contract, preferred_element_type=F32
+    )
     out[...] = (SCALE * made).astype(BF16)
 
 
 def up_gradient(here, upper, near_g, across_g):
-    vmem = pl.BlockSpec(memory_space=pltpu.VMEM)
+    vmem, hbm = pl.BlockSpec(memory_space=pltpu.VMEM), pl.BlockSpec(memory_space=pltpu.HBM)
+    upper = pltpu.with_memory_space_constraint(upper, pltpu.HBM)
+    near_g = pltpu.with_memory_space_constraint(near_g, pltpu.HBM)
+    across_g = pltpu.with_memory_space_constraint(across_g, pltpu.HBM)
     return pl.pallas_call(
         up_kernel,
-        out_shape=jax.ShapeDtypeStruct((upper.shape[1], near_g.shape[1] - MARKS), BF16),
-        in_specs=[pl.BlockSpec(memory_space=pltpu.SMEM)] + [vmem] * 3,
+        out_shape=jax.ShapeDtypeStruct((upper.shape[1], across_g.shape[1]), BF16),
+        in_specs=[pl.BlockSpec(memory_space=pltpu.SMEM), hbm, hbm, hbm],
         out_specs=vmem,
+        scratch_shapes=[
+            pltpu.VMEM(upper.shape, BF16),
+            pltpu.VMEM(across_g.shape, BF16),
+            pltpu.VMEM(across_g.shape, BF16),
+            pltpu.SemaphoreType.DMA((3,)),
+        ],
         cost_estimate=pl.CostEstimate(
-            flops=2 * upper.shape[0] * upper.shape[1] * near_g.shape[1],
-            bytes_accessed=4 * near_g.shape[0] * near_g.shape[1],
+            flops=2 * upper.shape[0] * upper.shape[1] * across_g.shape[1],
+            bytes_accessed=4 * across_g.shape[0] * across_g.shape[1],
             transcendentals=0,
         ),
         name="up",
@@ -599,7 +625,7 @@
         0, False, capacity, out_width, width, spot, half_g, which, [half_mine], [half_other]
     )
     landed_near = land(made_near)
-    (sent,) = gate(lax.optimization_barrier((sent, made_near))[0])
+    (sent,) = gate(lax.optimization_barrier((sent, half_g))[0])
     got = lax.all_to_all(
         sent.reshape(n_dev, capacity, width),
         "ad",
@@ -629,7 +655,7 @@
     )
     near_rank = pull_rows(near_g, up, count, rank_size)
     across_rank = flipped(pull_rows(far_g, far_up, count, rank_size), half_size)
-    across_g = flipped(lax.optimization_barrier((far_g, got))[0], half_size)
+    across_g = flipped(lax.optimization_barrier((far_g[:, :out_width], got))[0], half_size)
 
     pair_hot = pair_sequence_order[0][:, None] == jnp.arange(seqs, dtype=jnp.int32)
     at_me = (jnp.arange(n_dev, dtype=jnp.int32) == me)[:, None]

time: 186 us -> 184 us (0.989)
    unnamed x32 -> x34, local copies, waits for them, and re-layouts: 5.93 us -> 5.32 us
where the time goes in v9:
time: 184 us
  waiting for transfers between devices  87.2 us (47%)
  Pallas kernels  36.9 us (20%)
  starting transfers between devices  34.6 us (19%)
  local copies, waits for them, and re-layouts  16.4 us (9%)
  other arithmetic  7.55 us (4%)
    ppermute x11, waiting for transfers between devices, flipped(): return lax.ppermute(block, 'ad', [(at, at ^ flip) for at in range(n_dev)])  62.1 us
    ppermute x11, starting transfers between devices, flipped(): return lax.ppermute(block, 'ad', [(at, at ^ flip) for at in range(n_dev)])  14.8 us
    all_to_all x1, waiting for transfers between devices, body(): lax.all_to_all(sent.reshape(n_dev, capacity, width), 'ad', split_axis=0,...  14.6 us
    all_to_all x1, waiting for transfers between devices, body(): lax.all_to_all(sent_g.reshape(half_size, 2 * capacity, out_width + MARKS)...  10.5 us
    all_to_all x1, starting transfers between devices, body(): told = lax.all_to_all(part, 'ad', split_axis=0, concat_axis=0, tiled=True)  9.46 us
    pallas_call x2, Pallas kernels, project(): pl.pallas_call(functools.partial(project_kernel, side, split, capacity, o...  9.29 us
    pallas_call x1, Pallas kernels, finish(): pl.pallas_call(functools.partial(finish_kernel, count, seqs, slots // n_d...  6.65 us
    unnamed x34, local copies, waits for them, and re-layouts  5.32 us
  transfers between devices with their start and end apart: 15, of which 9 were waited for; matrix products, arithmetic and copies ran while one was open for 10% of the time, Pallas kernels for 16%

profile of v9, /device:TPU:0, one launch (start us, length us, event | category | flops | bytes accessed | tf_op | source)
XLA Modules:
  0.0 183.6 jit_solution(6140390898436987251)
XLA Ops:
  0.6 2.3 %half.2.refs_0_ = bf16[64,9216]{1,0:T(8,128)(2,1)} custom-call(s32[1]{0:T(128)} %bitcast.4.which_ref, bf16[2,64,1024]{2,1,0:T(8,128)(2,1)} %up_hbm.3, bf16[2,64,8192]{2,1,0:T(8,128)(2,1)} %down_hbm.3), custom_call_target="tpu_custom_call" | custom-call | tf_op jit(solution)/shard_map/half/pallas_call | solution.py:552
  3.0 4.1 %collective-permute-start = (bf16[64,9216]{1,0:T(8,128)(2,1)}, bf16[64,9216]{1,0:T(8,128)(2,1)}, u32[]{:S(2)}, u32[]{:S(2)}) collective-permute-start(bf16[64,9216]{1,0:T(8,128)(2,1)} %half.2.refs_0_), channel_id=1, source_target_pairs={{0,8},{1,9},{2,10},{3,11},{4,12},{5,13},{6,14},{7,15},{8,0},{9,1},... | collective-permute-start | bytes 3538952 | tf_op jit(solution)/shard_map/ppermute | solution.py:588
  7.8 2.5 %slots.1 = (bf16[256,128]{1,0:T(8,128)(2,1)}, bf16[256,128]{1,0:T(8,128)(2,1)}, bf16[256,1152]{1,0:T(8,128)(2,1)}) custom-call(s32[1]{0:T(128)} %bitcast.1.half_ref.here_ref, s32[128,1]{1,0:T(8,128)} %gate.3.owner_ref, s32[1,128]{1,0:T(1,128)} %bitcast.41, s32[1,128]{1,0:T(1,128)} %segment_ref.1, bf16[128,1024]{1,0:T(8,128)(2,1)} %g_ref.1), custom_call_target="tpu_custom_call" | custom-call | tf_op jit(solution)/shard_map/slots/pallas_call | solution.py:475
  10.3 3.8 %all-to-all-start = ((bf16[8,32,1152]{2,1,0:T(8,128)(2,1)}), bf16[8,32,1152]{2,1,0:T(8,128)(2,1)S(1)}, u32[]{:S(2)}, u32[]{:S(2)}) async-start(bf16[8,32,1152]{2,1,0:T(8,128)(2,1)} %bitcast.33), calls=%async_computation | async-start | bytes 1179648 | tf_op jit(solution)/shard_map/all_to_all | solution.py:606
  14.3 1.4 gather_fusion.1
  15.7 1.4 gather_fusion
  17.2 1.6 copy-done.2
  19.7 3.0 %send.1.refs_0_ = bf16[256,8192]{1,0:T(8,128)(2,1)S(1)} custom-call(bf16[256,128]{1,0:T(8,128)(2,1)S(1)} %copy-done.7, bf16[128,8192]{1,0:T(8,128)(2,1)S(1)} %copy-done.2), custom_call_target="tpu_custom_call" | custom-call | flops 536870912 | bytes 6291456 | tf_op jit(solution)/shard_map/send/pallas_call | solution.py:513
  22.7 2.0 %copy-done.1 = bf16[256,8192]{1,0:T(8,128)(2,1)} copy-done((bf16[256,8192]{1,0:T(8,128)(2,1)}, bf16[256,8192]{1,0:T(8,128)(2,1)S(1)}, u32[]{:S(2)}) %copy-start.1) | copy-done | bytes 4194328
  25.1 2.3 %half.3.refs_1_ = bf16[64,9216]{1,0:T(8,128)(2,1)} custom-call(s32[1]{0:T(128)} %bitcast.19.which_ref, bf16[2,64,1024]{2,1,0:T(8,128)(2,1)} %up_hbm.3, bf16[2,64,8192]{2,1,0:T(8,128)(2,1)} %down_hbm.3), custom_call_target="tpu_custom_call" | custom-call | tf_op jit(solution)/shard_map/half/pallas_call | solution.py:552
  28.5 10.5 %all-to-all-done.g_ref = bf16[8,32,1152]{2,1,0:T(8,128)(2,1)S(1)} async-done(((bf16[8,32,1152]{2,1,0:T(8,128)(2,1)}), bf16[8,32,1152]{2,1,0:T(8,128)(2,1)S(1)}, u32[]{:S(2)}, u32[]{:S(2)}) %all-to-all-start) | async-done | bytes 589856 | tf_op jit(solution)/shard_map/all_to_all | solution.py:606
  39.8 4.6 %project.2 = (bf16[32,8192]{1,0:T(8,128)(2,1)}, bf16[32,8192]{1,0:T(8,128)(2,1)}, bf16[32,8192]{1,0:T(8,128)(2,1)}, bf16[32,8192]{1,0:T(8,128)(2,1)}) custom-call(s32[1]{0:T(128)} %bitcast.18.spot_ref, bf16[8,32,1152]{2,1,0:T(8,128)(2,1)} %copy-done.8, f32[2,128]{1,0:T(2,128)} %compare_convert_fusion.which.refs_0_, bf16[64,9216]{1,0:T(8,128)(2,1)} %half.2.refs_0_, ...), custom_call_target="tpu_custom_call" | custom-call | flops 1000 | bytes 1000 | tf_op jit(solution)/shard_map/project/pallas_call | solution.py:75
  44.4 1.5 collective-permute-start.3
  45.9 2.4 %collective-permute-start.4 = (bf16[32,8192]{1,0:T(8,128)(2,1)}, bf16[32,8192]{1,0:T(8,128)(2,1)}, u32[]{:S(2)}, u32[]{:S(2)}) collective-permute-start(bf16[32,8192]{1,0:T(8,128)(2,1)} %get-tuple-element.36), channel_id=1, source_target_pairs={{0,4},{1,5},{2,6},{3,7},{4,0},{5,1},{6,2},{7,3},{8,12},{9,13},{10,... | collective-permute-start | bytes 1572872 | tf_op jit(solution)/shard_map/ppermute | solution.py:588
  48.3 4.7 %all-to-all-start.1 = ((bf16[16,16,8192]{2,1,0:T(8,128)(2,1)}), bf16[16,16,8192]{2,1,0:T(8,128)(2,1)}, u32[]{:S(2)}, u32[]{:S(2)}) async-start(bf16[16,16,8192]{2,1,0:T(8,128)(2,1)} %bitcast.26), calls=%async_computation.1 | async-start | bytes 8388608 | tf_op jit(solution)/shard_map/all_to_all | solution.py:629
  53.0 6.6 %collective-permute-done.refs_0_ = bf16[64,9216]{1,0:T(8,128)(2,1)} collective-permute-done((bf16[64,9216]{1,0:T(8,128)(2,1)}, bf16[64,9216]{1,0:T(8,128)(2,1)}, u32[]{:S(2)}, u32[]{:S(2)}) %collective-permute-start) | collective-permute-done | bytes 1179680 | tf_op jit(solution)/shard_map/ppermute | solution.py:588
  59.6 1.8 collective-permute-start.1
  62.2 2.0 %pull.2.near_ref.refs_2_ = bf16[128,256]{1,0:T(8,128)(2,1)} custom-call(bf16[128,1152]{1,0:T(8,128)(2,1)} %bitcast.28, bf16[128,1024]{1,0:T(8,128)(2,1)} %bitcast.32), custom_call_target="tpu_custom_call" | custom-call | flops 1000 | bytes 1000 | tf_op jit(solution)/shard_map/pull/pallas_call | solution.py:131
  65.9 26.5 %collective-permute-done.4.refs_8_ = bf16[32,8192]{1,0:T(8,128)(2,1)} collective-permute-done((bf16[32,8192]{1,0:T(8,128)(2,1)}, bf16[32,8192]{1,0:T(8,128)(2,1)}, u32[]{:S(2)}, u32[]{:S(2)}) %collective-permute-start.4) | collective-permute-done | bytes 524320 | tf_op jit(solution)/shard_map/ppermute | solution.py:588
  93.4 15.7 %collective-permute-done.5.refs_9_ = bf16[32,8192]{1,0:T(8,128)(2,1)} collective-permute-done((bf16[32,8192]{1,0:T(8,128)(2,1)}, bf16[32,8192]{1,0:T(8,128)(2,1)}, u32[]{:S(2)}, u32[]{:S(2)}) %collective-permute-start.5) | collective-permute-done | bytes 524320 | tf_op jit(solution)/shard_map/ppermute | solution.py:588
  112.9 1.9 %pull.3 = bf16[128,256]{1,0:T(8,128)(2,1)} custom-call(bf16[128,1152]{1,0:T(8,128)(2,1)} %bitcast.31, bf16[128,1024]{1,0:T(8,128)(2,1)} %pad_maximum_fusion.5.up), custom_call_target="tpu_custom_call" | custom-call | flops 1000 | bytes 1000 | tf_op jit(solution)/shard_map/pull/pallas_call | solution.py:131
  114.8 4.7 %project.3 = (bf16[64,8192]{1,0:T(8,128)(2,1)}, bf16[64,8192]{1,0:T(8,128)(2,1)}) custom-call(s32[1]{0:T(128)} %bitcast.18.spot_ref, bf16[8,32,1152]{2,1,0:T(8,128)(2,1)} %copy-done.8, f32[2,128]{1,0:T(2,128)} %gate.5.which, bf16[64,9216]{1,0:T(8,128)(2,1)} %collective-permute-done.refs_0_, bf16[64,9216]{1,0:T(8,128)(2,1)} %copy-done.11), custom_call_target="tpu_custom_call" | custom-call | flops 1000 | bytes 1000 | tf_op jit(solution)/shard_map/project/pallas_call | solution.py:75
  120.0 2.0 %fusion.10 = (bf16[16,8192]{1,0:T(8,128)(2,1)S(1)}, bf16[16,8192]{1,0:T(8,128)(2,1)S(1)}, bf16[16,8192]{1,0:T(8,128)(2,1)S(1)}, bf16[16,8192]{1,0:T(8,128)(2,1)}) fusion(bf16[64,8192]{1,0:T(8,128)(2,1)} %get-tuple-element.39), kind=kLoop, calls=%fused_computation.32 | loop fusion | bytes 2097152 | tf_op jit(solution)/shard_map/slice | solution.py:645
  125.8 3.5 %collective-permute-start.10 = (bf16[32,8192]{1,0:T(8,128)(2,1)}, bf16[32,8192]{1,0:T(8,128)(2,1)}, u32[]{:S(2)}, u32[]{:S(2)}) collective-permute-start(bf16[32,8192]{1,0:T(8,128)(2,1)} %pad_maximum_fusion.4), channel_id=1, source_target_pairs={{0,6},{1,7},{2,4},{3,5},{4,2},{5,3},{6,0},{7,1},{8,14},{9,15},{10,... | collective-permute-start | bytes 1572872 | tf_op jit(solution)/shard_map/ppermute | solution.py:588
  129.3 14.6 %all-to-all-done.1 = bf16[16,16,8192]{2,1,0:T(8,128)(2,1)} async-done(((bf16[16,16,8192]{2,1,0:T(8,128)(2,1)}), bf16[16,16,8192]{2,1,0:T(8,128)(2,1)}, u32[]{:S(2)}, u32[]{:S(2)}) %all-to-all-start.1) | async-done | bytes 4194336 | tf_op jit(solution)/shard_map/all_to_all | solution.py:629
  143.9 7.6 %collective-permute-done.2.across_ref.refs_3_ = bf16[128,256]{1,0:T(8,128)(2,1)S(1)} collective-permute-done((bf16[128,256]{1,0:T(8,128)(2,1)}, bf16[128,256]{1,0:T(8,128)(2,1)S(1)}, u32[]{:S(2)}, u32[]{:S(2)}) %collective-permute-start.2) | collective-permute-done | bytes 65568 | tf_op jit(solution)/shard_map/ppermute | solution.py:588
  151.5 4.8 %score.1 = (f32[16,1,256]{2,1,0:T(1,128)}, bf16[256,128]{1,0:T(8,128)(2,1)}) custom-call(s32[1]{0:T(128)} %bitcast.1.half_ref.here_ref, f32[1,256]{1,0:T(1,128)S(1)} %fusion.3.own_ref, bf16[128,256]{1,0:T(8,128)(2,1)S(1)} %copy-done.5, bf16[128,256]{1,0:T(8,128)(2,1)S(1)} %collective-permute-done.2.across_ref.refs_3_, bf16[128,8192]{1,0:T(8,128)(2,1)S(1)} %bitcast.25, ...), custom_call_target="tpu_custom_call" | custom-call | flops 536870912 | bytes 6291456 | tf_op jit(solution)/shard_map/score/pallas_call | solution.py:198
  156.3 9.5 %all-to-all-start.2 = ((f32[16,1,256]{2,1,0:T(1,128)}), f32[16,1,256]{2,1,0:T(1,128)S(1)}, u32[]{:S(2)}, u32[]{:S(2)}) async-start(f32[16,1,256]{2,1,0:T(1,128)} %get-tuple-element.31), calls=%async_computation.2 | async-start | bytes 32768 | tf_op jit(solution)/shard_map/all_to_all | solution.py:675
  165.8 2.8 %collective-permute-start.11 = (bf16[128,1024]{1,0:T(8,128)(2,1)}, bf16[128,1024]{1,0:T(8,128)(2,1)}, u32[]{:S(2)}, u32[]{:S(2)}) collective-permute-start(bf16[128,1024]{1,0:T(8,128)(2,1)} %slice.83), channel_id=1, source_target_pairs={{0,8},{1,9},{2,10},{3,11},{4,12},{5,13},{6,14},{7,15},{8,0},{9,1},... | collective-permute-start | bytes 786440 | tf_op jit(solution)/shard_map/ppermute | solution.py:588
  169.7 4.7 %collective-permute-done.10.refs_14_ = bf16[32,8192]{1,0:T(8,128)(2,1)} collective-permute-done((bf16[32,8192]{1,0:T(8,128)(2,1)}, bf16[32,8192]{1,0:T(8,128)(2,1)}, u32[]{:S(2)}, u32[]{:S(2)}) %collective-permute-start.10) | collective-permute-done | bytes 524320 | tf_op jit(solution)/shard_map/ppermute | solution.py:588
  174.4 6.7 %finish.1 = (f32[2]{0:T(128)}, f32[128,1]{1,0:T(8,128)}, bf16[256,128]{1,0:T(8,128)(2,1)}, bf16[128,8192]{1,0:T(8,128)(2,1)}, bf16[128,8192]{1,0:T(8,128)(2,1)}) custom-call(s32[2]{0:T(128)S(1)} %pad_add_fusion.place_ref, f32[16,1,256]{2,1,0:T(1,128)S(1)} %all-to-all-done.2.told_ref, f32[128,128]{1,0:T(8,128)S(1)} %pad_convert_fusion.refs_0_, ...), custom_call_target="tpu_custom_call" | custom-call | flops 1073741824 | bytes 12582912 | tf_op jit(solution)/shard_map/finish/pallas_call | solution.py:367
  181.5 2.1 %up.1 = bf16[128,1024]{1,0:T(8,128)(2,1)} custom-call(s32[1]{0:T(128)} %bitcast.1.half_ref.here_ref, bf16[256,128]{1,0:T(8,128)(2,1)} %get-tuple-element.47.upper_hbm, bf16[128,1152]{1,0:T(8,128)(2,1)} %bitcast.29, bf16[128,1024]{1,0:T(8,128)(2,1)} %collective-permute-done.11.across_hbm), custom_call_target="tpu_custom_call" | custom-call | flops 67108864 | bytes 524288 | tf_op jit(solution)/shard_map/up/pallas_call | solution.py:419
  (83 shorter events, 17.0 us)
Async XLA Ops:
  0.6 6.5 %copy-start.13 = (s32[128,1]{0,1:T(1,128)S(1)}, s32[128,1]{0,1:T(1,128)}, u32[]{:S(2)}) copy-start(s32[128,1]{0,1:T(1,128)} %param.12) | copy-start | bytes 1540
  3.0 56.6 %collective-permute-start = (bf16[64,9216]{1,0:T(8,128)(2,1)}, bf16[64,9216]{1,0:T(8,128)(2,1)}, u32[]{:S(2)}, u32[]{:S(2)}) collective-permute-start(bf16[64,9216]{1,0:T(8,128)(2,1)} %half.2.refs_0_), channel_id=1, source_target_pairs={{0,8},{1,9},{2,10},{3,11},{4,12},{5,13},{6,14},{7,15},{8,0},{9,1},... | collective-permute-start | bytes 3538952 | tf_op jit(solution)/shard_map/ppermute | solution.py:588
  7.8 6.3 %copy-start.16 = (s32[8]{0:T(128)S(1)}, s32[8]{0:T(128)}, u32[]{:S(2)}) copy-start(s32[8]{0:T(128)} %constant.52.clone) | copy-start | bytes 100
  7.8 6.4 %copy-start.14 = (s32[1,4]{1,0:T(1,128)S(1)}, s32[1,4]{1,0:T(1,128)}, u32[]{:S(2)}) copy-start(s32[1,4]{1,0:T(1,128)} %param.15) | copy-start | bytes 52
  7.8 9.3 %copy-start.15 = (f32[1,4]{1,0:T(1,128)S(1)}, f32[1,4]{1,0:T(1,128)}, u32[]{:S(2)}) copy-start(f32[1,4]{1,0:T(1,128)} %param.16) | copy-start | bytes 52
  10.3 28.7 %all-to-all-start = ((bf16[8,32,1152]{2,1,0:T(8,128)(2,1)}), bf16[8,32,1152]{2,1,0:T(8,128)(2,1)S(1)}, u32[]{:S(2)}, u32[]{:S(2)}) async-start(bf16[8,32,1152]{2,1,0:T(8,128)(2,1)} %bitcast.33), calls=%async_computation | async-start | bytes 1179648 | tf_op jit(solution)/shard_map/all_to_all | solution.py:606
  17.2 1.6 copy-start.2
  18.8 0.8 copy-start.7
  22.7 2.0 %copy-start.1 = (bf16[256,8192]{1,0:T(8,128)(2,1)}, bf16[256,8192]{1,0:T(8,128)(2,1)S(1)}, u32[]{:S(2)}) copy-start(bf16[256,8192]{1,0:T(8,128)(2,1)S(1)} %send.1.refs_0_) | copy-start | bytes 12582916
  24.7 2.9 %copy-start.12 = (s32[1,128]{1,0:T(1,128)S(1)}, s32[1,128]{1,0:T(1,128)}, u32[]{:S(2)}) copy-start(s32[1,128]{1,0:T(1,128)} %segment_ref.1) | copy-start | bytes 1540
  39.0 0.8 copy-start.8
  44.4 20.5 %collective-permute-start.3 = (bf16[32,8192]{1,0:T(8,128)(2,1)}, bf16[32,8192]{1,0:T(8,128)(2,1)}, u32[]{:S(2)}, u32[]{:S(2)}) collective-permute-start(bf16[32,8192]{1,0:T(8,128)(2,1)} %get-tuple-element.35), channel_id=1, source_target_pairs={{0,2},{1,3},{2,0},{3,1},{4,6},{5,7},{6,4},{7,5},{8,10},{9,11},{10,... | collective-permute-start | bytes 1572872 | tf_op jit(solution)/shard_map/ppermute | solution.py:588
  45.9 46.5 %collective-permute-start.4 = (bf16[32,8192]{1,0:T(8,128)(2,1)}, bf16[32,8192]{1,0:T(8,128)(2,1)}, u32[]{:S(2)}, u32[]{:S(2)}) collective-permute-start(bf16[32,8192]{1,0:T(8,128)(2,1)} %get-tuple-element.36), channel_id=1, source_target_pairs={{0,4},{1,5},{2,6},{3,7},{4,0},{5,1},{6,2},{7,3},{8,12},{9,13},{10,... | collective-permute-start | bytes 1572872 | tf_op jit(solution)/shard_map/ppermute | solution.py:588
  48.3 60.8 %collective-permute-start.5 = (bf16[32,8192]{1,0:T(8,128)(2,1)}, bf16[32,8192]{1,0:T(8,128)(2,1)}, u32[]{:S(2)}, u32[]{:S(2)}) collective-permute-start(bf16[32,8192]{1,0:T(8,128)(2,1)} %get-tuple-element.37), channel_id=1, source_target_pairs={{0,6},{1,7},{2,4},{3,5},{4,2},{5,3},{6,0},{7,1},{8,14},{9,15},{10,... | collective-permute-start | bytes 1572872 | tf_op jit(solution)/shard_map/ppermute | solution.py:588
  48.3 13.1 %copy-start.9 = (bf16[8,32,1152]{2,1,0:T(8,128)(2,1)S(1)}, bf16[8,32,1152]{2,1,0:T(8,128)(2,1)}, u32[]{:S(2)}) copy-start(bf16[8,32,1152]{2,1,0:T(8,128)(2,1)} %copy-done.8) | copy-start | bytes 1769476
  48.3 95.6 %all-to-all-start.1 = ((bf16[16,16,8192]{2,1,0:T(8,128)(2,1)}), bf16[16,16,8192]{2,1,0:T(8,128)(2,1)}, u32[]{:S(2)}, u32[]{:S(2)}) async-start(bf16[16,16,8192]{2,1,0:T(8,128)(2,1)} %bitcast.26), calls=%async_computation.1 | async-start | bytes 8388608 | tf_op jit(solution)/shard_map/all_to_all | solution.py:629
  53.0 11.9 %copy-start.3 = (bf16[32,8192]{1,0:T(8,128)(2,1)S(1)}, bf16[32,8192]{1,0:T(8,128)(2,1)}, u32[]{:S(2)}) copy-start(bf16[32,8192]{1,0:T(8,128)(2,1)} %get-tuple-element.34.refs_6_) | copy-start | bytes 1572868
  59.6 51.5 %collective-permute-start.1 = (bf16[64,9216]{1,0:T(8,128)(2,1)}, bf16[64,9216]{1,0:T(8,128)(2,1)S(1)}, u32[]{:S(2)}, u32[]{:S(2)}) collective-permute-start(bf16[64,9216]{1,0:T(8,128)(2,1)} %collective-permute-done.refs_0_), channel_id=1, source_target_pairs={{0,16},{16,0},{1,17},{17,1},{2,18},{18,2},{3,19},{19,3},{4,20},{20... | collective-permute-start | bytes 3538952 | tf_op jit(solution)/shard_map/ppermute | solution.py:591
  62.2 48.9 %copy-start.10 = (bf16[8,16,1152]{2,1,0:T(8,128)(2,1)}, bf16[8,16,1152]{2,1,0:T(8,128)(2,1)S(1)}, u32[]{:S(2)}) copy-start(bf16[8,16,1152]{2,1,0:T(8,128)(2,1)S(1)} %get-tuple-element.60) | copy-start | bytes 884740
  111.1 63.3 %collective-permute-start.6 = (bf16[64,8192]{1,0:T(8,128)(2,1)}, bf16[64,8192]{1,0:T(8,128)(2,1)}, u32[]{:S(2)}, u32[]{:S(2)}) collective-permute-start(bf16[64,8192]{1,0:T(8,128)(2,1)} %pad_maximum_fusion), channel_id=1, source_target_pairs={{0,1},{1,0},{2,3},{3,2},{4,5},{5,4},{6,7},{7,6},{8,9},{9,8},{10,11... | collective-permute-start | bytes 3145736 | tf_op jit(solution)/shard_map/ppermute | solution.py:588
  111.1 1.8 copy-start.11
  114.8 36.7 %collective-permute-start.2 = (bf16[128,256]{1,0:T(8,128)(2,1)}, bf16[128,256]{1,0:T(8,128)(2,1)S(1)}, u32[]{:S(2)}, u32[]{:S(2)}) collective-permute-start(bf16[128,256]{1,0:T(8,128)(2,1)} %pull.3), channel_id=1, source_target_pairs={{0,8},{1,9},{2,10},{3,11},{4,12},{5,13},{6,14},{7,15},{8,0},{9,1},... | collective-permute-start | bytes 196616 | tf_op jit(solution)/shard_map/ppermute | solution.py:588
  119.5 3.0 %collective-permute-start.7 = (bf16[64,8192]{1,0:T(8,128)(2,1)}, bf16[64,8192]{1,0:T(8,128)(2,1)S(1)}, u32[]{:S(2)}, u32[]{:S(2)}) collective-permute-start(bf16[64,8192]{1,0:T(8,128)(2,1)} %get-tuple-element.40), channel_id=1, source_target_pairs={{0,1},{1,0},{2,3},{3,2},{4,5},{5,4},{6,7},{7,6},{8,9},{9,8},{10,11... | collective-permute-start | bytes 3145736 | tf_op jit(solution)/shard_map/ppermute | solution.py:588
  123.3 28.2 %copy-start = (bf16[2,64,8192]{2,1,0:T(8,128)(2,1)S(1)}, bf16[2,64,8192]{2,1,0:T(8,128)(2,1)}, u32[]{:S(2)}) copy-start(bf16[2,64,8192]{2,1,0:T(8,128)(2,1)} %down_hbm.3) | copy-start | bytes 6291460
  123.3 28.2 %copy-start.5 = (bf16[128,256]{1,0:T(8,128)(2,1)S(1)}, bf16[128,256]{1,0:T(8,128)(2,1)}, u32[]{:S(2)}) copy-start(bf16[128,256]{1,0:T(8,128)(2,1)} %pull.2.near_ref.refs_2_) | copy-start | bytes 196612
  124.1 45.6 %collective-permute-start.8 = (bf16[32,8192]{1,0:T(8,128)(2,1)}, bf16[32,8192]{1,0:T(8,128)(2,1)S(1)}, u32[]{:S(2)}, u32[]{:S(2)}) collective-permute-start(bf16[32,8192]{1,0:T(8,128)(2,1)} %pad_maximum_fusion.2), channel_id=1, source_target_pairs={{0,2},{1,3},{2,0},{3,1},{4,6},{5,7},{6,4},{7,5},{8,10},{9,11},{10,... | collective-permute-start | bytes 1572872 | tf_op jit(solution)/shard_map/ppermute | solution.py:588
  124.9 44.8 %collective-permute-start.9 = (bf16[32,8192]{1,0:T(8,128)(2,1)}, bf16[32,8192]{1,0:T(8,128)(2,1)}, u32[]{:S(2)}, u32[]{:S(2)}) collective-permute-start(bf16[32,8192]{1,0:T(8,128)(2,1)} %pad_maximum_fusion.3), channel_id=1, source_target_pairs={{0,4},{1,5},{2,6},{3,7},{4,0},{5,1},{6,2},{7,3},{8,12},{9,13},{10,... | collective-permute-start | bytes 1572872 | tf_op jit(solution)/shard_map/ppermute | solution.py:588
  125.8 48.6 %collective-permute-start.10 = (bf16[32,8192]{1,0:T(8,128)(2,1)}, bf16[32,8192]{1,0:T(8,128)(2,1)}, u32[]{:S(2)}, u32[]{:S(2)}) collective-permute-start(bf16[32,8192]{1,0:T(8,128)(2,1)} %pad_maximum_fusion.4), channel_id=1, source_target_pairs={{0,6},{1,7},{2,4},{3,5},{4,2},{5,3},{6,0},{7,1},{8,14},{9,15},{10,... | collective-permute-start | bytes 1572872 | tf_op jit(solution)/shard_map/ppermute | solution.py:588
  151.5 4.8 %copy-start.6 = (bf16[128,256]{1,0:T(8,128)(2,1)}, bf16[128,256]{1,0:T(8,128)(2,1)S(1)}, u32[]{:S(2)}) copy-start(bf16[128,256]{1,0:T(8,128)(2,1)S(1)} %collective-permute-done.2.across_ref.refs_3_) | copy-start | bytes 196612
  151.5 22.9 %copy-start.4 = (bf16[32,8192]{1,0:T(8,128)(2,1)S(1)}, bf16[32,8192]{1,0:T(8,128)(2,1)}, u32[]{:S(2)}) copy-start(bf16[32,8192]{1,0:T(8,128)(2,1)} %get-tuple-element.34.refs_6_) | copy-start | bytes 1572868
  156.3 18.1 %all-to-all-start.2 = ((f32[16,1,256]{2,1,0:T(1,128)}), f32[16,1,256]{2,1,0:T(1,128)S(1)}, u32[]{:S(2)}, u32[]{:S(2)}) async-start(f32[16,1,256]{2,1,0:T(1,128)} %get-tuple-element.31), calls=%async_computation.2 | async-start | bytes 32768 | tf_op jit(solution)/shard_map/all_to_all | solution.py:675
  165.8 15.7 %collective-permute-start.11 = (bf16[128,1024]{1,0:T(8,128)(2,1)}, bf16[128,1024]{1,0:T(8,128)(2,1)}, u32[]{:S(2)}, u32[]{:S(2)}) collective-permute-start(bf16[128,1024]{1,0:T(8,128)(2,1)} %slice.83), channel_id=1, source_target_pairs={{0,8},{1,9},{2,10},{3,11},{4,12},{5,13},{6,14},{7,15},{8,0},{9,1},... | collective-permute-start | bytes 786440 | tf_op jit(solution)/shard_map/ppermute | solution.py:588

commit v10 on v9

--- a/solution.py
+++ b/solution.py
@@ -257,7 +257,7 @@
         smalls, refs = refs[:3], refs[3:]
         got, grad_down, small_sems, got_sems, down_sems = refs
     lanes, width = grad_down.shape
-    parts = column_parts(width, 2048)
+    parts = column_parts(width, 4096)
     copies = [
         pltpu.make_async_copy(got_hbm.at[:, part], got.at[:, part], got_sems.at[at])
         for at, part in enumerate(parts)
@@ -339,7 +339,7 @@
     (slots, width), lanes = got.shape, smalls[0].shape[1]
     rows = row_marks.shape[0]
     n_dev = told.shape[0]
-    n_parts = len(column_parts(width, 2048))
+    n_parts = len(column_parts(width, 4096))
     together = not any(size % 16 for size in used)
     vmem, hbm = pl.BlockSpec(memory_space=pltpu.VMEM), pl.BlockSpec(memory_space=pltpu.HBM)
     sems = pltpu.SemaphoreType.DMA

time: 184 us -> 184 us (level)
  no operation moved by 1% of the time
where the time goes in v10:
time: 184 us
  waiting for transfers between devices  87.5 us (48%)
  Pallas kernels  36.6 us (20%)
  starting transfers between devices  34.6 us (19%)
  local copies, waits for them, and re-layouts  16.4 us (9%)
  other arithmetic  7.55 us (4%)
    ppermute x11, waiting for transfers between devices, flipped(): return lax.ppermute(block, 'ad', [(at, at ^ flip) for at in range(n_dev)])  62.3 us
    ppermute x11, starting transfers between devices, flipped(): return lax.ppermute(block, 'ad', [(at, at ^ flip) for at in range(n_dev)])  14.8 us
    all_to_all x1, waiting for transfers between devices, body(): lax.all_to_all(sent.reshape(n_dev, capacity, width), 'ad', split_axis=0,...  14.6 us
    all_to_all x1, waiting for transfers between devices, body(): lax.all_to_all(sent_g.reshape(half_size, 2 * capacity, out_width + MARKS)...  10.5 us
    all_to_all x1, starting transfers between devices, body(): told = lax.all_to_all(part, 'ad', split_axis=0, concat_axis=0, tiled=True)  9.46 us
    pallas_call x2, Pallas kernels, project(): pl.pallas_call(functools.partial(project_kernel, side, split, capacity, o...  9.29 us
    pallas_call x1, Pallas kernels, finish(): pl.pallas_call(functools.partial(finish_kernel, count, seqs, slots // n_d...  6.38 us
    unnamed x34, local copies, waits for them, and re-layouts  5.32 us
  transfers between devices with their start and end apart: 15, of which 9 were waited for; matrix products, arithmetic and copies ran while one was open for 10% of the time, Pallas kernels for 16%

profile of v10, /device:TPU:0, one launch (start us, length us, event | category | flops | bytes accessed | tf_op | source)
XLA Modules:
  0.0 183.6 jit_solution(3671826952018367113)
XLA Ops:
  0.6 2.3 %half.2.refs_0_ = bf16[64,9216]{1,0:T(8,128)(2,1)} custom-call(s32[1]{0:T(128)} %bitcast.4.which_ref, bf16[2,64,1024]{2,1,0:T(8,128)(2,1)} %up_hbm.3, bf16[2,64,8192]{2,1,0:T(8,128)(2,1)} %down_hbm.3), custom_call_target="tpu_custom_call" | custom-call | tf_op jit(solution)/shard_map/half/pallas_call | solution.py:552
  3.0 4.1 %collective-permute-start = (bf16[64,9216]{1,0:T(8,128)(2,1)}, bf16[64,9216]{1,0:T(8,128)(2,1)}, u32[]{:S(2)}, u32[]{:S(2)}) collective-permute-start(bf16[64,9216]{1,0:T(8,128)(2,1)} %half.2.refs_0_), channel_id=1, source_target_pairs={{0,8},{1,9},{2,10},{3,11},{4,12},{5,13},{6,14},{7,15},{8,0},{9,1},... | collective-permute-start | bytes 3538952 | tf_op jit(solution)/shard_map/ppermute | solution.py:588
  7.8 2.5 %slots.1 = (bf16[256,128]{1,0:T(8,128)(2,1)}, bf16[256,128]{1,0:T(8,128)(2,1)}, bf16[256,1152]{1,0:T(8,128)(2,1)}) custom-call(s32[1]{0:T(128)} %bitcast.1.half_ref.here_ref, s32[128,1]{1,0:T(8,128)} %gate.3.owner_ref, s32[1,128]{1,0:T(1,128)} %bitcast.41, s32[1,128]{1,0:T(1,128)} %segment_ref.1, bf16[128,1024]{1,0:T(8,128)(2,1)} %g_ref.1), custom_call_target="tpu_custom_call" | custom-call | tf_op jit(solution)/shard_map/slots/pallas_call | solution.py:475
  10.3 3.8 %all-to-all-start = ((bf16[8,32,1152]{2,1,0:T(8,128)(2,1)}), bf16[8,32,1152]{2,1,0:T(8,128)(2,1)S(1)}, u32[]{:S(2)}, u32[]{:S(2)}) async-start(bf16[8,32,1152]{2,1,0:T(8,128)(2,1)} %bitcast.33), calls=%async_computation | async-start | bytes 1179648 | tf_op jit(solution)/shard_map/all_to_all | solution.py:606
  14.3 1.4 gather_fusion.1
  15.7 1.4 gather_fusion
  17.2 1.6 copy-done.2
  19.7 3.0 %send.1.refs_0_ = bf16[256,8192]{1,0:T(8,128)(2,1)S(1)} custom-call(bf16[256,128]{1,0:T(8,128)(2,1)S(1)} %copy-done.7, bf16[128,8192]{1,0:T(8,128)(2,1)S(1)} %copy-done.2), custom_call_target="tpu_custom_call" | custom-call | flops 536870912 | bytes 6291456 | tf_op jit(solution)/shard_map/send/pallas_call | solution.py:513
  22.7 2.0 %copy-done.1 = bf16[256,8192]{1,0:T(8,128)(2,1)} copy-done((bf16[256,8192]{1,0:T(8,128)(2,1)}, bf16[256,8192]{1,0:T(8,128)(2,1)S(1)}, u32[]{:S(2)}) %copy-start.1) | copy-done | bytes 4194328
  25.1 2.3 %half.3.refs_1_ = bf16[64,9216]{1,0:T(8,128)(2,1)} custom-call(s32[1]{0:T(128)} %bitcast.19.which_ref, bf16[2,64,1024]{2,1,0:T(8,128)(2,1)} %up_hbm.3, bf16[2,64,8192]{2,1,0:T(8,128)(2,1)} %down_hbm.3), custom_call_target="tpu_custom_call" | custom-call | tf_op jit(solution)/shard_map/half/pallas_call | solution.py:552
  28.5 10.5 %all-to-all-done.g_ref = bf16[8,32,1152]{2,1,0:T(8,128)(2,1)S(1)} async-done(((bf16[8,32,1152]{2,1,0:T(8,128)(2,1)}), bf16[8,32,1152]{2,1,0:T(8,128)(2,1)S(1)}, u32[]{:S(2)}, u32[]{:S(2)}) %all-to-all-start) | async-done | bytes 589856 | tf_op jit(solution)/shard_map/all_to_all | solution.py:606
  39.8 4.6 %project.2 = (bf16[32,8192]{1,0:T(8,128)(2,1)}, bf16[32,8192]{1,0:T(8,128)(2,1)}, bf16[32,8192]{1,0:T(8,128)(2,1)}, bf16[32,8192]{1,0:T(8,128)(2,1)}) custom-call(s32[1]{0:T(128)} %bitcast.18.spot_ref, bf16[8,32,1152]{2,1,0:T(8,128)(2,1)} %copy-done.8, f32[2,128]{1,0:T(2,128)} %compare_convert_fusion.which.refs_0_, bf16[64,9216]{1,0:T(8,128)(2,1)} %half.2.refs_0_, ...), custom_call_target="tpu_custom_call" | custom-call | flops 1000 | bytes 1000 | tf_op jit(solution)/shard_map/project/pallas_call | solution.py:75
  44.4 1.5 collective-permute-start.3
  45.9 2.4 %collective-permute-start.4 = (bf16[32,8192]{1,0:T(8,128)(2,1)}, bf16[32,8192]{1,0:T(8,128)(2,1)}, u32[]{:S(2)}, u32[]{:S(2)}) collective-permute-start(bf16[32,8192]{1,0:T(8,128)(2,1)} %get-tuple-element.36), channel_id=1, source_target_pairs={{0,4},{1,5},{2,6},{3,7},{4,0},{5,1},{6,2},{7,3},{8,12},{9,13},{10,... | collective-permute-start | bytes 1572872 | tf_op jit(solution)/shard_map/ppermute | solution.py:588
  48.3 4.7 %all-to-all-start.1 = ((bf16[16,16,8192]{2,1,0:T(8,128)(2,1)}), bf16[16,16,8192]{2,1,0:T(8,128)(2,1)}, u32[]{:S(2)}, u32[]{:S(2)}) async-start(bf16[16,16,8192]{2,1,0:T(8,128)(2,1)} %bitcast.26), calls=%async_computation.1 | async-start | bytes 8388608 | tf_op jit(solution)/shard_map/all_to_all | solution.py:629
  53.0 6.6 %collective-permute-done.refs_0_ = bf16[64,9216]{1,0:T(8,128)(2,1)} collective-permute-done((bf16[64,9216]{1,0:T(8,128)(2,1)}, bf16[64,9216]{1,0:T(8,128)(2,1)}, u32[]{:S(2)}, u32[]{:S(2)}) %collective-permute-start) | collective-permute-done | bytes 1179680 | tf_op jit(solution)/shard_map/ppermute | solution.py:588
  59.6 1.8 collective-permute-start.1
  62.2 2.0 %pull.2.near_ref.refs_2_ = bf16[128,256]{1,0:T(8,128)(2,1)} custom-call(bf16[128,1152]{1,0:T(8,128)(2,1)} %bitcast.28, bf16[128,1024]{1,0:T(8,128)(2,1)} %bitcast.32), custom_call_target="tpu_custom_call" | custom-call | flops 1000 | bytes 1000 | tf_op jit(solution)/shard_map/pull/pallas_call | solution.py:131
  65.9 26.5 %collective-permute-done.4.refs_8_ = bf16[32,8192]{1,0:T(8,128)(2,1)} collective-permute-done((bf16[32,8192]{1,0:T(8,128)(2,1)}, bf16[32,8192]{1,0:T(8,128)(2,1)}, u32[]{:S(2)}, u32[]{:S(2)}) %collective-permute-start.4) | collective-permute-done | bytes 524320 | tf_op jit(solution)/shard_map/ppermute | solution.py:588
  93.4 15.7 %collective-permute-done.5.refs_9_ = bf16[32,8192]{1,0:T(8,128)(2,1)} collective-permute-done((bf16[32,8192]{1,0:T(8,128)(2,1)}, bf16[32,8192]{1,0:T(8,128)(2,1)}, u32[]{:S(2)}, u32[]{:S(2)}) %collective-permute-start.5) | collective-permute-done | bytes 524320 | tf_op jit(solution)/shard_map/ppermute | solution.py:588
  112.9 1.9 %pull.3 = bf16[128,256]{1,0:T(8,128)(2,1)} custom-call(bf16[128,1152]{1,0:T(8,128)(2,1)} %bitcast.31, bf16[128,1024]{1,0:T(8,128)(2,1)} %pad_maximum_fusion.5.up), custom_call_target="tpu_custom_call" | custom-call | flops 1000 | bytes 1000 | tf_op jit(solution)/shard_map/pull/pallas_call | solution.py:131
  114.8 4.7 %project.3 = (bf16[64,8192]{1,0:T(8,128)(2,1)}, bf16[64,8192]{1,0:T(8,128)(2,1)}) custom-call(s32[1]{0:T(128)} %bitcast.18.spot_ref, bf16[8,32,1152]{2,1,0:T(8,128)(2,1)} %copy-done.8, f32[2,128]{1,0:T(2,128)} %gate.5.which, bf16[64,9216]{1,0:T(8,128)(2,1)} %collective-permute-done.refs_0_, bf16[64,9216]{1,0:T(8,128)(2,1)} %copy-done.11), custom_call_target="tpu_custom_call" | custom-call | flops 1000 | bytes 1000 | tf_op jit(solution)/shard_map/project/pallas_call | solution.py:75
  120.0 2.0 %fusion.10 = (bf16[16,8192]{1,0:T(8,128)(2,1)S(1)}, bf16[16,8192]{1,0:T(8,128)(2,1)S(1)}, bf16[16,8192]{1,0:T(8,128)(2,1)S(1)}, bf16[16,8192]{1,0:T(8,128)(2,1)}) fusion(bf16[64,8192]{1,0:T(8,128)(2,1)} %get-tuple-element.39), kind=kLoop, calls=%fused_computation.32 | loop fusion | bytes 2097152 | tf_op jit(solution)/shard_map/slice | solution.py:645
  125.8 3.5 %collective-permute-start.10 = (bf16[32,8192]{1,0:T(8,128)(2,1)}, bf16[32,8192]{1,0:T(8,128)(2,1)}, u32[]{:S(2)}, u32[]{:S(2)}) collective-permute-start(bf16[32,8192]{1,0:T(8,128)(2,1)} %pad_maximum_fusion.4), channel_id=1, source_target_pairs={{0,6},{1,7},{2,4},{3,5},{4,2},{5,3},{6,0},{7,1},{8,14},{9,15},{10,... | collective-permute-start | bytes 1572872 | tf_op jit(solution)/shard_map/ppermute | solution.py:588
  129.3 14.6 %all-to-all-done.1 = bf16[16,16,8192]{2,1,0:T(8,128)(2,1)} async-done(((bf16[16,16,8192]{2,1,0:T(8,128)(2,1)}), bf16[16,16,8192]{2,1,0:T(8,128)(2,1)}, u32[]{:S(2)}, u32[]{:S(2)}) %all-to-all-start.1) | async-done | bytes 4194336 | tf_op jit(solution)/shard_map/all_to_all | solution.py:629
  143.9 7.6 %collective-permute-done.2.across_ref.refs_3_ = bf16[128,256]{1,0:T(8,128)(2,1)S(1)} collective-permute-done((bf16[128,256]{1,0:T(8,128)(2,1)}, bf16[128,256]{1,0:T(8,128)(2,1)S(1)}, u32[]{:S(2)}, u32[]{:S(2)}) %collective-permute-start.2) | collective-permute-done | bytes 65568 | tf_op jit(solution)/shard_map/ppermute | solution.py:588
  151.5 4.8 %score.1 = (f32[16,1,256]{2,1,0:T(1,128)}, bf16[256,128]{1,0:T(8,128)(2,1)}) custom-call(s32[1]{0:T(128)} %bitcast.1.half_ref.here_ref, f32[1,256]{1,0:T(1,128)S(1)} %fusion.3.own_ref, bf16[128,256]{1,0:T(8,128)(2,1)S(1)} %copy-done.5, bf16[128,256]{1,0:T(8,128)(2,1)S(1)} %collective-permute-done.2.across_ref.refs_3_, bf16[128,8192]{1,0:T(8,128)(2,1)S(1)} %bitcast.25, ...), custom_call_target="tpu_custom_call" | custom-call | flops 536870912 | bytes 6291456 | tf_op jit(solution)/shard_map/score/pallas_call | solution.py:198
  156.3 9.5 %all-to-all-start.2 = ((f32[16,1,256]{2,1,0:T(1,128)}), f32[16,1,256]{2,1,0:T(1,128)S(1)}, u32[]{:S(2)}, u32[]{:S(2)}) async-start(f32[16,1,256]{2,1,0:T(1,128)} %get-tuple-element.31), calls=%async_computation.2 | async-start | bytes 32768 | tf_op jit(solution)/shard_map/all_to_all | solution.py:675
  165.8 2.8 %collective-permute-start.11 = (bf16[128,1024]{1,0:T(8,128)(2,1)}, bf16[128,1024]{1,0:T(8,128)(2,1)}, u32[]{:S(2)}, u32[]{:S(2)}) collective-permute-start(bf16[128,1024]{1,0:T(8,128)(2,1)} %slice.83), channel_id=1, source_target_pairs={{0,8},{1,9},{2,10},{3,11},{4,12},{5,13},{6,14},{7,15},{8,0},{9,1},... | collective-permute-start | bytes 786440 | tf_op jit(solution)/shard_map/ppermute | solution.py:588
  169.7 4.7 %collective-permute-done.10.refs_14_ = bf16[32,8192]{1,0:T(8,128)(2,1)} collective-permute-done((bf16[32,8192]{1,0:T(8,128)(2,1)}, bf16[32,8192]{1,0:T(8,128)(2,1)}, u32[]{:S(2)}, u32[]{:S(2)}) %collective-permute-start.10) | collective-permute-done | bytes 524320 | tf_op jit(solution)/shard_map/ppermute | solution.py:588
  174.4 6.4 %finish.1 = (f32[2]{0:T(128)}, f32[128,1]{1,0:T(8,128)}, bf16[256,128]{1,0:T(8,128)(2,1)}, bf16[128,8192]{1,0:T(8,128)(2,1)}, bf16[128,8192]{1,0:T(8,128)(2,1)}) custom-call(s32[2]{0:T(128)S(1)} %pad_add_fusion.place_ref, f32[16,1,256]{2,1,0:T(1,128)S(1)} %all-to-all-done.2.told_ref, f32[128,128]{1,0:T(8,128)S(1)} %pad_convert_fusion.refs_0_, ...), custom_call_target="tpu_custom_call" | custom-call | flops 1073741824 | bytes 12582912 | tf_op jit(solution)/shard_map/finish/pallas_call | solution.py:367
  181.5 2.1 %up.1 = bf16[128,1024]{1,0:T(8,128)(2,1)} custom-call(s32[1]{0:T(128)} %bitcast.1.half_ref.here_ref, bf16[256,128]{1,0:T(8,128)(2,1)} %get-tuple-element.47.upper_hbm, bf16[128,1152]{1,0:T(8,128)(2,1)} %bitcast.29, bf16[128,1024]{1,0:T(8,128)(2,1)} %collective-permute-done.11.across_hbm), custom_call_target="tpu_custom_call" | custom-call | flops 67108864 | bytes 524288 | tf_op jit(solution)/shard_map/up/pallas_call | solution.py:419
  (83 shorter events, 17.2 us)
Async XLA Ops:
  0.6 6.5 %copy-start.13 = (s32[128,1]{0,1:T(1,128)S(1)}, s32[128,1]{0,1:T(1,128)}, u32[]{:S(2)}) copy-start(s32[128,1]{0,1:T(1,128)} %param.12) | copy-start | bytes 1540
  3.0 56.6 %collective-permute-start = (bf16[64,9216]{1,0:T(8,128)(2,1)}, bf16[64,9216]{1,0:T(8,128)(2,1)}, u32[]{:S(2)}, u32[]{:S(2)}) collective-permute-start(bf16[64,9216]{1,0:T(8,128)(2,1)} %half.2.refs_0_), channel_id=1, source_target_pairs={{0,8},{1,9},{2,10},{3,11},{4,12},{5,13},{6,14},{7,15},{8,0},{9,1},... | collective-permute-start | bytes 3538952 | tf_op jit(solution)/shard_map/ppermute | solution.py:588
  7.8 6.3 %copy-start.16 = (s32[8]{0:T(128)S(1)}, s32[8]{0:T(128)}, u32[]{:S(2)}) copy-start(s32[8]{0:T(128)} %constant.52.clone) | copy-start | bytes 100
  7.8 6.4 %copy-start.14 = (s32[1,4]{1,0:T(1,128)S(1)}, s32[1,4]{1,0:T(1,128)}, u32[]{:S(2)}) copy-start(s32[1,4]{1,0:T(1,128)} %param.15) | copy-start | bytes 52
  7.8 9.3 %copy-start.15 = (f32[1,4]{1,0:T(1,128)S(1)}, f32[1,4]{1,0:T(1,128)}, u32[]{:S(2)}) copy-start(f32[1,4]{1,0:T(1,128)} %param.16) | copy-start | bytes 52
  10.3 28.7 %all-to-all-start = ((bf16[8,32,1152]{2,1,0:T(8,128)(2,1)}), bf16[8,32,1152]{2,1,0:T(8,128)(2,1)S(1)}, u32[]{:S(2)}, u32[]{:S(2)}) async-start(bf16[8,32,1152]{2,1,0:T(8,128)(2,1)} %bitcast.33), calls=%async_computation | async-start | bytes 1179648 | tf_op jit(solution)/shard_map/all_to_all | solution.py:606
  17.2 1.6 copy-start.2
  18.8 0.8 copy-start.7
  22.7 2.0 %copy-start.1 = (bf16[256,8192]{1,0:T(8,128)(2,1)}, bf16[256,8192]{1,0:T(8,128)(2,1)S(1)}, u32[]{:S(2)}) copy-start(bf16[256,8192]{1,0:T(8,128)(2,1)S(1)} %send.1.refs_0_) | copy-start | bytes 12582916
  24.7 2.9 %copy-start.12 = (s32[1,128]{1,0:T(1,128)S(1)}, s32[1,128]{1,0:T(1,128)}, u32[]{:S(2)}) copy-start(s32[1,128]{1,0:T(1,128)} %segment_ref.1) | copy-start | bytes 1540
  39.0 0.8 copy-start.8
  44.4 20.5 %collective-permute-start.3 = (bf16[32,8192]{1,0:T(8,128)(2,1)}, bf16[32,8192]{1,0:T(8,128)(2,1)}, u32[]{:S(2)}, u32[]{:S(2)}) collective-permute-start(bf16[32,8192]{1,0:T(8,128)(2,1)} %get-tuple-element.35), channel_id=1, source_target_pairs={{0,2},{1,3},{2,0},{3,1},{4,6},{5,7},{6,4},{7,5},{8,10},{9,11},{10,... | collective-permute-start | bytes 1572872 | tf_op jit(solution)/shard_map/ppermute | solution.py:588
  45.9 46.5 %collective-permute-start.4 = (bf16[32,8192]{1,0:T(8,128)(2,1)}, bf16[32,8192]{1,0:T(8,128)(2,1)}, u32[]{:S(2)}, u32[]{:S(2)}) collective-permute-start(bf16[32,8192]{1,0:T(8,128)(2,1)} %get-tuple-element.36), channel_id=1, source_target_pairs={{0,4},{1,5},{2,6},{3,7},{4,0},{5,1},{6,2},{7,3},{8,12},{9,13},{10,... | collective-permute-start | bytes 1572872 | tf_op jit(solution)/shard_map/ppermute | solution.py:588
  48.3 60.8 %collective-permute-start.5 = (bf16[32,8192]{1,0:T(8,128)(2,1)}, bf16[32,8192]{1,0:T(8,128)(2,1)}, u32[]{:S(2)}, u32[]{:S(2)}) collective-permute-start(bf16[32,8192]{1,0:T(8,128)(2,1)} %get-tuple-element.37), channel_id=1, source_target_pairs={{0,6},{1,7},{2,4},{3,5},{4,2},{5,3},{6,0},{7,1},{8,14},{9,15},{10,... | collective-permute-start | bytes 1572872 | tf_op jit(solution)/shard_map/ppermute | solution.py:588
  48.3 13.1 %copy-start.9 = (bf16[8,32,1152]{2,1,0:T(8,128)(2,1)S(1)}, bf16[8,32,1152]{2,1,0:T(8,128)(2,1)}, u32[]{:S(2)}) copy-start(bf16[8,32,1152]{2,1,0:T(8,128)(2,1)} %copy-done.8) | copy-start | bytes 1769476
  48.3 95.6 %all-to-all-start.1 = ((bf16[16,16,8192]{2,1,0:T(8,128)(2,1)}), bf16[16,16,8192]{2,1,0:T(8,128)(2,1)}, u32[]{:S(2)}, u32[]{:S(2)}) async-start(bf16[16,16,8192]{2,1,0:T(8,128)(2,1)} %bitcast.26), calls=%async_computation.1 | async-start | bytes 8388608 | tf_op jit(solution)/shard_map/all_to_all | solution.py:629
  53.0 11.9 %copy-start.3 = (bf16[32,8192]{1,0:T(8,128)(2,1)S(1)}, bf16[32,8192]{1,0:T(8,128)(2,1)}, u32[]{:S(2)}) copy-start(bf16[32,8192]{1,0:T(8,128)(2,1)} %get-tuple-element.34.refs_6_) | copy-start | bytes 1572868
  59.6 51.5 %collective-permute-start.1 = (bf16[64,9216]{1,0:T(8,128)(2,1)}, bf16[64,9216]{1,0:T(8,128)(2,1)S(1)}, u32[]{:S(2)}, u32[]{:S(2)}) collective-permute-start(bf16[64,9216]{1,0:T(8,128)(2,1)} %collective-permute-done.refs_0_), channel_id=1, source_target_pairs={{0,16},{16,0},{1,17},{17,1},{2,18},{18,2},{3,19},{19,3},{4,20},{20... | collective-permute-start | bytes 3538952 | tf_op jit(solution)/shard_map/ppermute | solution.py:591
  62.2 48.9 %copy-start.10 = (bf16[8,16,1152]{2,1,0:T(8,128)(2,1)}, bf16[8,16,1152]{2,1,0:T(8,128)(2,1)S(1)}, u32[]{:S(2)}) copy-start(bf16[8,16,1152]{2,1,0:T(8,128)(2,1)S(1)} %get-tuple-element.60) | copy-start | bytes 884740
  111.1 63.3 %collective-permute-start.6 = (bf16[64,8192]{1,0:T(8,128)(2,1)}, bf16[64,8192]{1,0:T(8,128)(2,1)}, u32[]{:S(2)}, u32[]{:S(2)}) collective-permute-start(bf16[64,8192]{1,0:T(8,128)(2,1)} %pad_maximum_fusion), channel_id=1, source_target_pairs={{0,1},{1,0},{2,3},{3,2},{4,5},{5,4},{6,7},{7,6},{8,9},{9,8},{10,11... | collective-permute-start | bytes 3145736 | tf_op jit(solution)/shard_map/ppermute | solution.py:588
  111.1 1.8 copy-start.11
  114.8 36.7 %collective-permute-start.2 = (bf16[128,256]{1,0:T(8,128)(2,1)}, bf16[128,256]{1,0:T(8,128)(2,1)S(1)}, u32[]{:S(2)}, u32[]{:S(2)}) collective-permute-start(bf16[128,256]{1,0:T(8,128)(2,1)} %pull.3), channel_id=1, source_target_pairs={{0,8},{1,9},{2,10},{3,11},{4,12},{5,13},{6,14},{7,15},{8,0},{9,1},... | collective-permute-start | bytes 196616 | tf_op jit(solution)/shard_map/ppermute | solution.py:588
  119.5 3.0 %collective-permute-start.7 = (bf16[64,8192]{1,0:T(8,128)(2,1)}, bf16[64,8192]{1,0:T(8,128)(2,1)S(1)}, u32[]{:S(2)}, u32[]{:S(2)}) collective-permute-start(bf16[64,8192]{1,0:T(8,128)(2,1)} %get-tuple-element.40), channel_id=1, source_target_pairs={{0,1},{1,0},{2,3},{3,2},{4,5},{5,4},{6,7},{7,6},{8,9},{9,8},{10,11... | collective-permute-start | bytes 3145736 | tf_op jit(solution)/shard_map/ppermute | solution.py:588
  123.3 28.2 %copy-start = (bf16[2,64,8192]{2,1,0:T(8,128)(2,1)S(1)}, bf16[2,64,8192]{2,1,0:T(8,128)(2,1)}, u32[]{:S(2)}) copy-start(bf16[2,64,8192]{2,1,0:T(8,128)(2,1)} %down_hbm.3) | copy-start | bytes 6291460
  123.3 28.2 %copy-start.5 = (bf16[128,256]{1,0:T(8,128)(2,1)S(1)}, bf16[128,256]{1,0:T(8,128)(2,1)}, u32[]{:S(2)}) copy-start(bf16[128,256]{1,0:T(8,128)(2,1)} %pull.2.near_ref.refs_2_) | copy-start | bytes 196612
  124.1 45.6 %collective-permute-start.8 = (bf16[32,8192]{1,0:T(8,128)(2,1)}, bf16[32,8192]{1,0:T(8,128)(2,1)S(1)}, u32[]{:S(2)}, u32[]{:S(2)}) collective-permute-start(bf16[32,8192]{1,0:T(8,128)(2,1)} %pad_maximum_fusion.2), channel_id=1, source_target_pairs={{0,2},{1,3},{2,0},{3,1},{4,6},{5,7},{6,4},{7,5},{8,10},{9,11},{10,... | collective-permute-start | bytes 1572872 | tf_op jit(solution)/shard_map/ppermute | solution.py:588
  124.9 44.8 %collective-permute-start.9 = (bf16[32,8192]{1,0:T(8,128)(2,1)}, bf16[32,8192]{1,0:T(8,128)(2,1)}, u32[]{:S(2)}, u32[]{:S(2)}) collective-permute-start(bf16[32,8192]{1,0:T(8,128)(2,1)} %pad_maximum_fusion.3), channel_id=1, source_target_pairs={{0,4},{1,5},{2,6},{3,7},{4,0},{5,1},{6,2},{7,3},{8,12},{9,13},{10,... | collective-permute-start | bytes 1572872 | tf_op jit(solution)/shard_map/ppermute | solution.py:588
  125.8 48.6 %collective-permute-start.10 = (bf16[32,8192]{1,0:T(8,128)(2,1)}, bf16[32,8192]{1,0:T(8,128)(2,1)}, u32[]{:S(2)}, u32[]{:S(2)}) collective-permute-start(bf16[32,8192]{1,0:T(8,128)(2,1)} %pad_maximum_fusion.4), channel_id=1, source_target_pairs={{0,6},{1,7},{2,4},{3,5},{4,2},{5,3},{6,0},{7,1},{8,14},{9,15},{10,... | collective-permute-start | bytes 1572872 | tf_op jit(solution)/shard_map/ppermute | solution.py:588
  151.5 4.8 %copy-start.6 = (bf16[128,256]{1,0:T(8,128)(2,1)}, bf16[128,256]{1,0:T(8,128)(2,1)S(1)}, u32[]{:S(2)}) copy-start(bf16[128,256]{1,0:T(8,128)(2,1)S(1)} %collective-permute-done.2.across_ref.refs_3_) | copy-start | bytes 196612
  151.5 22.9 %copy-start.4 = (bf16[32,8192]{1,0:T(8,128)(2,1)S(1)}, bf16[32,8192]{1,0:T(8,128)(2,1)}, u32[]{:S(2)}) copy-start(bf16[32,8192]{1,0:T(8,128)(2,1)} %get-tuple-element.34.refs_6_) | copy-start | bytes 1572868
  156.3 18.1 %all-to-all-start.2 = ((f32[16,1,256]{2,1,0:T(1,128)}), f32[16,1,256]{2,1,0:T(1,128)S(1)}, u32[]{:S(2)}, u32[]{:S(2)}) async-start(f32[16,1,256]{2,1,0:T(1,128)} %get-tuple-element.31), calls=%async_computation.2 | async-start | bytes 32768 | tf_op jit(solution)/shard_map/all_to_all | solution.py:675
  165.8 15.7 %collective-permute-start.11 = (bf16[128,1024]{1,0:T(8,128)(2,1)}, bf16[128,1024]{1,0:T(8,128)(2,1)}, u32[]{:S(2)}, u32[]{:S(2)}) collective-permute-start(bf16[128,1024]{1,0:T(8,128)(2,1)} %slice.83), channel_id=1, source_target_pairs={{0,8},{1,9},{2,10},{3,11},{4,12},{5,13},{6,14},{7,15},{8,0},{9,1},... | collective-permute-start | bytes 786440 | tf_op jit(solution)/shard_map/ppermute | solution.py:588
